TPU v7x, 32 devices: a whole 2x2x4 slice. The times are simulated.
32 devices in a mesh: groups: 2 (over y), seq: 4 (over z), head: 2 (over x), sub: 2 (over core).
Axes of the slice: x: 2, y: 2, z: 4, core: 2. Of those that a mesh axis runs over, the one named last changes fastest.
Arguments:
- queries: bfloat16 [2816, 64, 128], P(('groups', 'seq'), ('head', 'sub')), parts along dimension 0, may hold values from -0.5 to 0.5
- keys: bfloat16 [2816, 64, 128], P(('groups', 'seq'), ('head', 'sub')), parts along dimension 0, may hold values from -0.5 to 0.5
- values: bfloat16 [2816, 64, 128], P(('groups', 'seq'), ('head', 'sub')), parts along dimension 0, may hold values from -0.625 to 0.625
- output_gradient: bfloat16 [2816, 64, 128], P(('groups', 'seq'), ('head', 'sub')), parts along dimension 0, may hold values from -6 to 6
- decay_exponent: int32 [64], P(('head', 'sub')), may hold values from 5 to 19
- forget_spikes: float32 [2816, 64], P(('groups', 'seq'), ('head', 'sub')), parts along dimension 0, may hold values from 0 to 0.69
Outputs:
- query_grad: bfloat16 [2816, 64, 128], P(('groups', 'seq'), ('head', 'sub')), parts along dimension 0
- key_grad: bfloat16 [2816, 64, 128], P(('groups', 'seq'), ('head', 'sub')), parts along dimension 0
- value_grad: bfloat16 [2816, 64, 128], P(('groups', 'seq'), ('head', 'sub')), parts along dimension 0
There are 2 independent parts, one for each index of `groups`. A program takes and returns all parts, laid end to end along the dimension named above; an argument that names none is the same for every part. Nothing has to cross between parts.
All inputs are finite; a program needn't handle non-finite values.
Results may differ from a plain program's by a relative error of at most 0.0075.
Values may be sent and summed in bfloat16 or wider, within the bound.
No kernel may reach another device: no remote copies, remote signals or barrier semaphores. Data moves between devices by JAX's collectives and lax.ppermute only.
A program may use at most 128 MiB of HBM per device.

v0:
```python
import jax
import jax.numpy as jnp
from jax import lax
from jax.sharding import PartitionSpec as P


def entering(part, axis, combine, identity, reverse):
    count = lax.axis_size(axis)
    place = lax.axis_index(axis)
    ahead = count - 1 - place if reverse else place
    gathered = jax.tree.map(lambda a: lax.all_gather(a, axis), part)
    state = jax.tree.map(lambda a, e: jnp.zeros_like(a) + jnp.asarray(e, a.dtype), part, identity)

    def one(hop, state):
        source = count - 1 - hop if reverse else hop
        return combine(
            state, jax.tree.map(lambda a: lax.dynamic_index_in_dim(a, source, 0, False), gathered)
        )

    return lax.fori_loop(0, ahead, one, state)


def forget_parts(decay_exponent, forget_spikes):
    forget_logs = jnp.exp2(-decay_exponent.astype(jnp.float32))[None, :] + forget_spikes
    inside_span = jnp.cumsum(forget_logs, axis=0)
    whole_span_decay = inside_span[-1]
    entry_decay = jnp.exp(-inside_span)
    exit_decay = jnp.exp(-(whole_span_decay[None, :] - inside_span))
    return (inside_span, whole_span_decay, entry_decay, exit_decay)


def combine_states(earlier, latter):
    return (earlier[0] * latter[0], latter[0][:, None, None] * earlier[1] + latter[1])


def per_device(queries, keys, values, output_gradient, decay_exponent, forget_spikes):
    inside_span, whole_span_decay, entry_decay, exit_decay = forget_parts(
        decay_exponent, forget_spikes
    )
    key_out = (keys.astype(jnp.float32) * exit_decay[:, :, None]).astype(jnp.bfloat16)
    query_in = (queries.astype(jnp.float32) * entry_decay[:, :, None]).astype(jnp.bfloat16)
    kv_sum = jnp.einsum("thd,the->hde", key_out, values, preferred_element_type=jnp.float32).astype(
        jnp.bfloat16
    )
    grad_sum = jnp.einsum(
        "thd,the->hde", query_in, output_gradient, preferred_element_type=jnp.float32
    ).astype(jnp.bfloat16)
    span_fade = jnp.exp(-whole_span_decay)
    zero_state = jnp.zeros(kv_sum.shape, jnp.float32)
    identity = (jnp.ones_like(span_fade), zero_state)
    _, leading_state = entering(
        (span_fade, kv_sum.astype(jnp.float32)), "seq", combine_states, identity, False
    )
    _, trailing_state = entering(
        (span_fade, grad_sum.astype(jnp.float32)), "seq", combine_states, identity, True
    )
    prefix_b = leading_state.astype(jnp.bfloat16)
    suffix_b = trailing_state.astype(jnp.bfloat16)
    length = inside_span.shape[0]
    causal = jnp.arange(length)[:, None] >= jnp.arange(length)[None, :]
    spread = inside_span.T[:, :, None] - inside_span.T[:, None, :]
    weight = jnp.where(causal[None], jnp.exp(-jnp.maximum(spread, 0.0)), 0.0)
    scores = jnp.einsum("thd,shd->hts", queries, keys, preferred_element_type=jnp.float32)
    probes = jnp.einsum("the,she->hts", output_gradient, values, preferred_element_type=jnp.float32)
    masked_scores = (scores * weight).astype(jnp.bfloat16)
    masked_probes = (probes * weight).astype(jnp.bfloat16)
    query_grad = jnp.einsum(
        "hts,shd->thd", masked_probes, keys, preferred_element_type=jnp.float32
    ) + entry_decay[:, :, None] * jnp.einsum(
        "the,hde->thd", output_gradient, prefix_b, preferred_element_type=jnp.float32
    )
    key_grad = jnp.einsum(
        "hts,thd->shd", masked_probes, queries, preferred_element_type=jnp.float32
    ) + exit_decay[:, :, None] * jnp.einsum(
        "she,hde->shd", values, suffix_b, preferred_element_type=jnp.float32
    )
    value_grad = jnp.einsum(
        "hts,the->she", masked_scores, output_gradient, preferred_element_type=jnp.float32
    ) + exit_decay[:, :, None] * jnp.einsum(
        "shd,hde->she", keys, suffix_b, preferred_element_type=jnp.float32
    )
    return (
        query_grad.astype(jnp.bfloat16),
        key_grad.astype(jnp.bfloat16),
        value_grad.astype(jnp.bfloat16),
    )


def solution(mesh):
    in_specs = (
        P(("groups", "seq"), ("head", "sub"), None),
        P(("groups", "seq"), ("head", "sub"), None),
        P(("groups", "seq"), ("head", "sub"), None),
        P(("groups", "seq"), ("head", "sub"), None),
        P(("head", "sub")),
        P(("groups", "seq"), ("head", "sub")),
    )
    out_specs = (
        P(("groups", "seq"), ("head", "sub"), None),
        P(("groups", "seq"), ("head", "sub"), None),
        P(("groups", "seq"), ("head", "sub"), None),
    )
    return jax.shard_map(
        per_device, mesh=mesh, in_specs=in_specs, out_specs=out_specs, check_vma=False
    )
```

profile of v0, /device:TPU:0, one launch (start us, length us, event | category | flops | bytes accessed | tf_op | source)
XLA Modules:
  0.0 211.0 jit_solution(10579353862757904111)
XLA Ops:
  7.2 0.8 multiply_exponential_fusion
  8.0 0.8 add_bitcast_fusion.1
  8.8 0.9 reduce-window.6
  9.9 0.2 slice_reduce_fusion.1
  10.2 4.9 %fusion.17 = f32[16,128,128]{2,1,0:T(8,128)} fusion(f32[352,16]{0,1:T(8,128)S(1)} %get-tuple-element.167, bf16[352,16,128]{2,1,0:T(8,128)(2,1)} %param.10, bf16[352,16,128]{2,1,0:T(8,128)(2,1)} %param.13), kind=kOutput, calls=%fused_computation.28 | convolution fusion | flops 187236352 | bytes 3954688 | tf_op jit(solution)/shard_map/thd,the->hde/dot_general | solution.py:45
  15.2 3.5 %fusion.16 = f32[16,128,128]{2,1,0:T(8,128)} fusion(f32[352,16]{0,1:T(8,128)S(1)} %get-tuple-element.168, bf16[352,16,128]{2,1,0:T(8,128)(2,1)S(1)} %copy-done, bf16[352,16,128]{2,1,0:T(8,128)(2,1)S(1)} %copy-done.2), kind=kOutput, calls=%fused_computation.27 | convolution fusion | flops 187236352 | bytes 3954688 | tf_op jit(solution)/shard_map/thd,the->hde/dot_general | solution.py:42
  18.8 12.7 %all-gather.2 = f32[4,1,16]{2,1,0:T(1,128)S(1)} all-gather(f32[1,1,16]{2,1,0:T(1,128)S(1)} %bitcast.68), channel_id=1, replica_groups=mesh['groups'=2,'seq'=4,'head'=2,'sub'=2] {'seq'}, dimensions={0}, use_global_device_ids=true | all-gather | bytes 320 | tf_op jit(solution)/shard_map/all_gather | solution.py:11
  31.5 5.5 %multiply_convert_fusion.1 = bf16[16,352,352]{2,1,0:T(8,128)(2,1)} fusion(f32[16,352]{1,0:T(8,128)S(1)} %get-tuple-element.169, pred[352,352]{1,0:T(8,128)(4,1)S(1)} %iota_compare_fusion, bf16[352,16,128]{2,1,0:T(8,128)(2,1)S(1)} %copy-done, bf16[352,16,128]{2,1,0:T(8,128)(2,1)} %param.13), kind=kOutput, calls=%fused_computation.5 | convolution fusion | flops 519405568 | bytes 6994944 | tf_op jit(solution)/shard_map/the,she->hts/dot_general | solution.py:64
  37.0 61.8 %all-gather.8.cloned.1.call-done = f32[64,128,128]{2,1,0:T(8,128)} async-done(((f32[16,128,128]{2,1,0:T(8,128)}), f32[64,128,128]{2,1,0:T(8,128)}) %all-gather.8.cloned.1.call-update) | async-done | bytes 4194320 | tf_op jit(solution)/shard_map/all_gather | solution.py:11
  98.9 4.5 %while.27 = (s32[]{:T(128)}, f32[16,128,128]{2,1,0:T(8,128)S(1)}, s32[]{:T(128)}, f32[4,16]{1,0:T(4,128)S(1)}, f32[4,16,128,128]{3,2,1,0:T(8,128)}, /*index=5*/s32[]{:T(128)}, s32[]{:T(128)}, s32[]{:T(128)}, s32[]{:T(128)}) while((s32[]{:T(128)}, f32[16,128,128]{2,1,0:T(8,128)S(1)}, s32[]{:T(128)}, f32[4,16]{1,0:T(4,128)S(1)}, ...), condition=%wide.region_5.6_spmd, body=%wide.region_4.5_spmd.sunk | while | flops 524294 | bytes 3146075 | solution.py:20
  98.9 1.4 bitcast_add_fusion.5
  100.4 1.4 bitcast_add_fusion.5
  101.9 1.5 bitcast_add_fusion.5
  103.4 2.2 %fusion.22 = f32[16,128,352]{1,2,0:T(8,128)} fusion(bf16[352,16,128]{2,1,0:T(8,128)(2,1)S(1)} %copy-done, f32[16,128,128]{2,1,0:T(8,128)S(1)} %get-tuple-element.132), kind=kOutput, calls=%fused_computation.32 | convolution fusion | flops 184811520 | bytes 5373952 | tf_op jit(solution)/shard_map/she,hde->shd/dot_general | solution.py:74
  105.6 2.2 %fusion.26 = f32[16,128,352]{1,2,0:T(8,128)} fusion(bf16[352,16,128]{2,1,0:T(8,128)(2,1)S(1)} %copy-done.3, f32[16,128,128]{2,1,0:T(8,128)S(1)} %get-tuple-element.132), kind=kOutput, calls=%fused_computation.36 | convolution fusion | flops 184811520 | bytes 5373952 | tf_op jit(solution)/shard_map/shd,hde->she/dot_general | solution.py:79
  107.8 72.5 %all-gather.6.cloned.1.call-done = f32[64,128,128]{2,1,0:T(8,128)} async-done(((f32[16,128,128]{2,1,0:T(8,128)}), f32[64,128,128]{2,1,0:T(8,128)}) %all-gather.6.cloned.1.call-update) | async-done | bytes 4194320 | tf_op jit(solution)/shard_map/all_gather | solution.py:11
  180.6 2.1 fusion.34
  182.7 4.3 %fusion.9 = bf16[352,16,128]{2,0,1:T(8,128)(2,1)S(1)} fusion(f32[16,128,352]{1,2,0:T(8,128)S(1)} %fusion.34, bf16[16,352,352]{2,1,0:T(8,128)(2,1)} %multiply_convert_fusion.1, f32[352,16]{0,1:T(8,128)S(1)} %get-tuple-element.167, bf16[352,16,128]{2,1,0:T(8,128)(2,1)} %param.11), kind=kOutput, calls=%fused_computation.18 | convolution fusion | flops 509673472 | bytes 9754624 | tf_op jit(solution)/shard_map/hts,shd->thd/dot_general | solution.py:67
  186.9 1.7 copy.89
  188.6 0.7 copy-done.1
  189.3 2.4 %fusion.7 = bf16[352,16,128]{2,0,1:T(8,128)(2,1)S(1)} fusion(f32[16,128,352]{1,2,0:T(8,128)S(1)} %copy-done.1, bf16[16,352,352]{2,1,0:T(8,128)(2,1)S(1)} %bitcast.64, f32[352,16]{0,1:T(8,128)S(1)} %get-tuple-element.168, bf16[352,16,128]{2,1,0:T(8,128)(2,1)S(1)} %copy-done.5), kind=kOutput, calls=%fused_computation.15 | convolution fusion | flops 509673472 | bytes 9754624 | tf_op jit(solution)/shard_map/hts,thd->shd/dot_general | solution.py:72
  191.7 1.7 copy.90
  193.3 7.8 %fusion.5 = bf16[352,16,128]{2,0,1:T(8,128)(2,1)} fusion(f32[16,128,352]{1,2,0:T(8,128)} %fusion.26, f32[16,352]{1,0:T(8,128)S(1)} %get-tuple-element.169, pred[352,352]{1,0:T(8,128)(4,1)S(1)} %iota_compare_fusion, f32[352,16]{0,1:T(8,128)S(1)} %get-tuple-element.168, bf16[352,16,128]{2,1,0:T(8,128)(2,1)} %param.10, ...), kind=kOutput, calls=%fused_computation.12 | convolution fusion | flops 1029079040 | bytes 8819712 | tf_op jit(solution)/shard_map/hts,the->she/dot_general | solution.py:77
  201.1 3.0 %copy.91 = bf16[352,16,128]{2,1,0:T(8,128)(2,1)} copy(bf16[352,16,128]{2,0,1:T(8,128)(2,1)} %fusion.5) | data formatting | bytes 2883584
  (32 shorter events, 1.0 us)
Async XLA Ops:
  7.2 8.1 %copy-start = (bf16[352,16,128]{2,1,0:T(8,128)(2,1)S(1)}, bf16[352,16,128]{2,1,0:T(8,128)(2,1)}, u32[]{:S(2)}) copy-start(bf16[352,16,128]{2,1,0:T(8,128)(2,1)} %param.12) | copy-start | bytes 4325380
  7.2 91.6 %all-gather.8.cloned.1.call-start = ((), (), s32[]{:S(2)}) async-start(), calls=%async_computation.1 | async-start | bytes 5242880 | tf_op jit(solution)/shard_map/all_gather | solution.py:11
  10.2 5.0 %copy-start.2 = (bf16[352,16,128]{2,1,0:T(8,128)(2,1)S(1)}, bf16[352,16,128]{2,1,0:T(8,128)(2,1)}, u32[]{:S(2)}) copy-start(bf16[352,16,128]{2,1,0:T(8,128)(2,1)} %param.11) | copy-start | bytes 4325380
  15.2 165.1 %all-gather.6.cloned.1.call-start = ((), (), s32[]{:S(2)}) async-start(), calls=%async_computation | async-start | bytes 5242880 | tf_op jit(solution)/shard_map/all_gather | solution.py:11
  103.4 2.2 %copy-start.3 = (bf16[352,16,128]{2,1,0:T(8,128)(2,1)S(1)}, bf16[352,16,128]{2,1,0:T(8,128)(2,1)}, u32[]{:S(2)}) copy-start(bf16[352,16,128]{2,1,0:T(8,128)(2,1)} %param.11) | copy-start | bytes 4325380
  180.6 8.0 %slice-start = ((s8[4325376]{0:T(1024)(128)(4,1)}), s8[4194304]{0:T(1024)(128)(4,1)S(1)}, s32[]{:S(2)}) async-start(s8[4325376]{0:T(1024)(128)(4,1)} %bitcast.63), calls=%async_computation.2 | async-start | bytes 8388608
  182.6 6.0 %slice-start.1 = ((s8[4325376]{0:T(1024)(128)(4,1)}), s8[131072]{0:T(1024)(128)(4,1)S(1)}, s32[]{:S(2)}) async-start(s8[4325376]{0:T(1024)(128)(4,1)} %bitcast.63), calls=%async_computation.3 | async-start | bytes 262144
  182.6 6.0 %copy-start.5 = (bf16[352,16,128]{2,1,0:T(8,128)(2,1)S(1)}, bf16[352,16,128]{2,1,0:T(8,128)(2,1)}, u32[]{:S(2)}) copy-start(bf16[352,16,128]{2,1,0:T(8,128)(2,1)} %param.10) | copy-start | bytes 4325380
  186.9 2.3 %copy-start.1 = (f32[16,128,352]{1,2,0:T(8,128)S(1)}, f32[16,128,352]{1,2,0:T(8,128)}, u32[]{:S(2)}) copy-start(f32[16,128,352]{1,2,0:T(8,128)} %fusion.22) | copy-start | bytes 8650756
  191.7 1.7 copy-start.4
Sparse Core Ops, SparseCore 0:
  15.3 83.4 all-gather.7
  100.9 79.2 all-gather.5
where the time goes:
time: 212 us; the launch traced here: 211 us
  waiting for transfers between devices  134 us (63%)
  matrix products  34.8 us (16%)
  between operations  14.2 us (7%)
  blocking collectives  12.7 us (6%)
  local copies, waits for them, and re-layouts  7.41 us (3%)
  other arithmetic  7.22 us (3%)
    all_gather x2, waiting for transfers between devices, entering(): gathered = jax.tree.map(lambda a: lax.all_gather(a, axis), part)  134 us
    all_gather x1, blocking collectives, entering(): gathered = jax.tree.map(lambda a: lax.all_gather(a, axis), part)  12.7 us
    dot_general x1, matrix products, per_device(): jnp.einsum('hts,the->she', masked_scores, output_gradient, preferred_elem...  7.77 us
    unnamed x19, local copies, waits for them, and re-layouts  7.04 us
    dot_general x1, matrix products, per_device(): jnp.einsum('the,she->hts', output_gradient, values, preferred_element_typ...  5.52 us
    dot_general x1, matrix products, per_device(): jnp.einsum('thd,the->hde', query_in, output_gradient, preferred_element_t...  4.9 us
    add x3, other arithmetic, combine_states(): latter[0][:, None, None] * earlier[1] + latter[1]  4.35 us
    dot_general x1, matrix products, per_device(): jnp.einsum('hts,shd->thd', masked_probes, keys, preferred_element_type=jn...  4.26 us
  transfers between devices with their start and end apart: 2, of which 2 were waited for; matrix products, arithmetic and copies ran while one was open for 9% of the time, Pallas kernels for 0%

commit v1 on v0

v1 whole, which is shorter than its diff:
```python
import functools

import jax
import jax.numpy as jnp
from jax import lax
from jax.experimental import pallas as pl
from jax.experimental.pallas import tpu as pltpu
from jax.sharding import PartitionSpec as P

VMEM = pl.BlockSpec(memory_space=pltpu.VMEM)
SMEM = pl.BlockSpec(memory_space=pltpu.SMEM)
ANY = pl.BlockSpec(memory_space=pl.ANY)
BF16, F32 = jnp.bfloat16, jnp.float32
NT = (((1,), (1,)), ((), ()))
TN = (((0,), (0,)), ((), ()))
NN = (((1,), (0,)), ((), ()))
UNROLL = 4
MIB = 2**20


def dot(a, b, dims=NN):
    return lax.dot_general(a, b, dims, preferred_element_type=F32)


def running_forget(decay, spikes):
    heads, length = spikes.shape
    wide = -(-length // 128) * 128
    head = lax.broadcasted_iota(jnp.int32, (heads, 1), 0)
    exponent = jnp.zeros((heads, 1), jnp.int32)
    for h in range(heads):
        exponent = jnp.where(head == h, decay[h], exponent)
    forget = jnp.exp2(-exponent.astype(F32)) + spikes[...]
    if wide > length:
        forget = jnp.concatenate([forget, jnp.zeros((heads, wide - length), F32)], axis=1)
    lane = lax.broadcasted_iota(jnp.int32, forget.shape, 1)
    step = 1
    while step < length:
        forget = forget + jnp.where(lane >= step, pltpu.roll(forget, step, 1), 0.0)
        step *= 2
    return forget


def column_of(columns, h, length):
    return jnp.broadcast_to(columns[:length, h : h + 1], (length, 128))


def kv_sum_of(k, v, column):
    leave = jnp.exp(column - column[-1:])
    return dot((k.astype(F32) * leave).astype(BF16), v, TN).astype(BF16)


def grad_sum_of(q, g, column):
    return dot((q.astype(F32) * jnp.exp(-column)).astype(BF16), g, TN).astype(BF16)


def first_kernel(count, heads, decay, spikes, q, k, v, g, payload, left, right, sems):
    place = lax.axis_index("seq")
    length = spikes.shape[1]

    def run(a, b, sum_of):
        copies = [
            pltpu.make_async_copy(a, left, sems.at[0]),
            pltpu.make_async_copy(b, right, sems.at[1]),
        ]
        for copy in copies:
            copy.start()
        columns = running_forget(decay, spikes).T
        for copy in copies:
            copy.wait()
        a_h = jnp.swapaxes(left[:, :heads, :], 0, 1)
        b_h = jnp.swapaxes(right[:, :heads, :], 0, 1)
        for h in range(heads):
            payload[h] = sum_of(a_h[h], b_h[h], column_of(columns, h, length))

    @pl.when(place == 0)
    def _():
        run(k, v, kv_sum_of)

    @pl.when(place == count - 1)
    def _():
        run(q, g, grad_sum_of)


def sums_kernel(
    count, heads, decay, spikes, q, k, v, g, qh, kh, vh, gh, col, row, kv, grad, fade, *payloads
):
    all_heads, length = spikes.shape
    place = lax.axis_index("seq")
    within = running_forget(decay, spikes)
    row[...] = within[:, None, :]
    fade[...] = jnp.broadcast_to(jnp.exp(-within[:, length - 1 : length])[:, :, None], fade.shape)
    columns = within.T
    for h in range(all_heads):
        col[h] = column_of(columns, h, length)
    kh[...] = jnp.swapaxes(k[...], 0, 1)
    vh[...] = jnp.swapaxes(v[...], 0, 1)

    @pl.when(place < count - 1)
    def _():
        for h in range(all_heads):
            kv[h] = kv_sum_of(kh[h], vh[h], col[h])

    qh[...] = jnp.swapaxes(q[...], 0, 1)
    gh[...] = jnp.swapaxes(g[...], 0, 1)

    @pl.when(place > 0)
    def _():
        for h in range(all_heads):
            grad[h] = grad_sum_of(qh[h], gh[h], col[h])

    for i, payload in enumerate(payloads):
        start = (i + 1) * heads

        @pl.when(place == 0)
        def _():
            payload[...] = kv[start : start + heads]

        @pl.when(place == count - 1)
        def _():
            payload[...] = grad[start : start + heads]


def merge_kernel(count, hop, start, got, kv, grad, fade, payload):
    place = lax.axis_index("seq")
    heads = got.shape[0]
    cut = slice(start, start + heads)
    for at, own in ((hop, kv), (count - 1 - hop, grad)):

        @pl.when(place == at)
        def _():
            payload[...] = (fade[cut] * got[...].astype(F32) + own[cut].astype(F32)).astype(BF16)


def intra_kernel(start, col, row, qh, kh, vh, gh, qg, kg, vg):
    heads, length, _ = qg.shape
    edges = list(range(0, length, 256)) + [length]
    blocks = list(zip(edges[:-1], edges[1:]))

    def one(i, carry):
        h = start + i
        q, k, v, g = qh[h], kh[h], vh[h], gh[h]
        qt, gt = q.T, g.T
        scores, probes = {}, {}
        for t0, t1 in blocks:
            for s0, s1 in blocks:
                if s0 > t0:
                    continue
                column = col[h, t0:t1, :]
                if s1 - s0 > 128:
                    column = jnp.concatenate([column, column], axis=1)
                spread = row[h, :, s0:s1] - column[:, : s1 - s0]
                weight = jnp.exp(jnp.minimum(spread, 0.0))
                if s0 == t0:
                    t = lax.broadcasted_iota(jnp.int32, spread.shape, 0)
                    s = lax.broadcasted_iota(jnp.int32, spread.shape, 1)
                    weight = jnp.where(t >= s, weight, 0.0)
                scores[t0, s0] = (dot(q[t0:t1], k[s0:s1], NT) * weight).astype(BF16)
                probes[t0, s0] = (dot(g[t0:t1], v[s0:s1], NT) * weight).astype(BF16)
        for t0, t1 in blocks:
            qg[i, t0:t1, :] = sum(dot(probes[t0, s0], k[s0:s1]) for s0, s1 in blocks if s0 <= t0)
        for s0, s1 in blocks:
            after = [(t0, t1) for t0, t1 in blocks if t0 >= s0]
            kg[i, s0:s1, :] = sum(dot(qt[:, t0:t1], probes[t0, s0]) for t0, t1 in after).T
            vg[i, s0:s1, :] = sum(dot(gt[:, t0:t1], scores[t0, s0]) for t0, t1 in after).T
        return carry

    lax.fori_loop(0, heads, one, 0, unroll=min(UNROLL, heads))


def final_kernel(count, chunks, last, col, kh, vh, gh, *rest):
    hops = 1 if last else count - 2
    intra, rest = rest[: 3 * chunks], rest[3 * chunks :]
    arrived, rest = rest[: hops * chunks], rest[hops * chunks :]
    if last:
        rest = rest[3:]
    outs, (state, by_head, tokens, sems) = rest[:3], rest[3:]
    all_heads, length, _ = kh.shape
    heads = all_heads // chunks
    place = lax.axis_index("seq")

    def take(from_hop):
        for hop in [count - 1] if last else range(1, count - 1):

            @pl.when(place == from_hop(hop))
            def _():
                for c in range(chunks):
                    state[c * heads : (c + 1) * heads] = arrived[c * hops + (0 if last else hop - 1)][...]

    def write(j, term):
        for c in range(chunks):

            def one(i, carry):
                h = c * heads + i
                by_head[j, h] = (intra[3 * c + j][i] + term(h)).astype(BF16)
                return carry

            lax.fori_loop(0, heads, one, 0, unroll=min(UNROLL, heads))
        tokens[j] = jnp.swapaxes(by_head[j], 0, 1)
        pltpu.make_async_copy(tokens.at[j], outs[j], sems.at[j]).start()

    def wait(j):
        pltpu.make_async_copy(tokens.at[j], outs[j], sems.at[j]).wait()

    def enter(h):
        return jnp.exp(-col[h])

    def leave(h):
        return jnp.exp(col[h] - col[h, length - 1 : length, :])

    does_q = place == count - 1 if last else place < count - 1
    does_kv = place == 0 if last else place > 0

    @pl.when(does_q)
    def _():
        if not last:

            @pl.when(place == 0)
            def _():
                state[...] = jnp.zeros_like(state)

        take(lambda hop: hop)
        write(0, lambda h: enter(h) * dot(gh[h], state[h], NT))

    @pl.when(does_kv)
    def _():
        if not last:

            @pl.when(place == count - 1)
            def _():
                state[...] = jnp.zeros_like(state)

        take(lambda hop: count - 1 - hop)
        write(1, lambda h: leave(h) * dot(vh[h], state[h], NT))
        write(2, lambda h: leave(h) * dot(kh[h], state[h]))

    @pl.when(does_q)
    def _():
        wait(0)

    @pl.when(does_kv)
    def _():
        wait(1)
        wait(2)


def per_device(count, queries, keys, values, output_gradient, decay_exponent, forget_spikes):
    length, all_heads, size = queries.shape
    heads = 8 if all_heads % 8 == 0 else all_heads
    chunks = all_heads // heads
    spikes = forget_spikes.T
    shape = jax.ShapeDtypeStruct
    wide = -(-length // 128) * 128
    by_head = shape((all_heads, length, size), BF16)
    by_head_f = shape((all_heads, length, size), F32)
    part_f = shape((heads, length, size), F32)
    states = shape((all_heads, size, size), BF16)
    state = shape((heads, size, size), BF16)
    flops = 2 * heads * length * size * size

    def call(kernel, outs, n_in, limit, n, nbytes, specs=None, **more):
        return pl.pallas_call(
            kernel,
            out_shape=outs,
            in_specs=specs or [VMEM] * n_in,
            compiler_params=pltpu.CompilerParams(vmem_limit_bytes=limit * MIB),
            cost_estimate=pl.CostEstimate(flops=n * flops, bytes_accessed=nbytes, transcendentals=0),
            **more,
        )

    tensors = (queries, keys, values, output_gradient)
    raw = pltpu.VMEM(queries.shape, BF16)
    first = call(
        functools.partial(first_kernel, count, heads),
        state,
        6,
        60,
        1,
        3 << 20,
        specs=[SMEM, VMEM] + [ANY] * 4,
        out_specs=VMEM,
        scratch_shapes=[raw, raw, pltpu.SemaphoreType.DMA((2,))],
    )(decay_exponent, spikes, *tensors)
    qh, kh, vh, gh, col, row, kv, grad, fade, *others = call(
        functools.partial(sums_kernel, count, heads),
        (by_head,) * 4
        + (by_head_f, shape((all_heads, 1, wide), F32), states, states)
        + (shape((all_heads, 1, size), F32),)
        + (state,) * (chunks - 1),
        6,
        8,
        4,
        8 << 20,
        specs=[SMEM] + [VMEM] * 5,
        out_specs=(VMEM,) * (9 + chunks - 1),
    )(decay_exponent, spikes, *tensors)

    payloads = [first, *others]
    arrived = [[] for _ in range(chunks)]
    for hop in range(1, count):
        pairs = [(hop - 1, hop), (count - hop, count - hop - 1)]
        for c in range(chunks):
            got = lax.ppermute(payloads[c], "seq", pairs)
            arrived[c].append(got)
            if hop < count - 1:
                payloads[c] = call(
                    functools.partial(merge_kernel, count, hop, c * heads),
                    state,
                    4,
                    4,
                    0,
                    1 << 20,
                    out_specs=VMEM,
                )(got, kv, grad, fade)
    intra = []
    for c in range(chunks):
        intra += call(
            functools.partial(intra_kernel, c * heads), (part_f,) * 3, 6, 8, 14, 4 << 20, out_specs=(VMEM,) * 3
        )(col, row, qh, kh, vh, gh)

    full = shape(queries.shape, BF16)

    def finish(last, outs):
        hops = 1 if last else count - 2
        came = [a for c in range(chunks) for a in (arrived[c][-1:] if last else arrived[c][:-1])]
        fixed = 4 + 3 * chunks + len(came)
        return call(
            functools.partial(final_kernel, count, chunks, last),
            (full,) * 3,
            fixed,
            16,
            3,
            8 << 20,
            specs=[VMEM] * fixed + [ANY] * len(outs),
            out_specs=(ANY,) * 3,
            scratch_shapes=[
                pltpu.VMEM(states.shape, BF16),
                pltpu.VMEM((3,) + by_head.shape, BF16),
                pltpu.VMEM((3,) + full.shape, BF16),
                pltpu.SemaphoreType.DMA((3,)),
            ],
            input_output_aliases={fixed + j: j for j in range(len(outs))},
        )(col, kh, vh, gh, *intra, *came, *outs)

    return tuple(finish(True, finish(False, ())))


def solution(mesh):
    tokens = P(("groups", "seq"), ("head", "sub"), None)
    in_specs = (tokens,) * 4 + (P(("head", "sub")), P(("groups", "seq"), ("head", "sub")))
    return jax.shard_map(
        functools.partial(per_device, mesh.shape["seq"]),
        mesh=mesh,
        in_specs=in_specs,
        out_specs=(tokens,) * 3,
        check_vma=False,
    )
```

time: 212 us -> 47.4 us (0.22)
  waiting for transfers between devices: 134 us -> 12.1 us
  matrix products: 34.8 us -> 0 us
  Pallas kernels: 0 us -> 23.3 us
  between operations: 14.2 us -> 0.99 us
  blocking collectives: 12.7 us -> 0 us
  starting transfers between devices: 0.08 us -> 7.7 us
  other arithmetic: 7.22 us -> 0 us
  local copies, waits for them, and re-layouts: 7.41 us -> 2.74 us
    all_gather x2 -> x0, waiting for transfers between devices: 134 us -> none  [entering(): gathered = jax.tree.map(lambda a: lax.all_gather(a, axis), part)]
    dot_general x9 -> x0, matrix products: 34.8 us -> none  [the longest x1 7.77 us: per_device(): jnp.einsum('hts,the->she', masked_scores, output_gradient, preferred_elem...]
    pallas_call x0 -> x10, Pallas kernels: none -> 23.3 us  [the longest x2 6.87 us: finish(): call(functools.partial(final_kernel, count, chunks, last), (full,) * 3, f...]
    all_gather x1 -> x0, blocking collectives: 12.7 us -> none  [entering(): gathered = jax.tree.map(lambda a: lax.all_gather(a, axis), part)]
    ppermute x0 -> x6, waiting for transfers between devices: none -> 12.1 us  [per_device(): got = lax.ppermute(payloads[c], 'seq', pairs)]
    ppermute x0 -> x6, starting transfers between devices: none -> 7.7 us  [per_device(): got = lax.ppermute(payloads[c], 'seq', pairs)]
    add x3 -> x0, other arithmetic: 4.35 us -> none  [combine_states(): latter[0][:, None, None] * earlier[1] + latter[1]]
    unnamed x19 -> x12, local copies, waits for them, and re-layouts: 7.04 us -> 2.74 us
  transfers between devices with their start and end apart: 2 -> 6, of which waited for: 2 -> 3; matrix products, arithmetic and copies ran while one was open for 9% -> 0% of each run, Pallas kernels for 0% -> 30%
where the time goes in v1:
time: 47.4 us; the launch traced here: 46.8 us
  Pallas kernels  23.3 us (49%)
  waiting for transfers between devices  12.1 us (26%)
  starting transfers between devices  7.7 us (16%)
  local copies, waits for them, and re-layouts  2.74 us (6%)
  between operations  0.99 us (2%)
    ppermute x6, waiting for transfers between devices, per_device(): got = lax.ppermute(payloads[c], 'seq', pairs)  12.1 us
    ppermute x6, starting transfers between devices, per_device(): got = lax.ppermute(payloads[c], 'seq', pairs)  7.7 us
    pallas_call x2, Pallas kernels, finish(): call(functools.partial(final_kernel, count, chunks, last), (full,) * 3, f...  6.87 us
    pallas_call x2, Pallas kernels, per_device(): call(functools.partial(intra_kernel, c * heads), (part_f,) * 3, 6, 8, 14,...  6.7 us
    pallas_call x1, Pallas kernels, per_device(): call(functools.partial(first_kernel, count, heads), state, 6, 60, 1, 3 <<...  4.92 us
    pallas_call x1, Pallas kernels, per_device(): call(functools.partial(sums_kernel, count, heads), (by_head,) * 4 + (by_h...  4.71 us
    unnamed x12, local copies, waits for them, and re-layouts  2.74 us
  transfers between devices with their start and end apart: 6, of which 3 were waited for; matrix products, arithmetic and copies ran while one was open for 0% of the time, Pallas kernels for 30%

profile of v1, /device:TPU:0, one launch (start us, length us, event | category | flops | bytes accessed | tf_op | source)
XLA Modules:
  0.0 46.8 jit_solution(12982815053568374518)
XLA Ops:
  0.6 0.0 copy-start
  0.6 0.0 copy-start.1
  0.7 0.0 copy-start.4
  0.7 4.9 %shard_map.88 = bf16[8,128,128]{2,1,0:T(8,128)(2,1)} custom-call(s32[16]{0:T(128)} %decay.3, f32[16,352]{1,0:T(8,128)} %bitcast.1, bf16[352,16,128]{2,1,0:T(8,128)(2,1)} %q.3, bf16[352,16,128]{2,1,0:T(8,128)(2,1)} %k.3, bf16[352,16,128]{2,1,0:T(8,128)(2,1)} %v.3, bf16[352,16,128]{2,1,0:T(8,128)(2,1)} %g.3), custom_call_target="tpu_custom_call" | custom-call | flops 92274688 | bytes 3145728 | tf_op jit(solution)/shard_map/pallas_call | solution.py:272
  5.6 1.7 %collective-permute-start = (bf16[8,128,128]{2,1,0:T(8,128)(2,1)}, bf16[8,128,128]{2,1,0:T(8,128)(2,1)S(1)}, u32[]{:S(2)}, u32[]{:S(2)}) collective-permute-start(bf16[8,128,128]{2,1,0:T(8,128)(2,1)} %shard_map.88), channel_id=1, source_target_pairs={{0,4},{12,8},{1,5},{13,9},{2,6},{14,10},{3,7},{15,11},{16,20},{28,... | collective-permute-start | bytes 786440 | tf_op jit(solution)/shard_map/ppermute | solution.py:302
  7.3 0.0 copy-start.2
  7.3 1.4 %copy-done.2 = bf16[352,16,128]{2,1,0:T(8,128)(2,1)S(1)} copy-done((bf16[352,16,128]{2,1,0:T(8,128)(2,1)S(1)}, bf16[352,16,128]{2,1,0:T(8,128)(2,1)}, u32[]{:S(2)}) %copy-start.2) | copy-done | bytes 1441816
  8.7 1.4 %copy-done.3 = bf16[352,16,128]{2,1,0:T(8,128)(2,1)S(1)} copy-done((bf16[352,16,128]{2,1,0:T(8,128)(2,1)S(1)}, bf16[352,16,128]{2,1,0:T(8,128)(2,1)}, u32[]{:S(2)}) %copy-start.3) | copy-done | bytes 1441816
  10.0 4.7 %shard_map.85 = (bf16[16,352,128]{2,1,0:T(8,128)(2,1)S(1)}, bf16[16,352,128]{2,1,0:T(8,128)(2,1)S(1)}, bf16[16,352,128]{2,1,0:T(8,128)(2,1)S(1)}, bf16[16,352,12...) custom-call(s32[16]{0:T(128)S(1)} %copy-done.5, ...), custom_call_target="tpu_custom_call" | custom-call | flops 369098752 | bytes 8388608 | tf_op jit(solution)/shard_map/pallas_call | solution.py:283
  14.7 2.1 %collective-permute-start.3 = (bf16[8,128,128]{2,1,0:T(8,128)(2,1)S(1)}, bf16[8,128,128]{2,1,0:T(8,128)(2,1)S(1)}, u32[]{:S(2)}, u32[]{:S(2)}) collective-permute-start(bf16[8,128,128]{2,1,0:T(8,128)(2,1)S(1)} %get-tuple-element.37), channel_id=1, source_target_pairs={{0,4},{12,8},{1,5},{13,9},{2,6},{14,10},{3,7},{15,11},{16,20},{28,... | collective-permute-start | bytes 786440 | tf_op jit(solution)/shard_map/ppermute | solution.py:302
  16.9 0.0 collective-permute-done.got.rest_6_
  16.9 0.7 %collective-permute-start.1 = (bf16[8,128,128]{2,1,0:T(8,128)(2,1)S(1)}, bf16[8,128,128]{2,1,0:T(8,128)(2,1)S(1)}, u32[]{:S(2)}, u32[]{:S(2)}) collective-permute-start(bf16[8,128,128]{2,1,0:T(8,128)(2,1)S(1)} %shard_map.89), channel_id=1, source_target_pairs={{4,8},{8,4},{5,9},{9,5},{6,10},{10,6},{7,11},{11,7},{20,24},{24,20... | collective-permute-start | bytes 786440 | tf_op jit(solution)/shard_map/ppermute | solution.py:302
  17.6 4.8 %collective-permute-done.3.got.rest_8_ = bf16[8,128,128]{2,1,0:T(8,128)(2,1)S(1)} collective-permute-done((bf16[8,128,128]{2,1,0:T(8,128)(2,1)S(1)}, bf16[8,128,128]{2,1,0:T(8,128)(2,1)S(1)}, u32[]{:S(2)}, u32[]{:S(2)}) %collective-permute-start.3) | collective-permute-done | bytes 262176 | tf_op jit(solution)/shard_map/ppermute | solution.py:302
  22.4 0.7 %collective-permute-start.4 = (bf16[8,128,128]{2,1,0:T(8,128)(2,1)S(1)}, bf16[8,128,128]{2,1,0:T(8,128)(2,1)S(1)}, u32[]{:S(2)}, u32[]{:S(2)}) collective-permute-start(bf16[8,128,128]{2,1,0:T(8,128)(2,1)S(1)} %shard_map.91), channel_id=1, source_target_pairs={{4,8},{8,4},{5,9},{9,5},{6,10},{10,6},{7,11},{11,7},{20,24},{24,20... | collective-permute-start | bytes 786440 | tf_op jit(solution)/shard_map/ppermute | solution.py:302
  23.1 0.0 collective-permute-done.1.got.rest_7_
  23.1 1.3 %collective-permute-start.2 = (bf16[8,128,128]{2,1,0:T(8,128)(2,1)S(1)}, bf16[8,128,128]{2,1,0:T(8,128)(2,1)S(1)}, u32[]{:S(2)}, u32[]{:S(2)}) collective-permute-start(bf16[8,128,128]{2,1,0:T(8,128)(2,1)S(1)} %shard_map.90), channel_id=1, source_target_pairs={{8,12},{4,0},{9,13},{5,1},{10,14},{6,2},{11,15},{7,3},{24,28},{20,... | collective-permute-start | bytes 786440 | tf_op jit(solution)/shard_map/ppermute | solution.py:302
  24.4 0.0 collective-permute-done.4.got.rest_9_
  24.5 1.3 %collective-permute-start.5 = (bf16[8,128,128]{2,1,0:T(8,128)(2,1)S(1)}, bf16[8,128,128]{2,1,0:T(8,128)(2,1)S(1)}, u32[]{:S(2)}, u32[]{:S(2)}) collective-permute-start(bf16[8,128,128]{2,1,0:T(8,128)(2,1)S(1)} %shard_map.92), channel_id=1, source_target_pairs={{8,12},{4,0},{9,13},{5,1},{10,14},{6,2},{11,15},{7,3},{24,28},{20,... | collective-permute-start | bytes 786440 | tf_op jit(solution)/shard_map/ppermute | solution.py:302
  25.8 3.4 %shard_map.87 = (f32[8,352,128]{2,1,0:T(8,128)S(1)}, f32[8,352,128]{2,1,0:T(8,128)S(1)}, f32[8,352,128]{2,1,0:T(8,128)S(1)}) custom-call(f32[16,352,128]{2,1,0:T(8,128)S(1)} %get-tuple-element.22.col, f32[16,1,384]{2,1,0:T(1,128)S(1)} %get-tuple-element.26.row, bf16[16,352,128]{2,1,0:T(8,128)(2,1)S(1)} %get-tuple-element.27.qh, ...), custom_call_target="tpu_custom_call" | custom-call | flops 1291845632 | bytes 4194304 | tf_op jit(solution)/shard_map/pallas_call | solution.py:316
  29.1 3.4 %shard_map.86 = (f32[8,352,128]{2,1,0:T(8,128)S(1)}, f32[8,352,128]{2,1,0:T(8,128)S(1)}, f32[8,352,128]{2,1,0:T(8,128)S(1)}) custom-call(f32[16,352,128]{2,1,0:T(8,128)S(1)} %get-tuple-element.22.col, f32[16,1,384]{2,1,0:T(1,128)S(1)} %get-tuple-element.26.row, bf16[16,352,128]{2,1,0:T(8,128)(2,1)S(1)} %get-tuple-element.27.qh, ...), custom_call_target="tpu_custom_call" | custom-call | flops 1291845632 | bytes 4194304 | tf_op jit(solution)/shard_map/pallas_call | solution.py:316
  32.5 2.7 %shard_map.93 = (bf16[352,16,128]{2,1,0:T(8,128)(2,1)}, bf16[352,16,128]{2,1,0:T(8,128)(2,1)}, bf16[352,16,128]{2,1,0:T(8,128)(2,1)}) custom-call(f32[16,352,128]{2,1,0:T(8,128)S(1)} %get-tuple-element.22.col, bf16[16,352,128]{2,1,0:T(8,128)(2,1)S(1)} %get-tuple-element.23.kh, bf16[16,352,128]{2,1,0:T(8,128)(2,1)S(1)} %get-tuple-element.24.vh, ...), custom_call_target="tpu_custom_call" | custom-call | flops 276824064 | bytes 8388608 | tf_op jit(solution)/shard_map/pallas_call | solution.py:326
  35.2 1.8 %collective-permute-done.2.rest_6_ = bf16[8,128,128]{2,1,0:T(8,128)(2,1)S(1)} collective-permute-done((bf16[8,128,128]{2,1,0:T(8,128)(2,1)S(1)}, bf16[8,128,128]{2,1,0:T(8,128)(2,1)S(1)}, u32[]{:S(2)}, u32[]{:S(2)}) %collective-permute-start.2) | collective-permute-done | bytes 262176 | tf_op jit(solution)/shard_map/ppermute | solution.py:302
  37.0 5.4 %collective-permute-done.5.rest_7_ = bf16[8,128,128]{2,1,0:T(8,128)(2,1)S(1)} collective-permute-done((bf16[8,128,128]{2,1,0:T(8,128)(2,1)S(1)}, bf16[8,128,128]{2,1,0:T(8,128)(2,1)S(1)}, u32[]{:S(2)}, u32[]{:S(2)}) %collective-permute-start.5) | collective-permute-done | bytes 262176 | tf_op jit(solution)/shard_map/ppermute | solution.py:302
  42.5 4.1 %shard_map.94 = (bf16[352,16,128]{2,1,0:T(8,128)(2,1)}, bf16[352,16,128]{2,1,0:T(8,128)(2,1)}, bf16[352,16,128]{2,1,0:T(8,128)(2,1)}) custom-call(f32[16,352,128]{2,1,0:T(8,128)S(1)} %get-tuple-element.22.col, bf16[16,352,128]{2,1,0:T(8,128)(2,1)S(1)} %get-tuple-element.23.kh, ...), custom_call_target="tpu_custom_call", output_to_operand_aliasing={{0}: (12, {}), {1}: (13, {}), {2}: (14, {})} | custom-call | flops 276824064 | bytes 8388608 | tf_op jit(solution)/shard_map/pallas_call | solution.py:326
  (10 shorter events, 0.1 us)
Async XLA Ops:
  0.6 6.6 %copy-start = (bf16[352,16,128]{2,1,0:T(8,128)(2,1)S(1)}, bf16[352,16,128]{2,1,0:T(8,128)(2,1)}, u32[]{:S(2)}) copy-start(bf16[352,16,128]{2,1,0:T(8,128)(2,1)} %q.3) | copy-start | bytes 4325380
  0.6 6.6 %copy-start.1 = (bf16[352,16,128]{2,1,0:T(8,128)(2,1)S(1)}, bf16[352,16,128]{2,1,0:T(8,128)(2,1)}, u32[]{:S(2)}) copy-start(bf16[352,16,128]{2,1,0:T(8,128)(2,1)} %k.3) | copy-start | bytes 4325380
  0.7 6.6 %copy-start.4 = (f32[352,16]{0,1:T(8,128)S(1)}, f32[352,16]{0,1:T(8,128)}, u32[]{:S(2)}) copy-start(f32[352,16]{0,1:T(8,128)} %param.11) | copy-start | bytes 67588
  0.7 6.6 %copy-start.5 = (s32[16]{0:T(128)S(1)}, s32[16]{0:T(128)}, u32[]{:S(2)}) copy-start(s32[16]{0:T(128)} %decay.3) | copy-start | bytes 196
  5.6 11.3 %collective-permute-start = (bf16[8,128,128]{2,1,0:T(8,128)(2,1)}, bf16[8,128,128]{2,1,0:T(8,128)(2,1)S(1)}, u32[]{:S(2)}, u32[]{:S(2)}) collective-permute-start(bf16[8,128,128]{2,1,0:T(8,128)(2,1)} %shard_map.88), channel_id=1, source_target_pairs={{0,4},{12,8},{1,5},{13,9},{2,6},{14,10},{3,7},{15,11},{16,20},{28,... | collective-permute-start | bytes 786440 | tf_op jit(solution)/shard_map/ppermute | solution.py:302
  7.3 1.4 %copy-start.2 = (bf16[352,16,128]{2,1,0:T(8,128)(2,1)S(1)}, bf16[352,16,128]{2,1,0:T(8,128)(2,1)}, u32[]{:S(2)}) copy-start(bf16[352,16,128]{2,1,0:T(8,128)(2,1)} %v.3) | copy-start | bytes 4325380
  8.7 1.4 %copy-start.3 = (bf16[352,16,128]{2,1,0:T(8,128)(2,1)S(1)}, bf16[352,16,128]{2,1,0:T(8,128)(2,1)}, u32[]{:S(2)}) copy-start(bf16[352,16,128]{2,1,0:T(8,128)(2,1)} %g.3) | copy-start | bytes 4325380
  14.7 7.7 %collective-permute-start.3 = (bf16[8,128,128]{2,1,0:T(8,128)(2,1)S(1)}, bf16[8,128,128]{2,1,0:T(8,128)(2,1)S(1)}, u32[]{:S(2)}, u32[]{:S(2)}) collective-permute-start(bf16[8,128,128]{2,1,0:T(8,128)(2,1)S(1)} %get-tuple-element.37), channel_id=1, source_target_pairs={{0,4},{12,8},{1,5},{13,9},{2,6},{14,10},{3,7},{15,11},{16,20},{28,... | collective-permute-start | bytes 786440 | tf_op jit(solution)/shard_map/ppermute | solution.py:302
  16.9 6.2 %collective-permute-start.1 = (bf16[8,128,128]{2,1,0:T(8,128)(2,1)S(1)}, bf16[8,128,128]{2,1,0:T(8,128)(2,1)S(1)}, u32[]{:S(2)}, u32[]{:S(2)}) collective-permute-start(bf16[8,128,128]{2,1,0:T(8,128)(2,1)S(1)} %shard_map.89), channel_id=1, source_target_pairs={{4,8},{8,4},{5,9},{9,5},{6,10},{10,6},{7,11},{11,7},{20,24},{24,20... | collective-permute-start | bytes 786440 | tf_op jit(solution)/shard_map/ppermute | solution.py:302
  22.4 2.0 %collective-permute-start.4 = (bf16[8,128,128]{2,1,0:T(8,128)(2,1)S(1)}, bf16[8,128,128]{2,1,0:T(8,128)(2,1)S(1)}, u32[]{:S(2)}, u32[]{:S(2)}) collective-permute-start(bf16[8,128,128]{2,1,0:T(8,128)(2,1)S(1)} %shard_map.91), channel_id=1, source_target_pairs={{4,8},{8,4},{5,9},{9,5},{6,10},{10,6},{7,11},{11,7},{20,24},{24,20... | collective-permute-start | bytes 786440 | tf_op jit(solution)/shard_map/ppermute | solution.py:302
  23.1 13.9 %collective-permute-start.2 = (bf16[8,128,128]{2,1,0:T(8,128)(2,1)S(1)}, bf16[8,128,128]{2,1,0:T(8,128)(2,1)S(1)}, u32[]{:S(2)}, u32[]{:S(2)}) collective-permute-start(bf16[8,128,128]{2,1,0:T(8,128)(2,1)S(1)} %shard_map.90), channel_id=1, source_target_pairs={{8,12},{4,0},{9,13},{5,1},{10,14},{6,2},{11,15},{7,3},{24,28},{20,... | collective-permute-start | bytes 786440 | tf_op jit(solution)/shard_map/ppermute | solution.py:302
  24.5 18.0 %collective-permute-start.5 = (bf16[8,128,128]{2,1,0:T(8,128)(2,1)S(1)}, bf16[8,128,128]{2,1,0:T(8,128)(2,1)S(1)}, u32[]{:S(2)}, u32[]{:S(2)}) collective-permute-start(bf16[8,128,128]{2,1,0:T(8,128)(2,1)S(1)} %shard_map.92), channel_id=1, source_target_pairs={{8,12},{4,0},{9,13},{5,1},{10,14},{6,2},{11,15},{7,3},{24,28},{20,... | collective-permute-start | bytes 786440 | tf_op jit(solution)/shard_map/ppermute | solution.py:302

commit v2 on v1

v2 whole, which is shorter than its diff:
```python
import functools

import jax
import jax.numpy as jnp
from jax import lax
from jax.experimental import pallas as pl
from jax.experimental.pallas import tpu as pltpu
from jax.sharding import PartitionSpec as P

VMEM = pl.BlockSpec(memory_space=pltpu.VMEM)
ANY = pl.BlockSpec(memory_space=pl.ANY)
BF16, F32 = jnp.bfloat16, jnp.float32
NT = (((1,), (1,)), ((), ()))
TN = (((0,), (0,)), ((), ()))
NN = (((1,), (0,)), ((), ()))
UNROLL = 4
CHUNKS = 3
DUE = {(0, 0): 5, (2, 1): 9}
MIB = 2**20
TOKEN = jax.ShapeDtypeStruct((8, 128), F32)


def dot(a, b, dims=NN):
    return lax.dot_general(a, b, dims, preferred_element_type=F32)


def running_forget(decay, spikes):
    heads, length = spikes.shape
    wide = -(-length // 128) * 128
    same = lax.broadcasted_iota(jnp.int32, (heads, heads), 0) == lax.broadcasted_iota(jnp.int32, (heads, heads), 1)
    exponent = jnp.sum(jnp.where(same, decay[...].astype(F32), 0.0), axis=1, keepdims=True)
    forget = jnp.exp2(-exponent) + spikes[...]
    if wide > length:
        forget = jnp.concatenate([forget, jnp.zeros((heads, wide - length), F32)], axis=1)
    lane = lax.broadcasted_iota(jnp.int32, forget.shape, 1)
    step = 1
    while step < length:
        forget = forget + jnp.where(lane >= step, pltpu.roll(forget, step, 1), 0.0)
        step *= 2
    return forget


def state_sum(left, right, fade):
    return dot((left.T.astype(F32) * fade).astype(BF16), right).astype(BF16)


def enter_of(within, h, length):
    return jnp.exp(-within[h : h + 1, :length])


def leave_of(within, h, length):
    return jnp.exp(within[h : h + 1, :length] - within[h : h + 1, length - 1 : length])


def first_kernel(count, heads, decay, spikes, q, k, v, g, *rest):
    payloads, (_, decay_v, spikes_v, left, right, sems) = rest[-6 - len(heads) : -6], rest[-6:]
    place = lax.axis_index("seq")
    length = spikes.shape[1]

    def run(a, b, fade_of):
        copies = [
            pltpu.make_async_copy(source, target, sems.at[i])
            for i, (source, target) in enumerate(
                ((spikes, spikes_v), (decay, decay_v), (a, left), (b, right))
            )
        ]
        for copy in copies:
            copy.start()
        for copy in copies[:2]:
            copy.wait()
        within = running_forget(decay_v, spikes_v)
        fades = {h: fade_of(within, h, length) for part in heads for h in part}
        for copy in copies[2:]:
            copy.wait()
        a_h = jnp.swapaxes(left[...], 0, 1)
        b_h = jnp.swapaxes(right[...], 0, 1)
        for part, payload in zip(heads, payloads):
            for i, h in enumerate(part):
                payload[i] = state_sum(a_h[h], b_h[h], fades[h])

    @pl.when(place == 0)
    def _():
        run(k, v, leave_of)

    @pl.when(place == count - 1)
    def _():
        run(q, g, enter_of)


def sums_kernel(count, decay, spikes, q, k, v, g, *rest):
    qh, kh, vh, gh, col, row, kv, grad, fade = rest[-9:]
    all_heads, length = spikes.shape
    place = lax.axis_index("seq")
    within = running_forget(decay, spikes)
    row[...] = within[:, None, :]
    fade[...] = jnp.broadcast_to(jnp.exp(-within[:, length - 1 : length])[:, :, None], fade.shape)
    kh[...] = jnp.swapaxes(k[...], 0, 1)
    vh[...] = jnp.swapaxes(v[...], 0, 1)
    qh[...] = jnp.swapaxes(q[...], 0, 1)
    gh[...] = jnp.swapaxes(g[...], 0, 1)

    @pl.when((place > 0) & (place < count - 1))
    def _():
        for h in range(all_heads):
            kv[h] = state_sum(kh[h], vh[h], leave_of(within, h, length))
            grad[h] = state_sum(qh[h], gh[h], enter_of(within, h, length))

    columns = within.T
    for h in range(all_heads):
        col[h] = jnp.broadcast_to(columns[:length, h : h + 1], (length, 128))


def merge_kernel(count, hop, start, got, kv, grad, fade, *rest):
    payload = rest[-2]
    place = lax.axis_index("seq")
    heads = got.shape[0]
    cut = slice(start, start + heads)
    for at, own in ((hop, kv), (count - 1 - hop, grad)):

        @pl.when(place == at)
        def _():
            payload[...] = (fade[cut] * got[...].astype(F32) + own[cut].astype(F32)).astype(BF16)


def intra_kernel(start, heads, col, row, qh, kh, vh, gh, *rest):
    qg, kg, vg = rest[-4:-1]
    length = qh.shape[1]
    edges = list(range(0, length, 256)) + [length]
    blocks = list(zip(edges[:-1], edges[1:]))

    def one(h, carry):
        q, k, v, g = qh[h], kh[h], vh[h], gh[h]
        qt, gt = q.T, g.T
        scores, probes = {}, {}
        for t0, t1 in blocks:
            for s0, s1 in blocks:
                if s0 > t0:
                    continue
                column = col[h, t0:t1, :]
                if s1 - s0 > 128:
                    column = jnp.concatenate([column, column], axis=1)
                spread = row[h, :, s0:s1] - column[:, : s1 - s0]
                weight = jnp.exp(jnp.minimum(spread, 0.0))
                if s0 == t0:
                    t = lax.broadcasted_iota(jnp.int32, spread.shape, 0)
                    s = lax.broadcasted_iota(jnp.int32, spread.shape, 1)
                    weight = jnp.where(t >= s, weight, 0.0)
                scores[t0, s0] = (dot(q[t0:t1], k[s0:s1], NT) * weight).astype(BF16)
                probes[t0, s0] = (dot(g[t0:t1], v[s0:s1], NT) * weight).astype(BF16)
        for t0, t1 in blocks:
            qg[h, t0:t1, :] = sum(dot(probes[t0, s0], k[s0:s1]) for s0, s1 in blocks if s0 <= t0)
        for s0, s1 in blocks:
            after = [(t0, t1) for t0, t1 in blocks if t0 >= s0]
            kg[h, s0:s1, :] = sum(dot(qt[:, t0:t1], probes[t0, s0]) for t0, t1 in after).T
            vg[h, s0:s1, :] = sum(dot(gt[:, t0:t1], scores[t0, s0]) for t0, t1 in after).T
        return carry

    lax.fori_loop(start, start + heads, one, 0, unroll=min(UNROLL, heads))


def terms(col, kh, vh, gh, state, start, h):
    length = kh.shape[1]

    def leave():
        return jnp.exp(col[h] - col[h, length - 1 : length, :])

    return (
        lambda: jnp.exp(-col[h]) * dot(gh[h], state[h - start], NT),
        lambda: leave() * dot(vh[h], state[h - start], NT),
        lambda: leave() * dot(kh[h], state[h - start]),
    )


def add_terms(which, target, slot, intra, col, kh, vh, gh, state, start, heads):
    def one(i, carry):
        h = start + i
        target[slot, i] = (intra[which][h] + terms(col, kh, vh, gh, state, start, h)[which]()).astype(BF16)
        return carry

    lax.fori_loop(0, heads, one, 0, unroll=min(2 * UNROLL, heads))


def out_copies(tokens, out, sem, parts=2):
    step = tokens.shape[0] // parts
    cuts = [slice(i * step, (i + 1) * step) for i in range(parts)]
    return [(cut, pltpu.make_async_copy(tokens.at[cut], out.at[cut], sem.at[i])) for i, cut in enumerate(cuts)]


def send_out(by_head, tokens, out, sem):
    for cut, copy in out_copies(tokens, out, sem):
        tokens[cut] = jnp.swapaxes(by_head[:, cut, :], 0, 1)
        copy.start()


def wait_out(tokens, out, sem):
    for _, copy in out_copies(tokens, out, sem):
        copy.wait()


def between_kernel(count, sizes, col, kh, vh, gh, qg, kg, vg, *rest):
    hops, chunks = count - 2, len(sizes)
    arrived = rest[: hops * chunks]
    *outs, state, by_head, tokens, sems = rest[-7:]
    intra = (qg, kg, vg)
    all_heads = kh.shape[0]
    place = lax.axis_index("seq")

    def take(end, came_from):
        @pl.when(place == end)
        def _():
            state[...] = jnp.zeros_like(state)

        for hop in range(1, count - 1):

            @pl.when(place == came_from(hop))
            def _():
                at = 0
                for c, heads in enumerate(sizes):
                    state[at : at + heads] = arrived[c * hops + hop - 1][...]
                    at += heads

    def write(which):
        add_terms(which, by_head, which, intra, col, kh, vh, gh, state, 0, all_heads)
        send_out(by_head[which], tokens.at[which], outs[which], sems.at[which])

    @pl.when(place < count - 1)
    def _():
        take(0, lambda hop: hop)
        write(0)

    @pl.when(place > 0)
    def _():
        take(count - 1, lambda hop: count - 1 - hop)
        write(1)
        write(2)

    @pl.when(place < count - 1)
    def _():
        wait_out(tokens.at[0], outs[0], sems.at[0])

    @pl.when(place > 0)
    def _():
        wait_out(tokens.at[1], outs[1], sems.at[1])
        wait_out(tokens.at[2], outs[2], sems.at[2])


def ends_kernel(count, start, col, kh, vh, gh, qg, kg, vg, got, *rest):
    by_head = rest[-1]
    heads = got.shape[0]
    place = lax.axis_index("seq")
    args = ((qg, kg, vg), col, kh, vh, gh, got, start, heads)

    @pl.when(place == count - 1)
    def _():
        add_terms(0, by_head, 0, *args)

    @pl.when(place == 0)
    def _():
        add_terms(1, by_head, 0, *args)
        add_terms(2, by_head, 1, *args)


def last_kernel(count, start, col, kh, vh, gh, qg, kg, vg, got, *rest):
    *outs, by_head, tokens, sems = rest[-6:]
    earlier = rest[:-9]
    heads = got.shape[0]
    place = lax.axis_index("seq")
    args = ((qg, kg, vg), col, kh, vh, gh, got, start, heads)

    def write(which, slot):
        add_terms(which, by_head, slot, *args)
        whole = jnp.concatenate([part[slot] for part in earlier] + [by_head[slot]], axis=0)
        send_out(whole, tokens.at[slot], outs[which], sems.at[slot])

    @pl.when(place == count - 1)
    def _():
        write(0, 0)
        wait_out(tokens.at[0], outs[0], sems.at[0])

    @pl.when(place == 0)
    def _():
        write(1, 0)
        write(2, 1)
        wait_out(tokens.at[0], outs[1], sems.at[0])
        wait_out(tokens.at[1], outs[2], sems.at[1])


def per_device(count, queries, keys, values, output_gradient, decay_exponent, forget_spikes):
    length, all_heads, size = queries.shape
    chunks = CHUNKS
    sizes = [all_heads // chunks + (c < all_heads % chunks) for c in range(chunks)]
    starts = [sum(sizes[:c]) for c in range(chunks)]
    spikes = forget_spikes.T
    shape = jax.ShapeDtypeStruct
    wide = -(-length // 128) * 128
    by_head = shape((all_heads, length, size), BF16)
    by_head_f = shape((all_heads, length, size), F32)
    states = shape((all_heads, size, size), BF16)
    full = shape(queries.shape, BF16)
    flops = 2 * length * size * size

    def state(c):
        return shape((sizes[c], size, size), BF16)

    def call(kernel, ins, outs, limit, cost, after=(), specs=None, out_spec=VMEM, **more):
        several = isinstance(outs, tuple)
        return pl.pallas_call(
            kernel,
            out_shape=outs,
            in_specs=(specs or [VMEM] * len(ins)) + [ANY] * len(after),
            out_specs=tuple(ANY if o is TOKEN else out_spec for o in outs) if several else out_spec,
            compiler_params=pltpu.CompilerParams(vmem_limit_bytes=limit * MIB),
            cost_estimate=pl.CostEstimate(flops=cost * flops, bytes_accessed=1 << 20, transcendentals=0),
            **more,
        )(*ins, *after)

    tensors = (queries, keys, values, output_gradient)
    raw = pltpu.VMEM(queries.shape, BF16)
    decay = decay_exponent[None, :]
    ranges = [range(a, a + n) for a, n in zip(starts, sizes)]
    payloads = []
    for part in (slice(0, 1), slice(1, chunks)):
        *several, token = call(
            functools.partial(first_kernel, count, ranges[part]),
            (decay, spikes, *tensors),
            (*(state(c) for c in range(chunks)[part]), TOKEN),
            52 if payloads else 60,
            sum(sizes[part]),
            specs=[ANY] * 6,
            scratch_shapes=[
                pltpu.VMEM(decay.shape, jnp.int32),
                pltpu.VMEM(spikes.shape, F32),
                raw,
                raw,
                pltpu.SemaphoreType.DMA((4,)),
            ],
        )
        payloads += several
    qh, kh, vh, gh, col, row, kv, grad, fade = call(
        functools.partial(sums_kernel, count),
        (decay, spikes, *tensors),
        (by_head,) * 4
        + (by_head_f, shape((all_heads, 1, wide), F32), states, states)
        + (shape((all_heads, 1, size), F32),),
        8,
        2 * all_heads,
        after=(token,),
    )

    intra, placed, done, merged = [], 0, (), ()
    ins = (col, row, qh, kh, vh, gh)

    def span_products(hop, chunk, before=None):
        nonlocal intra, placed, done
        due = all_heads if before is None else all_heads * DUE.get((hop, chunk), 0) // 16
        if due > placed:
            *intra, token = call(
                functools.partial(intra_kernel, placed, due - placed),
                (*ins, *intra),
                (by_head_f,) * 3 + (TOKEN,),
                8,
                5 * (due - placed),
                after=merged if before is None else before,
                input_output_aliases={len(ins) + j: j for j in range(len(intra))},
            )
            placed, done = due, (token,)

    arrived = [[] for _ in range(chunks)]
    span_products(0, 0, ())
    for hop in range(1, count):
        pairs = [(hop - 1, hop), (count - hop, count - hop - 1)]
        for c in range(chunks):
            got = lax.ppermute(payloads[c], "seq", pairs)
            arrived[c].append(got)
            if hop < count - 1:
                payloads[c], *merged = call(
                    functools.partial(merge_kernel, count, hop, starts[c]),
                    (got, kv, grad, fade),
                    (state(c), TOKEN),
                    4,
                    0,
                    after=done,
                )
                done = ()
                span_products(hop, c, merged)
    span_products(0, 0)

    common = (col, kh, vh, gh, *intra)
    came = [a for c in range(chunks) for a in arrived[c][:-1]]
    outs = call(
        functools.partial(between_kernel, count, sizes),
        (*common, *came),
        (full,) * 3,
        16,
        3 * all_heads,
        after=merged,
        out_spec=ANY,
        scratch_shapes=[
            pltpu.VMEM(states.shape, BF16),
            pltpu.VMEM((3,) + by_head.shape, BF16),
            pltpu.VMEM((3,) + full.shape, BF16),
            pltpu.SemaphoreType.DMA((3, 2)),
        ],
    )
    earlier = []
    for c in range(chunks - 1):
        earlier.append(
            call(
                functools.partial(ends_kernel, count, starts[c]),
                (*common, arrived[c][-1]),
                shape((2, sizes[c], length, size), BF16),
                8,
                2 * sizes[c],
                after=earlier[-1:],
            )
        )
    ins = (*common, arrived[-1][-1], *earlier)
    return tuple(
        call(
            functools.partial(last_kernel, count, starts[-1]),
            (*ins, *outs),
            (full,) * 3,
            8,
            2 * sizes[-1],
            specs=[VMEM] * len(ins) + [ANY] * 3,
            out_spec=ANY,
            scratch_shapes=[
                pltpu.VMEM((2, sizes[-1], length, size), BF16),
                pltpu.VMEM((2,) + full.shape, BF16),
                pltpu.SemaphoreType.DMA((2, 2)),
            ],
            input_output_aliases={len(ins) + j: j for j in range(3)},
        )
    )


def solution(mesh):
    tokens = P(("groups", "seq"), ("head", "sub"), None)
    in_specs = (tokens,) * 4 + (P(("head", "sub")), P(("groups", "seq"), ("head", "sub")))
    return jax.shard_map(
        functools.partial(per_device, mesh.shape["seq"]),
        mesh=mesh,
        in_specs=in_specs,
        out_specs=(tokens,) * 3,
        check_vma=False,
    )
```

time: 47.4 us -> 41.6 us (0.88)
  waiting for transfers between devices: 12.1 us -> 5.86 us
  starting transfers between devices: 7.7 us -> 11.3 us
  local copies, waits for them, and re-layouts: 2.74 us -> 0.03 us
    ppermute x6 -> x9, waiting for transfers between devices: 12.1 us -> 5.86 us  [per_device(): got = lax.ppermute(payloads[c], 'seq', pairs)]
    ppermute x6 -> x9, starting transfers between devices: 7.7 us -> 11.3 us  [per_device(): got = lax.ppermute(payloads[c], 'seq', pairs)]
    unnamed x12, local copies, waits for them, and re-layouts: 2.74 us -> 0.03 us
    pallas_call x10 -> x16, Pallas kernels: 23.3 us -> 23 us  [call(): pl.pallas_call(kernel, out_shape=outs, in_specs=(specs or [VMEM] * len(in...]
  transfers between devices with their start and end apart: 6 -> 9, of which waited for: 3 -> 3; matrix products, arithmetic and copies ran while one was open for 0% -> 0% of each run, Pallas kernels for 30% -> 42%
where the time goes in v2:
time: 41.6 us; the launch traced here: 41.3 us
  Pallas kernels  23 us (55%)
  starting transfers between devices  11.3 us (27%)
  waiting for transfers between devices  5.86 us (14%)
  between operations  1.11 us (3%)
    pallas_call x16, Pallas kernels, call(): pl.pallas_call(kernel, out_shape=outs, in_specs=(specs or [VMEM] * len(in...  23 us
    ppermute x9, starting transfers between devices, per_device(): got = lax.ppermute(payloads[c], 'seq', pairs)  11.3 us
    ppermute x9, waiting for transfers between devices, per_device(): got = lax.ppermute(payloads[c], 'seq', pairs)  5.86 us
  transfers between devices with their start and end apart: 9, of which 3 were waited for; matrix products, arithmetic and copies ran while one was open for 0% of the time, Pallas kernels for 42%

profile of v2, /device:TPU:0, one launch (start us, length us, event | category | flops | bytes accessed | tf_op | source)
XLA Modules:
  0.0 41.3 jit_solution(12838789240048340787)
XLA Ops:
  0.7 3.3 %shard_map.94 = (bf16[6,128,128]{2,1,0:T(8,128)(2,1)}, f32[8,128]{1,0:T(8,128)}) custom-call(s32[1,16]{1,0:T(1,128)} %bitcast.5, f32[16,352]{1,0:T(8,128)} %bitcast.2, bf16[352,16,128]{2,1,0:T(8,128)(2,1)} %q.5, bf16[352,16,128]{2,1,0:T(8,128)(2,1)} %k.5, bf16[352,16,128]{2,1,0:T(8,128)(2,1)} %v.5, bf16[352,16,128]{2,1,0:T(8,128)(2,1)} %g.5), custom_call_target="tpu_custom_call" | custom-call | flops 69206016 | bytes 1048576 | tf_op jit(solution)/shard_map/pallas_call | solution.py:307
  4.0 0.0 copy-start.2
  4.0 0.0 copy-start.3
  4.0 2.6 %collective-permute-start.5 = (bf16[6,128,128]{2,1,0:T(8,128)(2,1)}, bf16[6,128,128]{2,1,0:T(8,128)(2,1)S(1)}, u32[]{:S(2)}, u32[]{:S(2)}) collective-permute-start(bf16[6,128,128]{2,1,0:T(8,128)(2,1)} %get-tuple-element.65), channel_id=1, source_target_pairs={{0,4},{12,8},{1,5},{13,9},{2,6},{14,10},{3,7},{15,11},{16,20},{28,... | collective-permute-start | bytes 589832 | tf_op jit(solution)/shard_map/ppermute | solution.py:373
  6.7 2.9 %shard_map.85 = (bf16[5,128,128]{2,1,0:T(8,128)(2,1)S(1)}, bf16[5,128,128]{2,1,0:T(8,128)(2,1)S(1)}, f32[8,128]{1,0:T(8,128)S(1)}) custom-call(s32[1,16]{1,0:T(1,128)S(1)} %bitcast.6, f32[16,352]{1,0:T(8,128)S(1)} %bitcast.3, bf16[352,16,128]{2,1,0:T(8,128)(2,1)S(1)} %copy-done, bf16[352,16,128]{2,1,0:T(8,128)(2,1)} %k.5, bf16[352,16,128]{2,1,0:T(8,128)(2,1)} %v.5, ...), custom_call_target="tpu_custom_call" | custom-call | flops 115343360 | bytes 1048576 | tf_op jit(solution)/shard_map/pallas_call | solution.py:307
  9.6 1.3 %collective-permute-start = (bf16[5,128,128]{2,1,0:T(8,128)(2,1)S(1)}, bf16[5,128,128]{2,1,0:T(8,128)(2,1)S(1)}, u32[]{:S(2)}, u32[]{:S(2)}) collective-permute-start(bf16[5,128,128]{2,1,0:T(8,128)(2,1)S(1)} %get-tuple-element.48), channel_id=1, source_target_pairs={{0,4},{12,8},{1,5},{13,9},{2,6},{14,10},{3,7},{15,11},{16,20},{28,... | collective-permute-start | bytes 491528 | tf_op jit(solution)/shard_map/ppermute | solution.py:373
  10.9 1.3 %collective-permute-start.2 = (bf16[5,128,128]{2,1,0:T(8,128)(2,1)S(1)}, bf16[5,128,128]{2,1,0:T(8,128)(2,1)S(1)}, u32[]{:S(2)}, u32[]{:S(2)}) collective-permute-start(bf16[5,128,128]{2,1,0:T(8,128)(2,1)S(1)} %get-tuple-element.57), channel_id=1, source_target_pairs={{0,4},{12,8},{1,5},{13,9},{2,6},{14,10},{3,7},{15,11},{16,20},{28,... | collective-permute-start | bytes 491528 | tf_op jit(solution)/shard_map/ppermute | solution.py:373
  12.3 3.5 %shard_map.86 = (bf16[16,352,128]{2,1,0:T(8,128)(2,1)S(1)}, bf16[16,352,128]{2,1,0:T(8,128)(2,1)S(1)}, bf16[16,352,128]{2,1,0:T(8,128)(2,1)S(1)}, bf16[16,352,12...) custom-call(s32[1,16]{1,0:T(1,128)S(1)} %bitcast.7, ...), custom_call_target="tpu_custom_call" | custom-call | flops 369098752 | bytes 1048576 | tf_op jit(solution)/shard_map/pallas_call | solution.py:307
  15.7 2.0 %shard_map.87 = (f32[16,352,128]{2,1,0:T(8,128)S(1)}, f32[16,352,128]{2,1,0:T(8,128)S(1)}, f32[16,352,128]{2,1,0:T(8,128)S(1)}, f32[8,128]{1,0:T(8,128)S(1)}) custom-call(f32[16,352,128]{2,1,0:T(8,128)S(1)} %get-tuple-element.39.col, f32[16,1,384]{2,1,0:T(1,128)S(1)} %get-tuple-element.43.row, bf16[16,352,128]{2,1,0:T(8,128)(2,1)S(1)} %get-tuple-element.44.qh, ...), custom_call_target="tpu_custom_call" | custom-call | flops 288358400 | bytes 1048576 | tf_op jit(solution)/shard_map/pallas_call | solution.py:307
  17.8 0.7 %collective-permute-start.6 = (bf16[6,128,128]{2,1,0:T(8,128)(2,1)S(1)}, bf16[6,128,128]{2,1,0:T(8,128)(2,1)S(1)}, u32[]{:S(2)}, u32[]{:S(2)}) collective-permute-start(bf16[6,128,128]{2,1,0:T(8,128)(2,1)S(1)} %get-tuple-element.67), channel_id=1, source_target_pairs={{4,8},{8,4},{5,9},{9,5},{6,10},{10,6},{7,11},{11,7},{20,24},{24,20... | collective-permute-start | bytes 589832 | tf_op jit(solution)/shard_map/ppermute | solution.py:373
  18.5 0.7 %collective-permute-start.1 = (bf16[5,128,128]{2,1,0:T(8,128)(2,1)S(1)}, bf16[5,128,128]{2,1,0:T(8,128)(2,1)S(1)}, u32[]{:S(2)}, u32[]{:S(2)}) collective-permute-start(bf16[5,128,128]{2,1,0:T(8,128)(2,1)S(1)} %get-tuple-element.52), channel_id=1, source_target_pairs={{4,8},{8,4},{5,9},{9,5},{6,10},{10,6},{7,11},{11,7},{20,24},{24,20... | collective-permute-start | bytes 491528 | tf_op jit(solution)/shard_map/ppermute | solution.py:373
  19.2 0.7 %collective-permute-start.3 = (bf16[5,128,128]{2,1,0:T(8,128)(2,1)S(1)}, bf16[5,128,128]{2,1,0:T(8,128)(2,1)S(1)}, u32[]{:S(2)}, u32[]{:S(2)}) collective-permute-start(bf16[5,128,128]{2,1,0:T(8,128)(2,1)S(1)} %get-tuple-element.58), channel_id=1, source_target_pairs={{4,8},{8,4},{5,9},{9,5},{6,10},{10,6},{7,11},{11,7},{20,24},{24,20... | collective-permute-start | bytes 491528 | tf_op jit(solution)/shard_map/ppermute | solution.py:373
  19.9 1.3 %collective-permute-start.7 = (bf16[6,128,128]{2,1,0:T(8,128)(2,1)S(1)}, bf16[6,128,128]{2,1,0:T(8,128)(2,1)S(1)}, u32[]{:S(2)}, u32[]{:S(2)}) collective-permute-start(bf16[6,128,128]{2,1,0:T(8,128)(2,1)S(1)} %get-tuple-element.68), channel_id=1, source_target_pairs={{8,12},{4,0},{9,13},{5,1},{10,14},{6,2},{11,15},{7,3},{24,28},{20,... | collective-permute-start | bytes 589832 | tf_op jit(solution)/shard_map/ppermute | solution.py:373
  21.3 1.5 %collective-permute-start.8 = (bf16[5,128,128]{2,1,0:T(8,128)(2,1)S(1)}, bf16[5,128,128]{2,1,0:T(8,128)(2,1)S(1)}, u32[]{:S(2)}, u32[]{:S(2)}) collective-permute-start(bf16[5,128,128]{2,1,0:T(8,128)(2,1)S(1)} %get-tuple-element.69), channel_id=1, source_target_pairs={{8,12},{4,0},{9,13},{5,1},{10,14},{6,2},{11,15},{7,3},{24,28},{20,... | collective-permute-start | bytes 491528 | tf_op jit(solution)/shard_map/ppermute | solution.py:373
  22.8 1.7 %shard_map.90 = (f32[16,352,128]{2,1,0:T(8,128)S(1)}, f32[16,352,128]{2,1,0:T(8,128)S(1)}, f32[16,352,128]{2,1,0:T(8,128)S(1)}, f32[8,128]{1,0:T(8,128)S(1)}) custom-call(f32[16,352,128]{2,1,0:T(8,128)S(1)} %get-tuple-element.39.col, f32[16,1,384]{2,1,0:T(1,128)S(1)} %get-tuple-element.43.row, ...), custom_call_target="tpu_custom_call", output_to_operand_aliasing={{0}: (6, {}), {1}: (7, {}), {2}: (8, {})} | custom-call | flops 230686720 | bytes 1048576 | tf_op jit(solution)/shard_map/pallas_call | solution.py:307
  24.5 1.3 %collective-permute-start.4 = (bf16[5,128,128]{2,1,0:T(8,128)(2,1)S(1)}, bf16[5,128,128]{2,1,0:T(8,128)(2,1)S(1)}, u32[]{:S(2)}, u32[]{:S(2)}) collective-permute-start(bf16[5,128,128]{2,1,0:T(8,128)(2,1)S(1)} %get-tuple-element.64), channel_id=1, source_target_pairs={{8,12},{4,0},{9,13},{5,1},{10,14},{6,2},{11,15},{7,3},{24,28},{20,... | collective-permute-start | bytes 491528 | tf_op jit(solution)/shard_map/ppermute | solution.py:373
  25.8 3.5 %shard_map.93 = (f32[16,352,128]{2,1,0:T(8,128)S(1)}, f32[16,352,128]{2,1,0:T(8,128)S(1)}, f32[16,352,128]{2,1,0:T(8,128)S(1)}, f32[8,128]{1,0:T(8,128)}) custom-call(f32[16,352,128]{2,1,0:T(8,128)S(1)} %get-tuple-element.39.col, f32[16,1,384]{2,1,0:T(1,128)S(1)} %get-tuple-element.43.row, ...), custom_call_target="tpu_custom_call", output_to_operand_aliasing={{0}: (6, {}), {1}: (7, {}), {2}: (8, {})} | custom-call | flops 403701760 | bytes 1048576 | tf_op jit(solution)/shard_map/pallas_call | solution.py:307
  29.3 2.3 %shard_map.99 = (bf16[352,16,128]{2,1,0:T(8,128)(2,1)}, bf16[352,16,128]{2,1,0:T(8,128)(2,1)}, bf16[352,16,128]{2,1,0:T(8,128)(2,1)}) custom-call(f32[16,352,128]{2,1,0:T(8,128)S(1)} %get-tuple-element.39.col, bf16[16,352,128]{2,1,0:T(8,128)(2,1)S(1)} %get-tuple-element.40.kh, bf16[16,352,128]{2,1,0:T(8,128)(2,1)S(1)} %get-tuple-element.41.vh, ...), custom_call_target="tpu_custom_call" | custom-call | flops 553648128 | bytes 1048576 | tf_op jit(solution)/shard_map/pallas_call | solution.py:307
  31.6 1.4 %collective-permute-done.7.got = bf16[6,128,128]{2,1,0:T(8,128)(2,1)S(1)} collective-permute-done((bf16[6,128,128]{2,1,0:T(8,128)(2,1)S(1)}, bf16[6,128,128]{2,1,0:T(8,128)(2,1)S(1)}, u32[]{:S(2)}, u32[]{:S(2)}) %collective-permute-start.7) | collective-permute-done | bytes 196640 | tf_op jit(solution)/shard_map/ppermute | solution.py:373
  33.0 0.6 %shard_map.97.rest_0_ = bf16[2,6,352,128]{3,2,1,0:T(8,128)(2,1)S(1)} custom-call(f32[16,352,128]{2,1,0:T(8,128)S(1)} %get-tuple-element.39.col, bf16[16,352,128]{2,1,0:T(8,128)(2,1)S(1)} %get-tuple-element.40.kh, bf16[16,352,128]{2,1,0:T(8,128)(2,1)S(1)} %get-tuple-element.41.vh, bf16[16,352,128]{2,1,0:T(8,128)(2,1)S(1)} %get-tuple-element.42.gh, ...), custom_call_target="tpu_custom_call" | custom-call | flops 138412032 | bytes 1048576 | tf_op jit(solution)/shard_map/pallas_call | solution.py:307
  33.6 2.9 %collective-permute-done.8.got = bf16[5,128,128]{2,1,0:T(8,128)(2,1)S(1)} collective-permute-done((bf16[5,128,128]{2,1,0:T(8,128)(2,1)S(1)}, bf16[5,128,128]{2,1,0:T(8,128)(2,1)S(1)}, u32[]{:S(2)}, u32[]{:S(2)}) %collective-permute-start.8) | collective-permute-done | bytes 163872 | tf_op jit(solution)/shard_map/ppermute | solution.py:373
  36.5 0.5 %shard_map.98.rest_1_ = bf16[2,5,352,128]{3,2,1,0:T(8,128)(2,1)S(1)} custom-call(f32[16,352,128]{2,1,0:T(8,128)S(1)} %get-tuple-element.39.col, bf16[16,352,128]{2,1,0:T(8,128)(2,1)S(1)} %get-tuple-element.40.kh, bf16[16,352,128]{2,1,0:T(8,128)(2,1)S(1)} %get-tuple-element.41.vh, bf16[16,352,128]{2,1,0:T(8,128)(2,1)S(1)} %get-tuple-element.42.gh, ...), custom_call_target="tpu_custom_call" | custom-call | flops 115343360 | bytes 1048576 | tf_op jit(solution)/shard_map/pallas_call | solution.py:307
  37.1 1.6 %collective-permute-done.4.got = bf16[5,128,128]{2,1,0:T(8,128)(2,1)S(1)} collective-permute-done((bf16[5,128,128]{2,1,0:T(8,128)(2,1)S(1)}, bf16[5,128,128]{2,1,0:T(8,128)(2,1)S(1)}, u32[]{:S(2)}, u32[]{:S(2)}) %collective-permute-start.4) | collective-permute-done | bytes 163872 | tf_op jit(solution)/shard_map/ppermute | solution.py:373
  38.6 2.5 %shard_map.100 = (bf16[352,16,128]{2,1,0:T(8,128)(2,1)}, bf16[352,16,128]{2,1,0:T(8,128)(2,1)}, bf16[352,16,128]{2,1,0:T(8,128)(2,1)}) custom-call(f32[16,352,128]{2,1,0:T(8,128)S(1)} %get-tuple-element.39.col, bf16[16,352,128]{2,1,0:T(8,128)(2,1)S(1)} %get-tuple-element.40.kh, ...), custom_call_target="tpu_custom_call", output_to_operand_aliasing={{0}: (10, {}), {1}: (11, {}), {2}: (12, {})} | custom-call | flops 115343360 | bytes 1048576 | tf_op jit(solution)/shard_map/pallas_call | solution.py:307
  (22 shorter events, 0.2 us)
Async XLA Ops:
  0.6 6.0 %copy-start = (bf16[352,16,128]{2,1,0:T(8,128)(2,1)S(1)}, bf16[352,16,128]{2,1,0:T(8,128)(2,1)}, u32[]{:S(2)}) copy-start(bf16[352,16,128]{2,1,0:T(8,128)(2,1)} %q.5) | copy-start | bytes 4325380
  0.6 6.0 %copy-start.4 = (f32[352,16]{0,1:T(8,128)S(1)}, f32[352,16]{0,1:T(8,128)}, u32[]{:S(2)}) copy-start(f32[352,16]{0,1:T(8,128)} %param.11) | copy-start | bytes 67588
  0.7 6.0 %copy-start.5 = (s32[16]{0:T(128)S(1)}, s32[16]{0:T(128)}, u32[]{:S(2)}) copy-start(s32[16]{0:T(128)} %param.10) | copy-start | bytes 196
  4.0 8.3 %copy-start.1 = (bf16[352,16,128]{2,1,0:T(8,128)(2,1)S(1)}, bf16[352,16,128]{2,1,0:T(8,128)(2,1)}, u32[]{:S(2)}) copy-start(bf16[352,16,128]{2,1,0:T(8,128)(2,1)} %k.5) | copy-start | bytes 4325380
  4.0 8.3 %copy-start.2 = (bf16[352,16,128]{2,1,0:T(8,128)(2,1)S(1)}, bf16[352,16,128]{2,1,0:T(8,128)(2,1)}, u32[]{:S(2)}) copy-start(bf16[352,16,128]{2,1,0:T(8,128)(2,1)} %v.5) | copy-start | bytes 4325380
  4.0 8.3 %copy-start.3 = (bf16[352,16,128]{2,1,0:T(8,128)(2,1)S(1)}, bf16[352,16,128]{2,1,0:T(8,128)(2,1)}, u32[]{:S(2)}) copy-start(bf16[352,16,128]{2,1,0:T(8,128)(2,1)} %g.5) | copy-start | bytes 4325380
  4.0 13.7 %collective-permute-start.5 = (bf16[6,128,128]{2,1,0:T(8,128)(2,1)}, bf16[6,128,128]{2,1,0:T(8,128)(2,1)S(1)}, u32[]{:S(2)}, u32[]{:S(2)}) collective-permute-start(bf16[6,128,128]{2,1,0:T(8,128)(2,1)} %get-tuple-element.65), channel_id=1, source_target_pairs={{0,4},{12,8},{1,5},{13,9},{2,6},{14,10},{3,7},{15,11},{16,20},{28,... | collective-permute-start | bytes 589832 | tf_op jit(solution)/shard_map/ppermute | solution.py:373
  9.6 8.8 %collective-permute-start = (bf16[5,128,128]{2,1,0:T(8,128)(2,1)S(1)}, bf16[5,128,128]{2,1,0:T(8,128)(2,1)S(1)}, u32[]{:S(2)}, u32[]{:S(2)}) collective-permute-start(bf16[5,128,128]{2,1,0:T(8,128)(2,1)S(1)} %get-tuple-element.48), channel_id=1, source_target_pairs={{0,4},{12,8},{1,5},{13,9},{2,6},{14,10},{3,7},{15,11},{16,20},{28,... | collective-permute-start | bytes 491528 | tf_op jit(solution)/shard_map/ppermute | solution.py:373
  10.9 8.3 %collective-permute-start.2 = (bf16[5,128,128]{2,1,0:T(8,128)(2,1)S(1)}, bf16[5,128,128]{2,1,0:T(8,128)(2,1)S(1)}, u32[]{:S(2)}, u32[]{:S(2)}) collective-permute-start(bf16[5,128,128]{2,1,0:T(8,128)(2,1)S(1)} %get-tuple-element.57), channel_id=1, source_target_pairs={{0,4},{12,8},{1,5},{13,9},{2,6},{14,10},{3,7},{15,11},{16,20},{28,... | collective-permute-start | bytes 491528 | tf_op jit(solution)/shard_map/ppermute | solution.py:373
  17.8 2.1 %collective-permute-start.6 = (bf16[6,128,128]{2,1,0:T(8,128)(2,1)S(1)}, bf16[6,128,128]{2,1,0:T(8,128)(2,1)S(1)}, u32[]{:S(2)}, u32[]{:S(2)}) collective-permute-start(bf16[6,128,128]{2,1,0:T(8,128)(2,1)S(1)} %get-tuple-element.67), channel_id=1, source_target_pairs={{4,8},{8,4},{5,9},{9,5},{6,10},{10,6},{7,11},{11,7},{20,24},{24,20... | collective-permute-start | bytes 589832 | tf_op jit(solution)/shard_map/ppermute | solution.py:373
  18.5 2.7 %collective-permute-start.1 = (bf16[5,128,128]{2,1,0:T(8,128)(2,1)S(1)}, bf16[5,128,128]{2,1,0:T(8,128)(2,1)S(1)}, u32[]{:S(2)}, u32[]{:S(2)}) collective-permute-start(bf16[5,128,128]{2,1,0:T(8,128)(2,1)S(1)} %get-tuple-element.52), channel_id=1, source_target_pairs={{4,8},{8,4},{5,9},{9,5},{6,10},{10,6},{7,11},{11,7},{20,24},{24,20... | collective-permute-start | bytes 491528 | tf_op jit(solution)/shard_map/ppermute | solution.py:373
  19.2 5.2 %collective-permute-start.3 = (bf16[5,128,128]{2,1,0:T(8,128)(2,1)S(1)}, bf16[5,128,128]{2,1,0:T(8,128)(2,1)S(1)}, u32[]{:S(2)}, u32[]{:S(2)}) collective-permute-start(bf16[5,128,128]{2,1,0:T(8,128)(2,1)S(1)} %get-tuple-element.58), channel_id=1, source_target_pairs={{4,8},{8,4},{5,9},{9,5},{6,10},{10,6},{7,11},{11,7},{20,24},{24,20... | collective-permute-start | bytes 491528 | tf_op jit(solution)/shard_map/ppermute | solution.py:373
  19.9 13.1 %collective-permute-start.7 = (bf16[6,128,128]{2,1,0:T(8,128)(2,1)S(1)}, bf16[6,128,128]{2,1,0:T(8,128)(2,1)S(1)}, u32[]{:S(2)}, u32[]{:S(2)}) collective-permute-start(bf16[6,128,128]{2,1,0:T(8,128)(2,1)S(1)} %get-tuple-element.68), channel_id=1, source_target_pairs={{8,12},{4,0},{9,13},{5,1},{10,14},{6,2},{11,15},{7,3},{24,28},{20,... | collective-permute-start | bytes 589832 | tf_op jit(solution)/shard_map/ppermute | solution.py:373
  21.3 15.2 %collective-permute-start.8 = (bf16[5,128,128]{2,1,0:T(8,128)(2,1)S(1)}, bf16[5,128,128]{2,1,0:T(8,128)(2,1)S(1)}, u32[]{:S(2)}, u32[]{:S(2)}) collective-permute-start(bf16[5,128,128]{2,1,0:T(8,128)(2,1)S(1)} %get-tuple-element.69), channel_id=1, source_target_pairs={{8,12},{4,0},{9,13},{5,1},{10,14},{6,2},{11,15},{7,3},{24,28},{20,... | collective-permute-start | bytes 491528 | tf_op jit(solution)/shard_map/ppermute | solution.py:373
  24.5 14.1 %collective-permute-start.4 = (bf16[5,128,128]{2,1,0:T(8,128)(2,1)S(1)}, bf16[5,128,128]{2,1,0:T(8,128)(2,1)S(1)}, u32[]{:S(2)}, u32[]{:S(2)}) collective-permute-start(bf16[5,128,128]{2,1,0:T(8,128)(2,1)S(1)} %get-tuple-element.64), channel_id=1, source_target_pairs={{8,12},{4,0},{9,13},{5,1},{10,14},{6,2},{11,15},{7,3},{24,28},{20,... | collective-permute-start | bytes 491528 | tf_op jit(solution)/shard_map/ppermute | solution.py:373

commit v3 on v2

--- a/solution.py
+++ b/solution.py
@@ -72,11 +72,13 @@
         fades = {h: fade_of(within, h, length) for part in heads for h in part}
         for copy in copies[2:]:
             copy.wait()
-        a_h = jnp.swapaxes(left[...], 0, 1)
-        b_h = jnp.swapaxes(right[...], 0, 1)
+        low = heads[0][0] // 8 * 8
+        high = min(-(-(heads[-1][-1] + 1) // 8) * 8, left.shape[1])
+        a_h = jnp.swapaxes(left[:, low:high, :], 0, 1)
+        b_h = jnp.swapaxes(right[:, low:high, :], 0, 1)
         for part, payload in zip(heads, payloads):
             for i, h in enumerate(part):
-                payload[i] = state_sum(a_h[h], b_h[h], fades[h])
+                payload[i] = state_sum(a_h[h - low], b_h[h - low], fades[h])
 
     @pl.when(place == 0)
     def _():
@@ -323,7 +325,7 @@
         *several, token = call(
             functools.partial(first_kernel, count, ranges[part]),
             (decay, spikes, *tensors),
-            (*(state(c) for c in range(chunks)[part]), TOKEN),
+            (*(pltpu.VMEM((sizes[c], size, size), BF16) for c in range(chunks)[part]), TOKEN),
             52 if payloads else 60,
             sum(sizes[part]),
             specs=[ANY] * 6,

time: 41.6 us -> 40.5 us (0.974)
  Pallas kernels: 23 us -> 22.3 us
  waiting for transfers between devices: 5.86 us -> 5.44 us
    pallas_call x16, Pallas kernels: 23 us -> 22.3 us  [call(): pl.pallas_call(kernel, out_shape=outs, in_specs=(specs or [VMEM] * len(in...]
    ppermute x9, waiting for transfers between devices: 5.86 us -> 5.44 us  [per_device(): got = lax.ppermute(payloads[c], 'seq', pairs)]
  transfers between devices with their start and end apart: 9 -> 9, of which waited for: 3 -> 3; matrix products, arithmetic and copies ran while one was open for 0% -> 0% of each run, Pallas kernels for 42% -> 43%
where the time goes in v3:
time: 40.5 us; the launch traced here: 40.2 us
  Pallas kernels  22.3 us (55%)
  starting transfers between devices  11.3 us (28%)
  waiting for transfers between devices  5.44 us (13%)
  between operations  1.11 us (3%)
    pallas_call x16, Pallas kernels, call(): pl.pallas_call(kernel, out_shape=outs, in_specs=(specs or [VMEM] * len(in...  22.3 us
    ppermute x9, starting transfers between devices, per_device(): got = lax.ppermute(payloads[c], 'seq', pairs)  11.3 us
    ppermute x9, waiting for transfers between devices, per_device(): got = lax.ppermute(payloads[c], 'seq', pairs)  5.44 us
  transfers between devices with their start and end apart: 9, of which 3 were waited for; matrix products, arithmetic and copies ran while one was open for 0% of the time, Pallas kernels for 43%

profile of v3, /device:TPU:0, one launch (start us, length us, event | category | flops | bytes accessed | tf_op | source)
XLA Modules:
  0.0 40.2 jit_solution(15499212679901610445)
XLA Ops:
  0.7 2.6 %shard_map.94 = (bf16[6,128,128]{2,1,0:T(8,128)(2,1)S(1)}, f32[8,128]{1,0:T(8,128)}) custom-call(s32[1,16]{1,0:T(1,128)} %bitcast.5, f32[16,352]{1,0:T(8,128)} %bitcast.2, bf16[352,16,128]{2,1,0:T(8,128)(2,1)} %q.5, bf16[352,16,128]{2,1,0:T(8,128)(2,1)} %k.5, bf16[352,16,128]{2,1,0:T(8,128)(2,1)} %v.5, bf16[352,16,128]{2,1,0:T(8,128)(2,1)} %g.5), custom_call_target="tpu_custom_call" | custom-call | flops 69206016 | bytes 1048576 | tf_op jit(solution)/shard_map/pallas_call | solution.py:309
  3.3 0.0 copy-start.1
  3.3 0.0 copy-start.3
  3.3 2.6 %collective-permute-start.5 = (bf16[6,128,128]{2,1,0:T(8,128)(2,1)S(1)}, bf16[6,128,128]{2,1,0:T(8,128)(2,1)S(1)}, u32[]{:S(2)}, u32[]{:S(2)}) collective-permute-start(bf16[6,128,128]{2,1,0:T(8,128)(2,1)S(1)} %get-tuple-element.65), channel_id=1, source_target_pairs={{0,4},{12,8},{1,5},{13,9},{2,6},{14,10},{3,7},{15,11},{16,20},{28,... | collective-permute-start | bytes 589832 | tf_op jit(solution)/shard_map/ppermute | solution.py:375
  6.0 2.9 %shard_map.85 = (bf16[5,128,128]{2,1,0:T(8,128)(2,1)S(1)}, bf16[5,128,128]{2,1,0:T(8,128)(2,1)S(1)}, f32[8,128]{1,0:T(8,128)S(1)}) custom-call(s32[1,16]{1,0:T(1,128)S(1)} %bitcast.6, f32[16,352]{1,0:T(8,128)S(1)} %bitcast.3, bf16[352,16,128]{2,1,0:T(8,128)(2,1)S(1)} %copy-done, bf16[352,16,128]{2,1,0:T(8,128)(2,1)} %k.5, bf16[352,16,128]{2,1,0:T(8,128)(2,1)} %v.5, ...), custom_call_target="tpu_custom_call" | custom-call | flops 115343360 | bytes 1048576 | tf_op jit(solution)/shard_map/pallas_call | solution.py:309
  9.0 1.3 %collective-permute-start = (bf16[5,128,128]{2,1,0:T(8,128)(2,1)S(1)}, bf16[5,128,128]{2,1,0:T(8,128)(2,1)S(1)}, u32[]{:S(2)}, u32[]{:S(2)}) collective-permute-start(bf16[5,128,128]{2,1,0:T(8,128)(2,1)S(1)} %get-tuple-element.48), channel_id=1, source_target_pairs={{0,4},{12,8},{1,5},{13,9},{2,6},{14,10},{3,7},{15,11},{16,20},{28,... | collective-permute-start | bytes 491528 | tf_op jit(solution)/shard_map/ppermute | solution.py:375
  10.3 1.3 %collective-permute-start.2 = (bf16[5,128,128]{2,1,0:T(8,128)(2,1)S(1)}, bf16[5,128,128]{2,1,0:T(8,128)(2,1)S(1)}, u32[]{:S(2)}, u32[]{:S(2)}) collective-permute-start(bf16[5,128,128]{2,1,0:T(8,128)(2,1)S(1)} %get-tuple-element.57), channel_id=1, source_target_pairs={{0,4},{12,8},{1,5},{13,9},{2,6},{14,10},{3,7},{15,11},{16,20},{28,... | collective-permute-start | bytes 491528 | tf_op jit(solution)/shard_map/ppermute | solution.py:375
  11.6 3.5 %shard_map.86 = (bf16[16,352,128]{2,1,0:T(8,128)(2,1)S(1)}, bf16[16,352,128]{2,1,0:T(8,128)(2,1)S(1)}, bf16[16,352,128]{2,1,0:T(8,128)(2,1)S(1)}, bf16[16,352,12...) custom-call(s32[1,16]{1,0:T(1,128)S(1)} %bitcast.7, ...), custom_call_target="tpu_custom_call" | custom-call | flops 369098752 | bytes 1048576 | tf_op jit(solution)/shard_map/pallas_call | solution.py:309
  15.1 2.0 %shard_map.87 = (f32[16,352,128]{2,1,0:T(8,128)S(1)}, f32[16,352,128]{2,1,0:T(8,128)S(1)}, f32[16,352,128]{2,1,0:T(8,128)S(1)}, f32[8,128]{1,0:T(8,128)S(1)}) custom-call(f32[16,352,128]{2,1,0:T(8,128)S(1)} %get-tuple-element.39.col, f32[16,1,384]{2,1,0:T(1,128)S(1)} %get-tuple-element.43.row, bf16[16,352,128]{2,1,0:T(8,128)(2,1)S(1)} %get-tuple-element.44.qh, ...), custom_call_target="tpu_custom_call" | custom-call | flops 288358400 | bytes 1048576 | tf_op jit(solution)/shard_map/pallas_call | solution.py:309
  17.1 0.7 %collective-permute-start.6 = (bf16[6,128,128]{2,1,0:T(8,128)(2,1)S(1)}, bf16[6,128,128]{2,1,0:T(8,128)(2,1)S(1)}, u32[]{:S(2)}, u32[]{:S(2)}) collective-permute-start(bf16[6,128,128]{2,1,0:T(8,128)(2,1)S(1)} %get-tuple-element.67), channel_id=1, source_target_pairs={{4,8},{8,4},{5,9},{9,5},{6,10},{10,6},{7,11},{11,7},{20,24},{24,20... | collective-permute-start | bytes 589832 | tf_op jit(solution)/shard_map/ppermute | solution.py:375
  17.8 0.7 %collective-permute-start.1 = (bf16[5,128,128]{2,1,0:T(8,128)(2,1)S(1)}, bf16[5,128,128]{2,1,0:T(8,128)(2,1)S(1)}, u32[]{:S(2)}, u32[]{:S(2)}) collective-permute-start(bf16[5,128,128]{2,1,0:T(8,128)(2,1)S(1)} %get-tuple-element.52), channel_id=1, source_target_pairs={{4,8},{8,4},{5,9},{9,5},{6,10},{10,6},{7,11},{11,7},{20,24},{24,20... | collective-permute-start | bytes 491528 | tf_op jit(solution)/shard_map/ppermute | solution.py:375
  18.6 0.7 %collective-permute-start.3 = (bf16[5,128,128]{2,1,0:T(8,128)(2,1)S(1)}, bf16[5,128,128]{2,1,0:T(8,128)(2,1)S(1)}, u32[]{:S(2)}, u32[]{:S(2)}) collective-permute-start(bf16[5,128,128]{2,1,0:T(8,128)(2,1)S(1)} %get-tuple-element.58), channel_id=1, source_target_pairs={{4,8},{8,4},{5,9},{9,5},{6,10},{10,6},{7,11},{11,7},{20,24},{24,20... | collective-permute-start | bytes 491528 | tf_op jit(solution)/shard_map/ppermute | solution.py:375
  19.3 1.3 %collective-permute-start.7 = (bf16[6,128,128]{2,1,0:T(8,128)(2,1)S(1)}, bf16[6,128,128]{2,1,0:T(8,128)(2,1)S(1)}, u32[]{:S(2)}, u32[]{:S(2)}) collective-permute-start(bf16[6,128,128]{2,1,0:T(8,128)(2,1)S(1)} %get-tuple-element.68), channel_id=1, source_target_pairs={{8,12},{4,0},{9,13},{5,1},{10,14},{6,2},{11,15},{7,3},{24,28},{20,... | collective-permute-start | bytes 589832 | tf_op jit(solution)/shard_map/ppermute | solution.py:375
  20.6 1.5 %collective-permute-start.8 = (bf16[5,128,128]{2,1,0:T(8,128)(2,1)S(1)}, bf16[5,128,128]{2,1,0:T(8,128)(2,1)S(1)}, u32[]{:S(2)}, u32[]{:S(2)}) collective-permute-start(bf16[5,128,128]{2,1,0:T(8,128)(2,1)S(1)} %get-tuple-element.69), channel_id=1, source_target_pairs={{8,12},{4,0},{9,13},{5,1},{10,14},{6,2},{11,15},{7,3},{24,28},{20,... | collective-permute-start | bytes 491528 | tf_op jit(solution)/shard_map/ppermute | solution.py:375
  22.1 1.7 %shard_map.90 = (f32[16,352,128]{2,1,0:T(8,128)S(1)}, f32[16,352,128]{2,1,0:T(8,128)S(1)}, f32[16,352,128]{2,1,0:T(8,128)S(1)}, f32[8,128]{1,0:T(8,128)S(1)}) custom-call(f32[16,352,128]{2,1,0:T(8,128)S(1)} %get-tuple-element.39.col, f32[16,1,384]{2,1,0:T(1,128)S(1)} %get-tuple-element.43.row, ...), custom_call_target="tpu_custom_call", output_to_operand_aliasing={{0}: (6, {}), {1}: (7, {}), {2}: (8, {})} | custom-call | flops 230686720 | bytes 1048576 | tf_op jit(solution)/shard_map/pallas_call | solution.py:309
  23.8 1.3 %collective-permute-start.4 = (bf16[5,128,128]{2,1,0:T(8,128)(2,1)S(1)}, bf16[5,128,128]{2,1,0:T(8,128)(2,1)S(1)}, u32[]{:S(2)}, u32[]{:S(2)}) collective-permute-start(bf16[5,128,128]{2,1,0:T(8,128)(2,1)S(1)} %get-tuple-element.64), channel_id=1, source_target_pairs={{8,12},{4,0},{9,13},{5,1},{10,14},{6,2},{11,15},{7,3},{24,28},{20,... | collective-permute-start | bytes 491528 | tf_op jit(solution)/shard_map/ppermute | solution.py:375
  25.1 3.5 %shard_map.93 = (f32[16,352,128]{2,1,0:T(8,128)S(1)}, f32[16,352,128]{2,1,0:T(8,128)S(1)}, f32[16,352,128]{2,1,0:T(8,128)S(1)}, f32[8,128]{1,0:T(8,128)}) custom-call(f32[16,352,128]{2,1,0:T(8,128)S(1)} %get-tuple-element.39.col, f32[16,1,384]{2,1,0:T(1,128)S(1)} %get-tuple-element.43.row, ...), custom_call_target="tpu_custom_call", output_to_operand_aliasing={{0}: (6, {}), {1}: (7, {}), {2}: (8, {})} | custom-call | flops 403701760 | bytes 1048576 | tf_op jit(solution)/shard_map/pallas_call | solution.py:309
  28.6 2.3 %shard_map.99 = (bf16[352,16,128]{2,1,0:T(8,128)(2,1)}, bf16[352,16,128]{2,1,0:T(8,128)(2,1)}, bf16[352,16,128]{2,1,0:T(8,128)(2,1)}) custom-call(f32[16,352,128]{2,1,0:T(8,128)S(1)} %get-tuple-element.39.col, bf16[16,352,128]{2,1,0:T(8,128)(2,1)S(1)} %get-tuple-element.40.kh, bf16[16,352,128]{2,1,0:T(8,128)(2,1)S(1)} %get-tuple-element.41.vh, ...), custom_call_target="tpu_custom_call" | custom-call | flops 553648128 | bytes 1048576 | tf_op jit(solution)/shard_map/pallas_call | solution.py:309
  30.9 1.2 %collective-permute-done.7.got = bf16[6,128,128]{2,1,0:T(8,128)(2,1)S(1)} collective-permute-done((bf16[6,128,128]{2,1,0:T(8,128)(2,1)S(1)}, bf16[6,128,128]{2,1,0:T(8,128)(2,1)S(1)}, u32[]{:S(2)}, u32[]{:S(2)}) %collective-permute-start.7) | collective-permute-done | bytes 196640 | tf_op jit(solution)/shard_map/ppermute | solution.py:375
  32.1 0.6 %shard_map.97.rest_0_ = bf16[2,6,352,128]{3,2,1,0:T(8,128)(2,1)S(1)} custom-call(f32[16,352,128]{2,1,0:T(8,128)S(1)} %get-tuple-element.39.col, bf16[16,352,128]{2,1,0:T(8,128)(2,1)S(1)} %get-tuple-element.40.kh, bf16[16,352,128]{2,1,0:T(8,128)(2,1)S(1)} %get-tuple-element.41.vh, bf16[16,352,128]{2,1,0:T(8,128)(2,1)S(1)} %get-tuple-element.42.gh, ...), custom_call_target="tpu_custom_call" | custom-call | flops 138412032 | bytes 1048576 | tf_op jit(solution)/shard_map/pallas_call | solution.py:309
  32.8 2.9 %collective-permute-done.8.got = bf16[5,128,128]{2,1,0:T(8,128)(2,1)S(1)} collective-permute-done((bf16[5,128,128]{2,1,0:T(8,128)(2,1)S(1)}, bf16[5,128,128]{2,1,0:T(8,128)(2,1)S(1)}, u32[]{:S(2)}, u32[]{:S(2)}) %collective-permute-start.8) | collective-permute-done | bytes 163872 | tf_op jit(solution)/shard_map/ppermute | solution.py:375
  35.7 0.5 %shard_map.98.rest_1_ = bf16[2,5,352,128]{3,2,1,0:T(8,128)(2,1)S(1)} custom-call(f32[16,352,128]{2,1,0:T(8,128)S(1)} %get-tuple-element.39.col, bf16[16,352,128]{2,1,0:T(8,128)(2,1)S(1)} %get-tuple-element.40.kh, bf16[16,352,128]{2,1,0:T(8,128)(2,1)S(1)} %get-tuple-element.41.vh, bf16[16,352,128]{2,1,0:T(8,128)(2,1)S(1)} %get-tuple-element.42.gh, ...), custom_call_target="tpu_custom_call" | custom-call | flops 115343360 | bytes 1048576 | tf_op jit(solution)/shard_map/pallas_call | solution.py:309
  36.2 1.3 %collective-permute-done.4.got = bf16[5,128,128]{2,1,0:T(8,128)(2,1)S(1)} collective-permute-done((bf16[5,128,128]{2,1,0:T(8,128)(2,1)S(1)}, bf16[5,128,128]{2,1,0:T(8,128)(2,1)S(1)}, u32[]{:S(2)}, u32[]{:S(2)}) %collective-permute-start.4) | collective-permute-done | bytes 163872 | tf_op jit(solution)/shard_map/ppermute | solution.py:375
  37.5 2.5 %shard_map.100 = (bf16[352,16,128]{2,1,0:T(8,128)(2,1)}, bf16[352,16,128]{2,1,0:T(8,128)(2,1)}, bf16[352,16,128]{2,1,0:T(8,128)(2,1)}) custom-call(f32[16,352,128]{2,1,0:T(8,128)S(1)} %get-tuple-element.39.col, bf16[16,352,128]{2,1,0:T(8,128)(2,1)S(1)} %get-tuple-element.40.kh, ...), custom_call_target="tpu_custom_call", output_to_operand_aliasing={{0}: (10, {}), {1}: (11, {}), {2}: (12, {})} | custom-call | flops 115343360 | bytes 1048576 | tf_op jit(solution)/shard_map/pallas_call | solution.py:309
  (22 shorter events, 0.2 us)
Async XLA Ops:
  0.6 5.3 %copy-start = (bf16[352,16,128]{2,1,0:T(8,128)(2,1)S(1)}, bf16[352,16,128]{2,1,0:T(8,128)(2,1)}, u32[]{:S(2)}) copy-start(bf16[352,16,128]{2,1,0:T(8,128)(2,1)} %q.5) | copy-start | bytes 4325380
  0.6 5.3 %copy-start.4 = (f32[352,16]{0,1:T(8,128)S(1)}, f32[352,16]{0,1:T(8,128)}, u32[]{:S(2)}) copy-start(f32[352,16]{0,1:T(8,128)} %param.11) | copy-start | bytes 67588
  0.7 5.3 %copy-start.5 = (s32[16]{0:T(128)S(1)}, s32[16]{0:T(128)}, u32[]{:S(2)}) copy-start(s32[16]{0:T(128)} %param.10) | copy-start | bytes 196
  3.3 8.3 %copy-start.1 = (bf16[352,16,128]{2,1,0:T(8,128)(2,1)S(1)}, bf16[352,16,128]{2,1,0:T(8,128)(2,1)}, u32[]{:S(2)}) copy-start(bf16[352,16,128]{2,1,0:T(8,128)(2,1)} %k.5) | copy-start | bytes 4325380
  3.3 8.3 %copy-start.2 = (bf16[352,16,128]{2,1,0:T(8,128)(2,1)S(1)}, bf16[352,16,128]{2,1,0:T(8,128)(2,1)}, u32[]{:S(2)}) copy-start(bf16[352,16,128]{2,1,0:T(8,128)(2,1)} %v.5) | copy-start | bytes 4325380
  3.3 8.3 %copy-start.3 = (bf16[352,16,128]{2,1,0:T(8,128)(2,1)S(1)}, bf16[352,16,128]{2,1,0:T(8,128)(2,1)}, u32[]{:S(2)}) copy-start(bf16[352,16,128]{2,1,0:T(8,128)(2,1)} %g.5) | copy-start | bytes 4325380
  3.3 13.7 %collective-permute-start.5 = (bf16[6,128,128]{2,1,0:T(8,128)(2,1)S(1)}, bf16[6,128,128]{2,1,0:T(8,128)(2,1)S(1)}, u32[]{:S(2)}, u32[]{:S(2)}) collective-permute-start(bf16[6,128,128]{2,1,0:T(8,128)(2,1)S(1)} %get-tuple-element.65), channel_id=1, source_target_pairs={{0,4},{12,8},{1,5},{13,9},{2,6},{14,10},{3,7},{15,11},{16,20},{28,... | collective-permute-start | bytes 589832 | tf_op jit(solution)/shard_map/ppermute | solution.py:375
  9.0 8.8 %collective-permute-start = (bf16[5,128,128]{2,1,0:T(8,128)(2,1)S(1)}, bf16[5,128,128]{2,1,0:T(8,128)(2,1)S(1)}, u32[]{:S(2)}, u32[]{:S(2)}) collective-permute-start(bf16[5,128,128]{2,1,0:T(8,128)(2,1)S(1)} %get-tuple-element.48), channel_id=1, source_target_pairs={{0,4},{12,8},{1,5},{13,9},{2,6},{14,10},{3,7},{15,11},{16,20},{28,... | collective-permute-start | bytes 491528 | tf_op jit(solution)/shard_map/ppermute | solution.py:375
  10.3 8.3 %collective-permute-start.2 = (bf16[5,128,128]{2,1,0:T(8,128)(2,1)S(1)}, bf16[5,128,128]{2,1,0:T(8,128)(2,1)S(1)}, u32[]{:S(2)}, u32[]{:S(2)}) collective-permute-start(bf16[5,128,128]{2,1,0:T(8,128)(2,1)S(1)} %get-tuple-element.57), channel_id=1, source_target_pairs={{0,4},{12,8},{1,5},{13,9},{2,6},{14,10},{3,7},{15,11},{16,20},{28,... | collective-permute-start | bytes 491528 | tf_op jit(solution)/shard_map/ppermute | solution.py:375
  17.1 2.1 %collective-permute-start.6 = (bf16[6,128,128]{2,1,0:T(8,128)(2,1)S(1)}, bf16[6,128,128]{2,1,0:T(8,128)(2,1)S(1)}, u32[]{:S(2)}, u32[]{:S(2)}) collective-permute-start(bf16[6,128,128]{2,1,0:T(8,128)(2,1)S(1)} %get-tuple-element.67), channel_id=1, source_target_pairs={{4,8},{8,4},{5,9},{9,5},{6,10},{10,6},{7,11},{11,7},{20,24},{24,20... | collective-permute-start | bytes 589832 | tf_op jit(solution)/shard_map/ppermute | solution.py:375
  17.8 2.7 %collective-permute-start.1 = (bf16[5,128,128]{2,1,0:T(8,128)(2,1)S(1)}, bf16[5,128,128]{2,1,0:T(8,128)(2,1)S(1)}, u32[]{:S(2)}, u32[]{:S(2)}) collective-permute-start(bf16[5,128,128]{2,1,0:T(8,128)(2,1)S(1)} %get-tuple-element.52), channel_id=1, source_target_pairs={{4,8},{8,4},{5,9},{9,5},{6,10},{10,6},{7,11},{11,7},{20,24},{24,20... | collective-permute-start | bytes 491528 | tf_op jit(solution)/shard_map/ppermute | solution.py:375
  18.6 5.2 %collective-permute-start.3 = (bf16[5,128,128]{2,1,0:T(8,128)(2,1)S(1)}, bf16[5,128,128]{2,1,0:T(8,128)(2,1)S(1)}, u32[]{:S(2)}, u32[]{:S(2)}) collective-permute-start(bf16[5,128,128]{2,1,0:T(8,128)(2,1)S(1)} %get-tuple-element.58), channel_id=1, source_target_pairs={{4,8},{8,4},{5,9},{9,5},{6,10},{10,6},{7,11},{11,7},{20,24},{24,20... | collective-permute-start | bytes 491528 | tf_op jit(solution)/shard_map/ppermute | solution.py:375
  19.3 12.9 %collective-permute-start.7 = (bf16[6,128,128]{2,1,0:T(8,128)(2,1)S(1)}, bf16[6,128,128]{2,1,0:T(8,128)(2,1)S(1)}, u32[]{:S(2)}, u32[]{:S(2)}) collective-permute-start(bf16[6,128,128]{2,1,0:T(8,128)(2,1)S(1)} %get-tuple-element.68), channel_id=1, source_target_pairs={{8,12},{4,0},{9,13},{5,1},{10,14},{6,2},{11,15},{7,3},{24,28},{20,... | collective-permute-start | bytes 589832 | tf_op jit(solution)/shard_map/ppermute | solution.py:375
  20.6 15.0 %collective-permute-start.8 = (bf16[5,128,128]{2,1,0:T(8,128)(2,1)S(1)}, bf16[5,128,128]{2,1,0:T(8,128)(2,1)S(1)}, u32[]{:S(2)}, u32[]{:S(2)}) collective-permute-start(bf16[5,128,128]{2,1,0:T(8,128)(2,1)S(1)} %get-tuple-element.69), channel_id=1, source_target_pairs={{8,12},{4,0},{9,13},{5,1},{10,14},{6,2},{11,15},{7,3},{24,28},{20,... | collective-permute-start | bytes 491528 | tf_op jit(solution)/shard_map/ppermute | solution.py:375
  23.8 13.7 %collective-permute-start.4 = (bf16[5,128,128]{2,1,0:T(8,128)(2,1)S(1)}, bf16[5,128,128]{2,1,0:T(8,128)(2,1)S(1)}, u32[]{:S(2)}, u32[]{:S(2)}) collective-permute-start(bf16[5,128,128]{2,1,0:T(8,128)(2,1)S(1)} %get-tuple-element.64), channel_id=1, source_target_pairs={{8,12},{4,0},{9,13},{5,1},{10,14},{6,2},{11,15},{7,3},{24,28},{20,... | collective-permute-start | bytes 491528 | tf_op jit(solution)/shard_map/ppermute | solution.py:375

commit v4 on v3

--- a/solution.py
+++ b/solution.py
@@ -41,7 +41,7 @@
 
 
 def state_sum(left, right, fade):
-    return dot((left.T.astype(F32) * fade).astype(BF16), right).astype(BF16)
+    return dot((left.T.astype(F32) * fade).astype(BF16), right)
 
 
 def enter_of(within, h, length):
@@ -57,28 +57,41 @@
     place = lax.axis_index("seq")
     length = spikes.shape[1]
 
+    middle = length * 3 // 4 // 128 * 128
+    cuts = [slice(0, middle), slice(middle, length)] if middle else [slice(0, length)]
+    low = heads[0][0] // 8 * 8
+    high = min(-(-(heads[-1][-1] + 1) // 8) * 8, left.shape[1])
+    mine = [h for part in heads for h in part]
+
     def run(a, b, fade_of):
-        copies = [
-            pltpu.make_async_copy(source, target, sems.at[i])
-            for i, (source, target) in enumerate(
-                ((spikes, spikes_v), (decay, decay_v), (a, left), (b, right))
-            )
+        small = [
+            pltpu.make_async_copy(spikes, spikes_v, sems.at[0]),
+            pltpu.make_async_copy(decay, decay_v, sems.at[1]),
         ]
-        for copy in copies:
+        pairs = [
+            [
+                pltpu.make_async_copy(a.at[cut], left.at[cut], sems.at[2 + 2 * i]),
+                pltpu.make_async_copy(b.at[cut], right.at[cut], sems.at[3 + 2 * i]),
+            ]
+            for i, cut in enumerate(cuts)
+        ]
+        for copy in sum(pairs, small):
             copy.start()
-        for copy in copies[:2]:
+        for copy in small:
             copy.wait()
         within = running_forget(decay_v, spikes_v)
-        fades = {h: fade_of(within, h, length) for part in heads for h in part}
-        for copy in copies[2:]:
-            copy.wait()
-        low = heads[0][0] // 8 * 8
-        high = min(-(-(heads[-1][-1] + 1) // 8) * 8, left.shape[1])
-        a_h = jnp.swapaxes(left[:, low:high, :], 0, 1)
-        b_h = jnp.swapaxes(right[:, low:high, :], 0, 1)
+        fades = {h: fade_of(within, h, length) for h in mine}
+        sums = {h: 0.0 for h in mine}
+        for cut, pair in zip(cuts, pairs):
+            for copy in pair:
+                copy.wait()
+            a_h = jnp.swapaxes(left[cut, low:high, :], 0, 1)
+            b_h = jnp.swapaxes(right[cut, low:high, :], 0, 1)
+            for h in mine:
+                sums[h] += state_sum(a_h[h - low], b_h[h - low], fades[h][:, cut])
         for part, payload in zip(heads, payloads):
             for i, h in enumerate(part):
-                payload[i] = state_sum(a_h[h - low], b_h[h - low], fades[h])
+                payload[i] = sums[h].astype(BF16)
 
     @pl.when(place == 0)
     def _():
@@ -104,8 +117,8 @@
     @pl.when((place > 0) & (place < count - 1))
     def _():
         for h in range(all_heads):
-            kv[h] = state_sum(kh[h], vh[h], leave_of(within, h, length))
-            grad[h] = state_sum(qh[h], gh[h], enter_of(within, h, length))
+            kv[h] = state_sum(kh[h], vh[h], leave_of(within, h, length)).astype(BF16)
+            grad[h] = state_sum(qh[h], gh[h], enter_of(within, h, length)).astype(BF16)
 
     columns = within.T
     for h in range(all_heads):
@@ -157,7 +170,7 @@
             vg[h, s0:s1, :] = sum(dot(gt[:, t0:t1], scores[t0, s0]) for t0, t1 in after).T
         return carry
 
-    lax.fori_loop(start, start + heads, one, 0, unroll=min(UNROLL, heads))
+    lax.fori_loop(start, start + heads, one, 0, unroll=min(2 * UNROLL, heads))
 
 
 def terms(col, kh, vh, gh, state, start, h):
@@ -246,33 +259,52 @@
         wait_out(tokens.at[2], outs[2], sems.at[2])
 
 
-def ends_kernel(count, start, col, kh, vh, gh, qg, kg, vg, got, *rest):
-    by_head = rest[-1]
+def some_heads(parts, starts, low, high, slot):
+    pieces = []
+    for part, start in zip(parts, starts):
+        first, last = max(low - start, 0), min(high - start, part.shape[1])
+        if first < last:
+            pieces.append(part[slot, first:last])
+    return jnp.concatenate(pieces, axis=0)
+
+
+def ends_kernel(count, starts, c, ready, col, kh, vh, gh, qg, kg, vg, got, *rest):
+    by_head, tokens = rest[-2:] if ready else (rest[-1], None)
+    parts = [*rest[:c], by_head]
     heads = got.shape[0]
     place = lax.axis_index("seq")
-    args = ((qg, kg, vg), col, kh, vh, gh, got, start, heads)
+    args = ((qg, kg, vg), col, kh, vh, gh, got, starts[c], heads)
+
+    def lay_out(slot):
+        if ready:
+            tokens[slot, :, :ready, :] = jnp.swapaxes(some_heads(parts, starts, 0, ready, slot), 0, 1)
 
     @pl.when(place == count - 1)
     def _():
         add_terms(0, by_head, 0, *args)
+        lay_out(0)
 
     @pl.when(place == 0)
     def _():
         add_terms(1, by_head, 0, *args)
         add_terms(2, by_head, 1, *args)
-
-
-def last_kernel(count, start, col, kh, vh, gh, qg, kg, vg, got, *rest):
-    *outs, by_head, tokens, sems = rest[-6:]
-    earlier = rest[:-9]
-    heads = got.shape[0]
-    place = lax.axis_index("seq")
-    args = ((qg, kg, vg), col, kh, vh, gh, got, start, heads)
+        lay_out(0)
+        lay_out(1)
+
+
+def last_kernel(count, starts, ready, col, kh, vh, gh, qg, kg, vg, got, *rest):
+    *outs, tokens, by_head, sems = rest[-6:]
+    parts = [*rest[: len(starts) - 1], by_head]
+    all_heads = kh.shape[0]
+    place = lax.axis_index("seq")
+    args = ((qg, kg, vg), col, kh, vh, gh, got, starts[-1], got.shape[0])
 
     def write(which, slot):
         add_terms(which, by_head, slot, *args)
-        whole = jnp.concatenate([part[slot] for part in earlier] + [by_head[slot]], axis=0)
-        send_out(whole, tokens.at[slot], outs[which], sems.at[slot])
+        whole = some_heads(parts, starts, ready, all_heads, slot)
+        for cut, copy in out_copies(tokens.at[slot], outs[which], sems.at[slot]):
+            tokens[slot, cut, ready:, :] = jnp.swapaxes(whole[:, cut, :], 0, 1)
+            copy.start()
 
     @pl.when(place == count - 1)
     def _():
@@ -334,7 +366,7 @@
                 pltpu.VMEM(spikes.shape, F32),
                 raw,
                 raw,
-                pltpu.SemaphoreType.DMA((4,)),
+                pltpu.SemaphoreType.DMA((6,)),
             ],
         )
         payloads += several
@@ -404,36 +436,39 @@
             pltpu.SemaphoreType.DMA((3, 2)),
         ],
     )
-    earlier = []
+    ready = starts[-1] // 8 * 8
+    laid = shape((2,) + full.shape, BF16)
+    earlier, tokens = [], ()
     for c in range(chunks - 1):
-        earlier.append(
-            call(
-                functools.partial(ends_kernel, count, starts[c]),
-                (*common, arrived[c][-1]),
-                shape((2, sizes[c], length, size), BF16),
-                8,
-                2 * sizes[c],
-                after=earlier[-1:],
-            )
+        lays = ready if c == chunks - 2 else 0
+        part, *tokens = call(
+            functools.partial(ends_kernel, count, starts, c, lays),
+            (*common, arrived[c][-1], *earlier),
+            (shape((2, sizes[c], length, size), BF16),) + ((laid,) if lays else ()),
+            16,
+            2 * sizes[c],
         )
-    ins = (*common, arrived[-1][-1], *earlier)
-    return tuple(
-        call(
-            functools.partial(last_kernel, count, starts[-1]),
-            (*ins, *outs),
-            (full,) * 3,
-            8,
-            2 * sizes[-1],
-            specs=[VMEM] * len(ins) + [ANY] * 3,
-            out_spec=ANY,
-            scratch_shapes=[
-                pltpu.VMEM((2, sizes[-1], length, size), BF16),
-                pltpu.VMEM((2,) + full.shape, BF16),
-                pltpu.SemaphoreType.DMA((2, 2)),
-            ],
-            input_output_aliases={len(ins) + j: j for j in range(3)},
-        )
-    )
+        earlier.append(part)
+    ins = (*common, arrived[-1][-1], *earlier, *tokens, *outs)
+    fixed = len(ins) - 3
+    aliases = {fixed + j: j for j in range(3)}
+    if tokens:
+        aliases[fixed - 1] = 3
+    vmem, any_space = [VMEM] * fixed, [ANY] * 3
+    *outs, _ = pl.pallas_call(
+        functools.partial(last_kernel, count, starts, ready),
+        out_shape=(full,) * 3 + (laid,),
+        in_specs=vmem + any_space,
+        out_specs=(ANY,) * 3 + (VMEM,),
+        scratch_shapes=[
+            pltpu.VMEM((2, sizes[-1], length, size), BF16),
+            pltpu.SemaphoreType.DMA((2, 2)),
+        ],
+        compiler_params=pltpu.CompilerParams(vmem_limit_bytes=8 * MIB),
+        cost_estimate=pl.CostEstimate(flops=2 * sizes[-1] * flops, bytes_accessed=1 << 20, transcendentals=0),
+        input_output_aliases=aliases,
+    )(*ins)
+    return tuple(outs)
 
 
 def solution(mesh):

time: 40.5 us -> 40.2 us (level)
  Pallas kernels: 22.3 us -> 21.2 us
  waiting for transfers between devices: 5.44 us -> 6.1 us
    pallas_call x16 -> x15, Pallas kernels: 22.3 us -> 19.1 us  [call(): pl.pallas_call(kernel, out_shape=outs, in_specs=(specs or [VMEM] * len(in...]
    pallas_call x0 -> x1, Pallas kernels: none -> 2.12 us  [per_device(): pl.pallas_call(functools.partial(last_kernel, count, starts, ready), out_...]
    ppermute x9, waiting for transfers between devices: 5.44 us -> 6.1 us  [per_device(): got = lax.ppermute(payloads[c], 'seq', pairs)]
  transfers between devices with their start and end apart: 9 -> 9, of which waited for: 3 -> 3; matrix products, arithmetic and copies ran while one was open for 0% -> 0% of each run, Pallas kernels for 43% -> 42%
where the time goes in v4:
time: 40.2 us; the launch traced here: 39.9 us
  Pallas kernels  21.2 us (53%)
  starting transfers between devices  11.4 us (28%)
  waiting for transfers between devices  6.1 us (15%)
  between operations  1.11 us (3%)
    pallas_call x15, Pallas kernels, call(): pl.pallas_call(kernel, out_shape=outs, in_specs=(specs or [VMEM] * len(in...  19.1 us
    ppermute x9, starting transfers between devices, per_device(): got = lax.ppermute(payloads[c], 'seq', pairs)  11.4 us
    ppermute x9, waiting for transfers between devices, per_device(): got = lax.ppermute(payloads[c], 'seq', pairs)  6.1 us
    pallas_call x1, Pallas kernels, per_device(): pl.pallas_call(functools.partial(last_kernel, count, starts, ready), out_...  2.12 us
  transfers between devices with their start and end apart: 9, of which 3 were waited for; matrix products, arithmetic and copies ran while one was open for 0% of the time, Pallas kernels for 42%

profile of v4, /device:TPU:0, one launch (start us, length us, event | category | flops | bytes accessed | tf_op | source)
XLA Modules:
  0.0 39.9 jit_solution(7204498951259419412)
XLA Ops:
  0.7 2.5 %shard_map.94 = (bf16[6,128,128]{2,1,0:T(8,128)(2,1)S(1)}, f32[8,128]{1,0:T(8,128)}) custom-call(s32[1,16]{1,0:T(1,128)} %bitcast.5, f32[16,352]{1,0:T(8,128)} %bitcast.2, bf16[352,16,128]{2,1,0:T(8,128)(2,1)} %q.5, bf16[352,16,128]{2,1,0:T(8,128)(2,1)} %k.5, bf16[352,16,128]{2,1,0:T(8,128)(2,1)} %v.5, bf16[352,16,128]{2,1,0:T(8,128)(2,1)} %g.5), custom_call_target="tpu_custom_call" | custom-call | flops 69206016 | bytes 1048576 | tf_op jit(solution)/shard_map/pallas_call | solution.py:341
  3.2 0.0 copy-start.1
  3.2 0.0 copy-start.2
  3.2 2.8 %collective-permute-start.5 = (bf16[6,128,128]{2,1,0:T(8,128)(2,1)S(1)}, bf16[6,128,128]{2,1,0:T(8,128)(2,1)S(1)}, u32[]{:S(2)}, u32[]{:S(2)}) collective-permute-start(bf16[6,128,128]{2,1,0:T(8,128)(2,1)S(1)} %get-tuple-element.70), channel_id=1, source_target_pairs={{0,4},{12,8},{1,5},{13,9},{2,6},{14,10},{3,7},{15,11},{16,20},{28,... | collective-permute-start | bytes 589832 | tf_op jit(solution)/shard_map/ppermute | solution.py:407
  6.0 2.8 %shard_map.85 = (bf16[5,128,128]{2,1,0:T(8,128)(2,1)S(1)}, bf16[5,128,128]{2,1,0:T(8,128)(2,1)S(1)}, f32[8,128]{1,0:T(8,128)S(1)}) custom-call(s32[1,16]{1,0:T(1,128)S(1)} %bitcast.6, f32[16,352]{1,0:T(8,128)S(1)} %bitcast.3, bf16[352,16,128]{2,1,0:T(8,128)(2,1)S(1)} %copy-done, bf16[352,16,128]{2,1,0:T(8,128)(2,1)} %k.5, bf16[352,16,128]{2,1,0:T(8,128)(2,1)} %v.5, ...), custom_call_target="tpu_custom_call" | custom-call | flops 115343360 | bytes 1048576 | tf_op jit(solution)/shard_map/pallas_call | solution.py:341
  8.8 1.3 %collective-permute-start = (bf16[5,128,128]{2,1,0:T(8,128)(2,1)S(1)}, bf16[5,128,128]{2,1,0:T(8,128)(2,1)S(1)}, u32[]{:S(2)}, u32[]{:S(2)}) collective-permute-start(bf16[5,128,128]{2,1,0:T(8,128)(2,1)S(1)} %get-tuple-element.53), channel_id=1, source_target_pairs={{0,4},{12,8},{1,5},{13,9},{2,6},{14,10},{3,7},{15,11},{16,20},{28,... | collective-permute-start | bytes 491528 | tf_op jit(solution)/shard_map/ppermute | solution.py:407
  10.1 1.3 %collective-permute-start.2 = (bf16[5,128,128]{2,1,0:T(8,128)(2,1)S(1)}, bf16[5,128,128]{2,1,0:T(8,128)(2,1)S(1)}, u32[]{:S(2)}, u32[]{:S(2)}) collective-permute-start(bf16[5,128,128]{2,1,0:T(8,128)(2,1)S(1)} %get-tuple-element.62), channel_id=1, source_target_pairs={{0,4},{12,8},{1,5},{13,9},{2,6},{14,10},{3,7},{15,11},{16,20},{28,... | collective-permute-start | bytes 491528 | tf_op jit(solution)/shard_map/ppermute | solution.py:407
  11.5 3.5 %shard_map.86 = (bf16[16,352,128]{2,1,0:T(8,128)(2,1)S(1)}, bf16[16,352,128]{2,1,0:T(8,128)(2,1)S(1)}, bf16[16,352,128]{2,1,0:T(8,128)(2,1)S(1)}, bf16[16,352,12...) custom-call(s32[1,16]{1,0:T(1,128)S(1)} %bitcast.7, ...), custom_call_target="tpu_custom_call" | custom-call | flops 369098752 | bytes 1048576 | tf_op jit(solution)/shard_map/pallas_call | solution.py:341
  14.9 2.0 %shard_map.87 = (f32[16,352,128]{2,1,0:T(8,128)S(1)}, f32[16,352,128]{2,1,0:T(8,128)S(1)}, f32[16,352,128]{2,1,0:T(8,128)S(1)}, f32[8,128]{1,0:T(8,128)S(1)}) custom-call(f32[16,352,128]{2,1,0:T(8,128)S(1)} %get-tuple-element.44.col, f32[16,1,384]{2,1,0:T(1,128)S(1)} %get-tuple-element.48.row, bf16[16,352,128]{2,1,0:T(8,128)(2,1)S(1)} %get-tuple-element.49.qh, ...), custom_call_target="tpu_custom_call" | custom-call | flops 288358400 | bytes 1048576 | tf_op jit(solution)/shard_map/pallas_call | solution.py:341
  17.0 0.7 %collective-permute-start.6 = (bf16[6,128,128]{2,1,0:T(8,128)(2,1)S(1)}, bf16[6,128,128]{2,1,0:T(8,128)(2,1)S(1)}, u32[]{:S(2)}, u32[]{:S(2)}) collective-permute-start(bf16[6,128,128]{2,1,0:T(8,128)(2,1)S(1)} %get-tuple-element.72), channel_id=1, source_target_pairs={{4,8},{8,4},{5,9},{9,5},{6,10},{10,6},{7,11},{11,7},{20,24},{24,20... | collective-permute-start | bytes 589832 | tf_op jit(solution)/shard_map/ppermute | solution.py:407
  17.7 0.7 %collective-permute-start.1 = (bf16[5,128,128]{2,1,0:T(8,128)(2,1)S(1)}, bf16[5,128,128]{2,1,0:T(8,128)(2,1)S(1)}, u32[]{:S(2)}, u32[]{:S(2)}) collective-permute-start(bf16[5,128,128]{2,1,0:T(8,128)(2,1)S(1)} %get-tuple-element.57), channel_id=1, source_target_pairs={{4,8},{8,4},{5,9},{9,5},{6,10},{10,6},{7,11},{11,7},{20,24},{24,20... | collective-permute-start | bytes 491528 | tf_op jit(solution)/shard_map/ppermute | solution.py:407
  18.4 0.7 %collective-permute-start.3 = (bf16[5,128,128]{2,1,0:T(8,128)(2,1)S(1)}, bf16[5,128,128]{2,1,0:T(8,128)(2,1)S(1)}, u32[]{:S(2)}, u32[]{:S(2)}) collective-permute-start(bf16[5,128,128]{2,1,0:T(8,128)(2,1)S(1)} %get-tuple-element.63), channel_id=1, source_target_pairs={{4,8},{8,4},{5,9},{9,5},{6,10},{10,6},{7,11},{11,7},{20,24},{24,20... | collective-permute-start | bytes 491528 | tf_op jit(solution)/shard_map/ppermute | solution.py:407
  19.2 1.3 %collective-permute-start.7 = (bf16[6,128,128]{2,1,0:T(8,128)(2,1)S(1)}, bf16[6,128,128]{2,1,0:T(8,128)(2,1)S(1)}, u32[]{:S(2)}, u32[]{:S(2)}) collective-permute-start(bf16[6,128,128]{2,1,0:T(8,128)(2,1)S(1)} %get-tuple-element.73), channel_id=1, source_target_pairs={{8,12},{4,0},{9,13},{5,1},{10,14},{6,2},{11,15},{7,3},{24,28},{20,... | collective-permute-start | bytes 589832 | tf_op jit(solution)/shard_map/ppermute | solution.py:407
  20.5 1.5 %collective-permute-start.8 = (bf16[5,128,128]{2,1,0:T(8,128)(2,1)S(1)}, bf16[5,128,128]{2,1,0:T(8,128)(2,1)S(1)}, u32[]{:S(2)}, u32[]{:S(2)}) collective-permute-start(bf16[5,128,128]{2,1,0:T(8,128)(2,1)S(1)} %get-tuple-element.74), channel_id=1, source_target_pairs={{8,12},{4,0},{9,13},{5,1},{10,14},{6,2},{11,15},{7,3},{24,28},{20,... | collective-permute-start | bytes 491528 | tf_op jit(solution)/shard_map/ppermute | solution.py:407
  22.0 1.7 %shard_map.90 = (f32[16,352,128]{2,1,0:T(8,128)S(1)}, f32[16,352,128]{2,1,0:T(8,128)S(1)}, f32[16,352,128]{2,1,0:T(8,128)S(1)}, f32[8,128]{1,0:T(8,128)S(1)}) custom-call(f32[16,352,128]{2,1,0:T(8,128)S(1)} %get-tuple-element.44.col, f32[16,1,384]{2,1,0:T(1,128)S(1)} %get-tuple-element.48.row, ...), custom_call_target="tpu_custom_call", output_to_operand_aliasing={{0}: (6, {}), {1}: (7, {}), {2}: (8, {})} | custom-call | flops 230686720 | bytes 1048576 | tf_op jit(solution)/shard_map/pallas_call | solution.py:341
  23.7 1.3 %collective-permute-start.4 = (bf16[5,128,128]{2,1,0:T(8,128)(2,1)S(1)}, bf16[5,128,128]{2,1,0:T(8,128)(2,1)S(1)}, u32[]{:S(2)}, u32[]{:S(2)}) collective-permute-start(bf16[5,128,128]{2,1,0:T(8,128)(2,1)S(1)} %get-tuple-element.69), channel_id=1, source_target_pairs={{8,12},{4,0},{9,13},{5,1},{10,14},{6,2},{11,15},{7,3},{24,28},{20,... | collective-permute-start | bytes 491528 | tf_op jit(solution)/shard_map/ppermute | solution.py:407
  25.0 2.7 %shard_map.93 = (f32[16,352,128]{2,1,0:T(8,128)S(1)}, f32[16,352,128]{2,1,0:T(8,128)S(1)}, f32[16,352,128]{2,1,0:T(8,128)S(1)}, f32[8,128]{1,0:T(8,128)}) custom-call(f32[16,352,128]{2,1,0:T(8,128)S(1)} %get-tuple-element.44.col, f32[16,1,384]{2,1,0:T(1,128)S(1)} %get-tuple-element.48.row, ...), custom_call_target="tpu_custom_call", output_to_operand_aliasing={{0}: (6, {}), {1}: (7, {}), {2}: (8, {})} | custom-call | flops 403701760 | bytes 1048576 | tf_op jit(solution)/shard_map/pallas_call | solution.py:341
  27.7 2.3 %shard_map.99 = (bf16[352,16,128]{2,1,0:T(8,128)(2,1)}, bf16[352,16,128]{2,1,0:T(8,128)(2,1)}, bf16[352,16,128]{2,1,0:T(8,128)(2,1)}) custom-call(f32[16,352,128]{2,1,0:T(8,128)S(1)} %get-tuple-element.44.col, bf16[16,352,128]{2,1,0:T(8,128)(2,1)S(1)} %get-tuple-element.45.kh, bf16[16,352,128]{2,1,0:T(8,128)(2,1)S(1)} %get-tuple-element.46.vh, ...), custom_call_target="tpu_custom_call" | custom-call | flops 553648128 | bytes 1048576 | tf_op jit(solution)/shard_map/pallas_call | solution.py:341
  29.9 2.1 %collective-permute-done.7.got = bf16[6,128,128]{2,1,0:T(8,128)(2,1)S(1)} collective-permute-done((bf16[6,128,128]{2,1,0:T(8,128)(2,1)S(1)}, bf16[6,128,128]{2,1,0:T(8,128)(2,1)S(1)}, u32[]{:S(2)}, u32[]{:S(2)}) %collective-permute-start.7) | collective-permute-done | bytes 196640 | tf_op jit(solution)/shard_map/ppermute | solution.py:407
  32.0 0.5 %shard_map.97.rest_0_ = bf16[2,6,352,128]{3,2,1,0:T(8,128)(2,1)S(1)} custom-call(f32[16,352,128]{2,1,0:T(8,128)S(1)} %get-tuple-element.44.col, bf16[16,352,128]{2,1,0:T(8,128)(2,1)S(1)} %get-tuple-element.45.kh, bf16[16,352,128]{2,1,0:T(8,128)(2,1)S(1)} %get-tuple-element.46.vh, bf16[16,352,128]{2,1,0:T(8,128)(2,1)S(1)} %get-tuple-element.47.gh, ...), custom_call_target="tpu_custom_call" | custom-call | flops 138412032 | bytes 1048576 | tf_op jit(solution)/shard_map/pallas_call | solution.py:341
  32.6 3.0 %collective-permute-done.8.got = bf16[5,128,128]{2,1,0:T(8,128)(2,1)S(1)} collective-permute-done((bf16[5,128,128]{2,1,0:T(8,128)(2,1)S(1)}, bf16[5,128,128]{2,1,0:T(8,128)(2,1)S(1)}, u32[]{:S(2)}, u32[]{:S(2)}) %collective-permute-start.8) | collective-permute-done | bytes 163872 | tf_op jit(solution)/shard_map/ppermute | solution.py:407
  35.5 1.0 %shard_map.98 = (bf16[2,5,352,128]{3,2,1,0:T(8,128)(2,1)S(1)}, bf16[2,352,16,128]{3,2,1,0:T(8,128)(2,1)S(1)}) custom-call(f32[16,352,128]{2,1,0:T(8,128)S(1)} %get-tuple-element.44.col, bf16[16,352,128]{2,1,0:T(8,128)(2,1)S(1)} %get-tuple-element.45.kh, bf16[16,352,128]{2,1,0:T(8,128)(2,1)S(1)} %get-tuple-element.46.vh, ...), custom_call_target="tpu_custom_call" | custom-call | flops 115343360 | bytes 1048576 | tf_op jit(solution)/shard_map/pallas_call | solution.py:341
  36.6 1.0 %collective-permute-done.4.got = bf16[5,128,128]{2,1,0:T(8,128)(2,1)S(1)} collective-permute-done((bf16[5,128,128]{2,1,0:T(8,128)(2,1)S(1)}, bf16[5,128,128]{2,1,0:T(8,128)(2,1)S(1)}, u32[]{:S(2)}, u32[]{:S(2)}) %collective-permute-start.4) | collective-permute-done | bytes 163872 | tf_op jit(solution)/shard_map/ppermute | solution.py:407
  37.6 2.1 %shard_map.100 = (bf16[352,16,128]{2,1,0:T(8,128)(2,1)}, bf16[352,16,128]{2,1,0:T(8,128)(2,1)}, bf16[352,16,128]{2,1,0:T(8,128)(2,1)}, bf16[2,352,16,128]{3,2,1,0:T(8,128)(2,1)S(1)}) custom-call(f32[16,352,128]{2,1,0:T(8,128)S(1)} %get-tuple-element.44.col, ...), custom_call_target="tpu_custom_call", output_to_operand_aliasing={{0}: (11, {}), {1}: (12, {}), {2}: (13, {}), {3}: (10, {})} | custom-call | flops 115343360 | bytes 1048576 | tf_op jit(solution)/shard_map/pallas_call | solution.py:458
  (22 shorter events, 0.2 us)
Async XLA Ops:
  0.6 5.4 %copy-start = (bf16[352,16,128]{2,1,0:T(8,128)(2,1)S(1)}, bf16[352,16,128]{2,1,0:T(8,128)(2,1)}, u32[]{:S(2)}) copy-start(bf16[352,16,128]{2,1,0:T(8,128)(2,1)} %q.5) | copy-start | bytes 4325380
  0.6 5.4 %copy-start.4 = (f32[352,16]{0,1:T(8,128)S(1)}, f32[352,16]{0,1:T(8,128)}, u32[]{:S(2)}) copy-start(f32[352,16]{0,1:T(8,128)} %param.11) | copy-start | bytes 67588
  0.7 5.4 %copy-start.5 = (s32[16]{0:T(128)S(1)}, s32[16]{0:T(128)}, u32[]{:S(2)}) copy-start(s32[16]{0:T(128)} %param.10) | copy-start | bytes 196
  3.2 8.3 %copy-start.1 = (bf16[352,16,128]{2,1,0:T(8,128)(2,1)S(1)}, bf16[352,16,128]{2,1,0:T(8,128)(2,1)}, u32[]{:S(2)}) copy-start(bf16[352,16,128]{2,1,0:T(8,128)(2,1)} %k.5) | copy-start | bytes 4325380
  3.2 8.3 %copy-start.2 = (bf16[352,16,128]{2,1,0:T(8,128)(2,1)S(1)}, bf16[352,16,128]{2,1,0:T(8,128)(2,1)}, u32[]{:S(2)}) copy-start(bf16[352,16,128]{2,1,0:T(8,128)(2,1)} %v.5) | copy-start | bytes 4325380
  3.2 8.3 %copy-start.3 = (bf16[352,16,128]{2,1,0:T(8,128)(2,1)S(1)}, bf16[352,16,128]{2,1,0:T(8,128)(2,1)}, u32[]{:S(2)}) copy-start(bf16[352,16,128]{2,1,0:T(8,128)(2,1)} %g.5) | copy-start | bytes 4325380
  3.2 13.7 %collective-permute-start.5 = (bf16[6,128,128]{2,1,0:T(8,128)(2,1)S(1)}, bf16[6,128,128]{2,1,0:T(8,128)(2,1)S(1)}, u32[]{:S(2)}, u32[]{:S(2)}) collective-permute-start(bf16[6,128,128]{2,1,0:T(8,128)(2,1)S(1)} %get-tuple-element.70), channel_id=1, source_target_pairs={{0,4},{12,8},{1,5},{13,9},{2,6},{14,10},{3,7},{15,11},{16,20},{28,... | collective-permute-start | bytes 589832 | tf_op jit(solution)/shard_map/ppermute | solution.py:407
  8.8 8.8 %collective-permute-start = (bf16[5,128,128]{2,1,0:T(8,128)(2,1)S(1)}, bf16[5,128,128]{2,1,0:T(8,128)(2,1)S(1)}, u32[]{:S(2)}, u32[]{:S(2)}) collective-permute-start(bf16[5,128,128]{2,1,0:T(8,128)(2,1)S(1)} %get-tuple-element.53), channel_id=1, source_target_pairs={{0,4},{12,8},{1,5},{13,9},{2,6},{14,10},{3,7},{15,11},{16,20},{28,... | collective-permute-start | bytes 491528 | tf_op jit(solution)/shard_map/ppermute | solution.py:407
  10.1 8.3 %collective-permute-start.2 = (bf16[5,128,128]{2,1,0:T(8,128)(2,1)S(1)}, bf16[5,128,128]{2,1,0:T(8,128)(2,1)S(1)}, u32[]{:S(2)}, u32[]{:S(2)}) collective-permute-start(bf16[5,128,128]{2,1,0:T(8,128)(2,1)S(1)} %get-tuple-element.62), channel_id=1, source_target_pairs={{0,4},{12,8},{1,5},{13,9},{2,6},{14,10},{3,7},{15,11},{16,20},{28,... | collective-permute-start | bytes 491528 | tf_op jit(solution)/shard_map/ppermute | solution.py:407
  17.0 2.1 %collective-permute-start.6 = (bf16[6,128,128]{2,1,0:T(8,128)(2,1)S(1)}, bf16[6,128,128]{2,1,0:T(8,128)(2,1)S(1)}, u32[]{:S(2)}, u32[]{:S(2)}) collective-permute-start(bf16[6,128,128]{2,1,0:T(8,128)(2,1)S(1)} %get-tuple-element.72), channel_id=1, source_target_pairs={{4,8},{8,4},{5,9},{9,5},{6,10},{10,6},{7,11},{11,7},{20,24},{24,20... | collective-permute-start | bytes 589832 | tf_op jit(solution)/shard_map/ppermute | solution.py:407
  17.7 2.7 %collective-permute-start.1 = (bf16[5,128,128]{2,1,0:T(8,128)(2,1)S(1)}, bf16[5,128,128]{2,1,0:T(8,128)(2,1)S(1)}, u32[]{:S(2)}, u32[]{:S(2)}) collective-permute-start(bf16[5,128,128]{2,1,0:T(8,128)(2,1)S(1)} %get-tuple-element.57), channel_id=1, source_target_pairs={{4,8},{8,4},{5,9},{9,5},{6,10},{10,6},{7,11},{11,7},{20,24},{24,20... | collective-permute-start | bytes 491528 | tf_op jit(solution)/shard_map/ppermute | solution.py:407
  18.4 5.2 %collective-permute-start.3 = (bf16[5,128,128]{2,1,0:T(8,128)(2,1)S(1)}, bf16[5,128,128]{2,1,0:T(8,128)(2,1)S(1)}, u32[]{:S(2)}, u32[]{:S(2)}) collective-permute-start(bf16[5,128,128]{2,1,0:T(8,128)(2,1)S(1)} %get-tuple-element.63), channel_id=1, source_target_pairs={{4,8},{8,4},{5,9},{9,5},{6,10},{10,6},{7,11},{11,7},{20,24},{24,20... | collective-permute-start | bytes 491528 | tf_op jit(solution)/shard_map/ppermute | solution.py:407
  19.2 12.9 %collective-permute-start.7 = (bf16[6,128,128]{2,1,0:T(8,128)(2,1)S(1)}, bf16[6,128,128]{2,1,0:T(8,128)(2,1)S(1)}, u32[]{:S(2)}, u32[]{:S(2)}) collective-permute-start(bf16[6,128,128]{2,1,0:T(8,128)(2,1)S(1)} %get-tuple-element.73), channel_id=1, source_target_pairs={{8,12},{4,0},{9,13},{5,1},{10,14},{6,2},{11,15},{7,3},{24,28},{20,... | collective-permute-start | bytes 589832 | tf_op jit(solution)/shard_map/ppermute | solution.py:407
  20.5 15.0 %collective-permute-start.8 = (bf16[5,128,128]{2,1,0:T(8,128)(2,1)S(1)}, bf16[5,128,128]{2,1,0:T(8,128)(2,1)S(1)}, u32[]{:S(2)}, u32[]{:S(2)}) collective-permute-start(bf16[5,128,128]{2,1,0:T(8,128)(2,1)S(1)} %get-tuple-element.74), channel_id=1, source_target_pairs={{8,12},{4,0},{9,13},{5,1},{10,14},{6,2},{11,15},{7,3},{24,28},{20,... | collective-permute-start | bytes 491528 | tf_op jit(solution)/shard_map/ppermute | solution.py:407
  23.7 13.9 %collective-permute-start.4 = (bf16[5,128,128]{2,1,0:T(8,128)(2,1)S(1)}, bf16[5,128,128]{2,1,0:T(8,128)(2,1)S(1)}, u32[]{:S(2)}, u32[]{:S(2)}) collective-permute-start(bf16[5,128,128]{2,1,0:T(8,128)(2,1)S(1)} %get-tuple-element.69), channel_id=1, source_target_pairs={{8,12},{4,0},{9,13},{5,1},{10,14},{6,2},{11,15},{7,3},{24,28},{20,... | collective-permute-start | bytes 491528 | tf_op jit(solution)/shard_map/ppermute | solution.py:407

commit v5 on v4

--- a/solution.py
+++ b/solution.py
@@ -15,7 +15,8 @@
 NN = (((1,), (0,)), ((), ()))
 UNROLL = 4
 CHUNKS = 3
-DUE = {(0, 0): 5, (2, 1): 9}
+FIRST_LIMIT, SUMS_LIMIT = 63, 49
+DUE = {(0, 0): 2, (2, 1): 6}
 MIB = 2**20
 TOKEN = jax.ShapeDtypeStruct((8, 128), F32)
 
@@ -103,26 +104,31 @@
 
 
 def sums_kernel(count, decay, spikes, q, k, v, g, *rest):
-    qh, kh, vh, gh, col, row, kv, grad, fade = rest[-9:]
+    qh, kh, vh, gh, col, row, kv, grad, fade = rest[-16:-7]
+    decay_v, spikes_v, *raws, sems = rest[-7:]
     all_heads, length = spikes.shape
     place = lax.axis_index("seq")
-    within = running_forget(decay, spikes)
+    moves = ((spikes, spikes_v), (decay, decay_v), *zip((k, v, q, g), raws))
+    copies = [pltpu.make_async_copy(source, target, sems.at[i]) for i, (source, target) in enumerate(moves)]
+    for copy in copies:
+        copy.start()
+    for copy in copies[:2]:
+        copy.wait()
+    within = running_forget(decay_v, spikes_v)
     row[...] = within[:, None, :]
     fade[...] = jnp.broadcast_to(jnp.exp(-within[:, length - 1 : length])[:, :, None], fade.shape)
-    kh[...] = jnp.swapaxes(k[...], 0, 1)
-    vh[...] = jnp.swapaxes(v[...], 0, 1)
-    qh[...] = jnp.swapaxes(q[...], 0, 1)
-    gh[...] = jnp.swapaxes(g[...], 0, 1)
+    columns = within.T
+    for h in range(all_heads):
+        col[h] = jnp.broadcast_to(columns[:length, h : h + 1], (length, 128))
+    for copy, raw, target in zip(copies[2:], raws, (kh, vh, qh, gh)):
+        copy.wait()
+        target[...] = jnp.swapaxes(raw[...], 0, 1)
 
     @pl.when((place > 0) & (place < count - 1))
     def _():
         for h in range(all_heads):
             kv[h] = state_sum(kh[h], vh[h], leave_of(within, h, length)).astype(BF16)
             grad[h] = state_sum(qh[h], gh[h], enter_of(within, h, length)).astype(BF16)
-
-    columns = within.T
-    for h in range(all_heads):
-        col[h] = jnp.broadcast_to(columns[:length, h : h + 1], (length, 128))
 
 
 def merge_kernel(count, hop, start, got, kv, grad, fade, *rest):
@@ -358,7 +364,7 @@
             functools.partial(first_kernel, count, ranges[part]),
             (decay, spikes, *tensors),
             (*(pltpu.VMEM((sizes[c], size, size), BF16) for c in range(chunks)[part]), TOKEN),
-            52 if payloads else 60,
+            FIRST_LIMIT,
             sum(sizes[part]),
             specs=[ANY] * 6,
             scratch_shapes=[
@@ -373,12 +379,24 @@
     qh, kh, vh, gh, col, row, kv, grad, fade = call(
         functools.partial(sums_kernel, count),
         (decay, spikes, *tensors),
-        (by_head,) * 4
-        + (by_head_f, shape((all_heads, 1, wide), F32), states, states)
-        + (shape((all_heads, 1, size), F32),),
-        8,
+        tuple(
+            pltpu.VMEM(o.shape, o.dtype)
+            for o in (*(by_head,) * 4, by_head_f, shape((all_heads, 1, wide), F32))
+            + (states, states, shape((all_heads, 1, size), F32))
+        ),
+        SUMS_LIMIT,
         2 * all_heads,
-        after=(token,),
+        after=payloads[-1:],
+        specs=[ANY] * 6,
+        scratch_shapes=[
+            pltpu.VMEM(decay.shape, jnp.int32),
+            pltpu.VMEM(spikes.shape, F32),
+            raw,
+            raw,
+            raw,
+            raw,
+            pltpu.SemaphoreType.DMA((6,)),
+        ],
     )
 
     intra, placed, done, merged = [], 0, (), ()

time: 40.2 us -> 39.5 us (0.983)
  waiting for transfers between devices: 6.1 us -> 4.14 us
  Pallas kernels: 21.2 us -> 22.8 us
    ppermute x9, waiting for transfers between devices: 6.1 us -> 4.14 us  [per_device(): got = lax.ppermute(payloads[c], 'seq', pairs)]
    pallas_call x15, Pallas kernels: 19.1 us -> 20.6 us  [call(): pl.pallas_call(kernel, out_shape=outs, in_specs=(specs or [VMEM] * len(in...]
  transfers between devices with their start and end apart: 9 -> 9, of which waited for: 3 -> 3; matrix products, arithmetic and copies ran while one was open for 0% -> 0% of each run, Pallas kernels for 42% -> 47%
where the time goes in v5:
time: 39.5 us; the launch traced here: 39.2 us
  Pallas kernels  22.8 us (58%)
  starting transfers between devices  11.3 us (29%)
  waiting for transfers between devices  4.14 us (10%)
  between operations  1.03 us (3%)
    pallas_call x15, Pallas kernels, call(): pl.pallas_call(kernel, out_shape=outs, in_specs=(specs or [VMEM] * len(in...  20.6 us
    ppermute x9, starting transfers between devices, per_device(): got = lax.ppermute(payloads[c], 'seq', pairs)  11.3 us
    ppermute x9, waiting for transfers between devices, per_device(): got = lax.ppermute(payloads[c], 'seq', pairs)  4.14 us
    pallas_call x1, Pallas kernels, per_device(): pl.pallas_call(functools.partial(last_kernel, count, starts, ready), out_...  2.12 us
  transfers between devices with their start and end apart: 9, of which 3 were waited for; matrix products, arithmetic and copies ran while one was open for 0% of the time, Pallas kernels for 47%

profile of v5, /device:TPU:0, one launch (start us, length us, event | category | flops | bytes accessed | tf_op | source)
XLA Modules:
  0.0 39.2 jit_solution(8114312389884481183)
XLA Ops:
  0.6 2.4 %shard_map.94 = (bf16[6,128,128]{2,1,0:T(8,128)(2,1)S(1)}, f32[8,128]{1,0:T(8,128)}) custom-call(s32[1,16]{1,0:T(1,128)} %bitcast.5, f32[16,352]{1,0:T(8,128)} %bitcast.2, bf16[352,16,128]{2,1,0:T(8,128)(2,1)} %q.5, bf16[352,16,128]{2,1,0:T(8,128)(2,1)} %k.5, bf16[352,16,128]{2,1,0:T(8,128)(2,1)} %v.5, bf16[352,16,128]{2,1,0:T(8,128)(2,1)} %g.5), custom_call_target="tpu_custom_call" | custom-call | flops 69206016 | bytes 1048576 | tf_op jit(solution)/shard_map/pallas_call | solution.py:347
  3.0 2.6 %collective-permute-start.5 = (bf16[6,128,128]{2,1,0:T(8,128)(2,1)S(1)}, bf16[6,128,128]{2,1,0:T(8,128)(2,1)S(1)}, u32[]{:S(2)}, u32[]{:S(2)}) collective-permute-start(bf16[6,128,128]{2,1,0:T(8,128)(2,1)S(1)} %get-tuple-element.68), channel_id=1, source_target_pairs={{0,4},{12,8},{1,5},{13,9},{2,6},{14,10},{3,7},{15,11},{16,20},{28,... | collective-permute-start | bytes 589832 | tf_op jit(solution)/shard_map/ppermute | solution.py:425
  5.7 2.8 %shard_map.85 = (bf16[5,128,128]{2,1,0:T(8,128)(2,1)S(1)}, bf16[5,128,128]{2,1,0:T(8,128)(2,1)S(1)}, f32[8,128]{1,0:T(8,128)}) custom-call(s32[1,16]{1,0:T(1,128)} %bitcast.6, f32[16,352]{1,0:T(8,128)} %bitcast.3, bf16[352,16,128]{2,1,0:T(8,128)(2,1)} %q.5, bf16[352,16,128]{2,1,0:T(8,128)(2,1)} %k.5, bf16[352,16,128]{2,1,0:T(8,128)(2,1)} %v.5, ...), custom_call_target="tpu_custom_call" | custom-call | flops 115343360 | bytes 1048576 | tf_op jit(solution)/shard_map/pallas_call | solution.py:347
  8.5 0.0 copy-start
  8.5 1.3 %collective-permute-start = (bf16[5,128,128]{2,1,0:T(8,128)(2,1)S(1)}, bf16[5,128,128]{2,1,0:T(8,128)(2,1)S(1)}, u32[]{:S(2)}, u32[]{:S(2)}) collective-permute-start(bf16[5,128,128]{2,1,0:T(8,128)(2,1)S(1)} %get-tuple-element.52), channel_id=1, source_target_pairs={{0,4},{12,8},{1,5},{13,9},{2,6},{14,10},{3,7},{15,11},{16,20},{28,... | collective-permute-start | bytes 491528 | tf_op jit(solution)/shard_map/ppermute | solution.py:425
  9.8 1.3 %collective-permute-start.2 = (bf16[5,128,128]{2,1,0:T(8,128)(2,1)S(1)}, bf16[5,128,128]{2,1,0:T(8,128)(2,1)S(1)}, u32[]{:S(2)}, u32[]{:S(2)}) collective-permute-start(bf16[5,128,128]{2,1,0:T(8,128)(2,1)S(1)} %get-tuple-element.42.rest_0_), channel_id=1, source_target_pairs={{0,4},{12,8},{1,5},{13,9},{2,6},{14,10},{3,7},{15,11},{16,20},{28,... | collective-permute-start | bytes 491528 | tf_op jit(solution)/shard_map/ppermute | solution.py:425
  11.1 4.6 %shard_map.86 = (bf16[16,352,128]{2,1,0:T(8,128)(2,1)S(1)}, bf16[16,352,128]{2,1,0:T(8,128)(2,1)S(1)}, bf16[16,352,128]{2,1,0:T(8,128)(2,1)S(1)}, bf16[16,352,12...) custom-call(s32[1,16]{1,0:T(1,128)} %bitcast.7, ...), custom_call_target="tpu_custom_call" | custom-call | flops 369098752 | bytes 1048576 | tf_op jit(solution)/shard_map/pallas_call | solution.py:347
  15.7 1.0 %shard_map.87 = (f32[16,352,128]{2,1,0:T(8,128)S(1)}, f32[16,352,128]{2,1,0:T(8,128)S(1)}, f32[16,352,128]{2,1,0:T(8,128)S(1)}, f32[8,128]{1,0:T(8,128)S(1)}) custom-call(f32[16,352,128]{2,1,0:T(8,128)S(1)} %get-tuple-element.43.col, f32[16,1,384]{2,1,0:T(1,128)S(1)} %get-tuple-element.47.row, bf16[16,352,128]{2,1,0:T(8,128)(2,1)S(1)} %get-tuple-element.48.qh, ...), custom_call_target="tpu_custom_call" | custom-call | flops 115343360 | bytes 1048576 | tf_op jit(solution)/shard_map/pallas_call | solution.py:347
  16.7 0.0 collective-permute-done.5.got.rest_0_
  16.7 0.7 %collective-permute-start.6 = (bf16[6,128,128]{2,1,0:T(8,128)(2,1)S(1)}, bf16[6,128,128]{2,1,0:T(8,128)(2,1)S(1)}, u32[]{:S(2)}, u32[]{:S(2)}) collective-permute-start(bf16[6,128,128]{2,1,0:T(8,128)(2,1)S(1)} %get-tuple-element.70), channel_id=1, source_target_pairs={{4,8},{8,4},{5,9},{9,5},{6,10},{10,6},{7,11},{11,7},{20,24},{24,20... | collective-permute-start | bytes 589832 | tf_op jit(solution)/shard_map/ppermute | solution.py:425
  17.4 0.7 %collective-permute-start.1 = (bf16[5,128,128]{2,1,0:T(8,128)(2,1)S(1)}, bf16[5,128,128]{2,1,0:T(8,128)(2,1)S(1)}, u32[]{:S(2)}, u32[]{:S(2)}) collective-permute-start(bf16[5,128,128]{2,1,0:T(8,128)(2,1)S(1)} %get-tuple-element.56), channel_id=1, source_target_pairs={{4,8},{8,4},{5,9},{9,5},{6,10},{10,6},{7,11},{11,7},{20,24},{24,20... | collective-permute-start | bytes 491528 | tf_op jit(solution)/shard_map/ppermute | solution.py:425
  18.1 0.7 %collective-permute-start.3 = (bf16[5,128,128]{2,1,0:T(8,128)(2,1)S(1)}, bf16[5,128,128]{2,1,0:T(8,128)(2,1)S(1)}, u32[]{:S(2)}, u32[]{:S(2)}) collective-permute-start(bf16[5,128,128]{2,1,0:T(8,128)(2,1)S(1)} %get-tuple-element.61), channel_id=1, source_target_pairs={{4,8},{8,4},{5,9},{9,5},{6,10},{10,6},{7,11},{11,7},{20,24},{24,20... | collective-permute-start | bytes 491528 | tf_op jit(solution)/shard_map/ppermute | solution.py:425
  18.9 1.3 %collective-permute-start.7 = (bf16[6,128,128]{2,1,0:T(8,128)(2,1)S(1)}, bf16[6,128,128]{2,1,0:T(8,128)(2,1)S(1)}, u32[]{:S(2)}, u32[]{:S(2)}) collective-permute-start(bf16[6,128,128]{2,1,0:T(8,128)(2,1)S(1)} %get-tuple-element.71), channel_id=1, source_target_pairs={{8,12},{4,0},{9,13},{5,1},{10,14},{6,2},{11,15},{7,3},{24,28},{20,... | collective-permute-start | bytes 589832 | tf_op jit(solution)/shard_map/ppermute | solution.py:425
  20.2 1.5 %collective-permute-start.8 = (bf16[5,128,128]{2,1,0:T(8,128)(2,1)S(1)}, bf16[5,128,128]{2,1,0:T(8,128)(2,1)S(1)}, u32[]{:S(2)}, u32[]{:S(2)}) collective-permute-start(bf16[5,128,128]{2,1,0:T(8,128)(2,1)S(1)} %get-tuple-element.72), channel_id=1, source_target_pairs={{8,12},{4,0},{9,13},{5,1},{10,14},{6,2},{11,15},{7,3},{24,28},{20,... | collective-permute-start | bytes 491528 | tf_op jit(solution)/shard_map/ppermute | solution.py:425
  21.7 1.7 %shard_map.90 = (f32[16,352,128]{2,1,0:T(8,128)S(1)}, f32[16,352,128]{2,1,0:T(8,128)S(1)}, f32[16,352,128]{2,1,0:T(8,128)S(1)}, f32[8,128]{1,0:T(8,128)S(1)}) custom-call(f32[16,352,128]{2,1,0:T(8,128)S(1)} %get-tuple-element.43.col, f32[16,1,384]{2,1,0:T(1,128)S(1)} %get-tuple-element.47.row, ...), custom_call_target="tpu_custom_call", output_to_operand_aliasing={{0}: (6, {}), {1}: (7, {}), {2}: (8, {})} | custom-call | flops 230686720 | bytes 1048576 | tf_op jit(solution)/shard_map/pallas_call | solution.py:347
  23.4 1.3 %collective-permute-start.4 = (bf16[5,128,128]{2,1,0:T(8,128)(2,1)S(1)}, bf16[5,128,128]{2,1,0:T(8,128)(2,1)S(1)}, u32[]{:S(2)}, u32[]{:S(2)}) collective-permute-start(bf16[5,128,128]{2,1,0:T(8,128)(2,1)S(1)} %get-tuple-element.67), channel_id=1, source_target_pairs={{8,12},{4,0},{9,13},{5,1},{10,14},{6,2},{11,15},{7,3},{24,28},{20,... | collective-permute-start | bytes 491528 | tf_op jit(solution)/shard_map/ppermute | solution.py:425
  24.7 4.3 %shard_map.93 = (f32[16,352,128]{2,1,0:T(8,128)S(1)}, f32[16,352,128]{2,1,0:T(8,128)S(1)}, f32[16,352,128]{2,1,0:T(8,128)S(1)}, f32[8,128]{1,0:T(8,128)}) custom-call(f32[16,352,128]{2,1,0:T(8,128)S(1)} %get-tuple-element.43.col, f32[16,1,384]{2,1,0:T(1,128)S(1)} %get-tuple-element.47.row, ...), custom_call_target="tpu_custom_call", output_to_operand_aliasing={{0}: (6, {}), {1}: (7, {}), {2}: (8, {})} | custom-call | flops 576716800 | bytes 1048576 | tf_op jit(solution)/shard_map/pallas_call | solution.py:347
  29.0 2.3 %shard_map.99 = (bf16[352,16,128]{2,1,0:T(8,128)(2,1)}, bf16[352,16,128]{2,1,0:T(8,128)(2,1)}, bf16[352,16,128]{2,1,0:T(8,128)(2,1)}) custom-call(f32[16,352,128]{2,1,0:T(8,128)S(1)} %get-tuple-element.43.col, bf16[16,352,128]{2,1,0:T(8,128)(2,1)S(1)} %get-tuple-element.44.kh, bf16[16,352,128]{2,1,0:T(8,128)(2,1)S(1)} %get-tuple-element.45.vh, ...), custom_call_target="tpu_custom_call" | custom-call | flops 553648128 | bytes 1048576 | tf_op jit(solution)/shard_map/pallas_call | solution.py:347
  31.2 0.4 collective-permute-done.7.got
  31.6 0.5 %shard_map.97.rest_0_ = bf16[2,6,352,128]{3,2,1,0:T(8,128)(2,1)S(1)} custom-call(f32[16,352,128]{2,1,0:T(8,128)S(1)} %get-tuple-element.43.col, bf16[16,352,128]{2,1,0:T(8,128)(2,1)S(1)} %get-tuple-element.44.kh, bf16[16,352,128]{2,1,0:T(8,128)(2,1)S(1)} %get-tuple-element.45.vh, bf16[16,352,128]{2,1,0:T(8,128)(2,1)S(1)} %get-tuple-element.46.gh, ...), custom_call_target="tpu_custom_call" | custom-call | flops 138412032 | bytes 1048576 | tf_op jit(solution)/shard_map/pallas_call | solution.py:347
  32.1 3.0 %collective-permute-done.8.got = bf16[5,128,128]{2,1,0:T(8,128)(2,1)S(1)} collective-permute-done((bf16[5,128,128]{2,1,0:T(8,128)(2,1)S(1)}, bf16[5,128,128]{2,1,0:T(8,128)(2,1)S(1)}, u32[]{:S(2)}, u32[]{:S(2)}) %collective-permute-start.8) | collective-permute-done | bytes 163872 | tf_op jit(solution)/shard_map/ppermute | solution.py:425
  35.1 1.0 %shard_map.98 = (bf16[2,5,352,128]{3,2,1,0:T(8,128)(2,1)S(1)}, bf16[2,352,16,128]{3,2,1,0:T(8,128)(2,1)S(1)}) custom-call(f32[16,352,128]{2,1,0:T(8,128)S(1)} %get-tuple-element.43.col, bf16[16,352,128]{2,1,0:T(8,128)(2,1)S(1)} %get-tuple-element.44.kh, bf16[16,352,128]{2,1,0:T(8,128)(2,1)S(1)} %get-tuple-element.45.vh, ...), custom_call_target="tpu_custom_call" | custom-call | flops 115343360 | bytes 1048576 | tf_op jit(solution)/shard_map/pallas_call | solution.py:347
  36.1 0.8 %collective-permute-done.4.got = bf16[5,128,128]{2,1,0:T(8,128)(2,1)S(1)} collective-permute-done((bf16[5,128,128]{2,1,0:T(8,128)(2,1)S(1)}, bf16[5,128,128]{2,1,0:T(8,128)(2,1)S(1)}, u32[]{:S(2)}, u32[]{:S(2)}) %collective-permute-start.4) | collective-permute-done | bytes 163872 | tf_op jit(solution)/shard_map/ppermute | solution.py:425
  36.9 2.1 %shard_map.100 = (bf16[352,16,128]{2,1,0:T(8,128)(2,1)}, bf16[352,16,128]{2,1,0:T(8,128)(2,1)}, bf16[352,16,128]{2,1,0:T(8,128)(2,1)}, bf16[2,352,16,128]{3,2,1,0:T(8,128)(2,1)S(1)}) custom-call(f32[16,352,128]{2,1,0:T(8,128)S(1)} %get-tuple-element.43.col, ...), custom_call_target="tpu_custom_call", output_to_operand_aliasing={{0}: (11, {}), {1}: (12, {}), {2}: (13, {}), {3}: (10, {})} | custom-call | flops 115343360 | bytes 1048576 | tf_op jit(solution)/shard_map/pallas_call | solution.py:476
  (12 shorter events, 0.1 us)
Async XLA Ops:
  3.0 13.6 %collective-permute-start.5 = (bf16[6,128,128]{2,1,0:T(8,128)(2,1)S(1)}, bf16[6,128,128]{2,1,0:T(8,128)(2,1)S(1)}, u32[]{:S(2)}, u32[]{:S(2)}) collective-permute-start(bf16[6,128,128]{2,1,0:T(8,128)(2,1)S(1)} %get-tuple-element.68), channel_id=1, source_target_pairs={{0,4},{12,8},{1,5},{13,9},{2,6},{14,10},{3,7},{15,11},{16,20},{28,... | collective-permute-start | bytes 589832 | tf_op jit(solution)/shard_map/ppermute | solution.py:425
  8.5 2.6 %copy-start = (bf16[5,128,128]{2,1,0:T(8,128)(2,1)}, bf16[5,128,128]{2,1,0:T(8,128)(2,1)S(1)}, u32[]{:S(2)}) copy-start(bf16[5,128,128]{2,1,0:T(8,128)(2,1)S(1)} %get-tuple-element.42.rest_0_) | copy-start | bytes 491524
  8.5 8.9 %collective-permute-start = (bf16[5,128,128]{2,1,0:T(8,128)(2,1)S(1)}, bf16[5,128,128]{2,1,0:T(8,128)(2,1)S(1)}, u32[]{:S(2)}, u32[]{:S(2)}) collective-permute-start(bf16[5,128,128]{2,1,0:T(8,128)(2,1)S(1)} %get-tuple-element.52), channel_id=1, source_target_pairs={{0,4},{12,8},{1,5},{13,9},{2,6},{14,10},{3,7},{15,11},{16,20},{28,... | collective-permute-start | bytes 491528 | tf_op jit(solution)/shard_map/ppermute | solution.py:425
  9.8 8.3 %collective-permute-start.2 = (bf16[5,128,128]{2,1,0:T(8,128)(2,1)S(1)}, bf16[5,128,128]{2,1,0:T(8,128)(2,1)S(1)}, u32[]{:S(2)}, u32[]{:S(2)}) collective-permute-start(bf16[5,128,128]{2,1,0:T(8,128)(2,1)S(1)} %get-tuple-element.42.rest_0_), channel_id=1, source_target_pairs={{0,4},{12,8},{1,5},{13,9},{2,6},{14,10},{3,7},{15,11},{16,20},{28,... | collective-permute-start | bytes 491528 | tf_op jit(solution)/shard_map/ppermute | solution.py:425
  16.7 2.1 %collective-permute-start.6 = (bf16[6,128,128]{2,1,0:T(8,128)(2,1)S(1)}, bf16[6,128,128]{2,1,0:T(8,128)(2,1)S(1)}, u32[]{:S(2)}, u32[]{:S(2)}) collective-permute-start(bf16[6,128,128]{2,1,0:T(8,128)(2,1)S(1)} %get-tuple-element.70), channel_id=1, source_target_pairs={{4,8},{8,4},{5,9},{9,5},{6,10},{10,6},{7,11},{11,7},{20,24},{24,20... | collective-permute-start | bytes 589832 | tf_op jit(solution)/shard_map/ppermute | solution.py:425
  17.4 2.7 %collective-permute-start.1 = (bf16[5,128,128]{2,1,0:T(8,128)(2,1)S(1)}, bf16[5,128,128]{2,1,0:T(8,128)(2,1)S(1)}, u32[]{:S(2)}, u32[]{:S(2)}) collective-permute-start(bf16[5,128,128]{2,1,0:T(8,128)(2,1)S(1)} %get-tuple-element.56), channel_id=1, source_target_pairs={{4,8},{8,4},{5,9},{9,5},{6,10},{10,6},{7,11},{11,7},{20,24},{24,20... | collective-permute-start | bytes 491528 | tf_op jit(solution)/shard_map/ppermute | solution.py:425
  18.1 5.2 %collective-permute-start.3 = (bf16[5,128,128]{2,1,0:T(8,128)(2,1)S(1)}, bf16[5,128,128]{2,1,0:T(8,128)(2,1)S(1)}, u32[]{:S(2)}, u32[]{:S(2)}) collective-permute-start(bf16[5,128,128]{2,1,0:T(8,128)(2,1)S(1)} %get-tuple-element.61), channel_id=1, source_target_pairs={{4,8},{8,4},{5,9},{9,5},{6,10},{10,6},{7,11},{11,7},{20,24},{24,20... | collective-permute-start | bytes 491528 | tf_op jit(solution)/shard_map/ppermute | solution.py:425
  18.9 12.7 %collective-permute-start.7 = (bf16[6,128,128]{2,1,0:T(8,128)(2,1)S(1)}, bf16[6,128,128]{2,1,0:T(8,128)(2,1)S(1)}, u32[]{:S(2)}, u32[]{:S(2)}) collective-permute-start(bf16[6,128,128]{2,1,0:T(8,128)(2,1)S(1)} %get-tuple-element.71), channel_id=1, source_target_pairs={{8,12},{4,0},{9,13},{5,1},{10,14},{6,2},{11,15},{7,3},{24,28},{20,... | collective-permute-start | bytes 589832 | tf_op jit(solution)/shard_map/ppermute | solution.py:425
  20.2 14.9 %collective-permute-start.8 = (bf16[5,128,128]{2,1,0:T(8,128)(2,1)S(1)}, bf16[5,128,128]{2,1,0:T(8,128)(2,1)S(1)}, u32[]{:S(2)}, u32[]{:S(2)}) collective-permute-start(bf16[5,128,128]{2,1,0:T(8,128)(2,1)S(1)} %get-tuple-element.72), channel_id=1, source_target_pairs={{8,12},{4,0},{9,13},{5,1},{10,14},{6,2},{11,15},{7,3},{24,28},{20,... | collective-permute-start | bytes 491528 | tf_op jit(solution)/shard_map/ppermute | solution.py:425
  23.4 13.6 %collective-permute-start.4 = (bf16[5,128,128]{2,1,0:T(8,128)(2,1)S(1)}, bf16[5,128,128]{2,1,0:T(8,128)(2,1)S(1)}, u32[]{:S(2)}, u32[]{:S(2)}) collective-permute-start(bf16[5,128,128]{2,1,0:T(8,128)(2,1)S(1)} %get-tuple-element.67), channel_id=1, source_target_pairs={{8,12},{4,0},{9,13},{5,1},{10,14},{6,2},{11,15},{7,3},{24,28},{20,... | collective-permute-start | bytes 491528 | tf_op jit(solution)/shard_map/ppermute | solution.py:425

commit v6 on v5

--- a/solution.py
+++ b/solution.py
@@ -16,7 +16,7 @@
 UNROLL = 4
 CHUNKS = 3
 FIRST_LIMIT, SUMS_LIMIT = 63, 49
-DUE = {(0, 0): 2, (2, 1): 6}
+DUE = {(0, 0): 1, (2, 1): 6}
 MIB = 2**20
 TOKEN = jax.ShapeDtypeStruct((8, 128), F32)
 
@@ -176,7 +176,7 @@
             vg[h, s0:s1, :] = sum(dot(gt[:, t0:t1], scores[t0, s0]) for t0, t1 in after).T
         return carry
 
-    lax.fori_loop(start, start + heads, one, 0, unroll=min(2 * UNROLL, heads))
+    lax.fori_loop(start, start + heads, one, 0, unroll=max(n for n in range(1, 2 * UNROLL + 1) if heads % n == 0))
 
 
 def terms(col, kh, vh, gh, state, start, h):

time: 39.5 us -> 39.5 us (level)
  transfers between devices with their start and end apart: 9 -> 9, of which waited for: 3 -> 3; matrix products, arithmetic and copies ran while one was open for 0% -> 0% of each run, Pallas kernels for 47% -> 46%
where the time goes in v6:
time: 39.5 us; the launch traced here: 39.2 us
  Pallas kernels  22.5 us (57%)
  starting transfers between devices  11.3 us (29%)
  waiting for transfers between devices  4.43 us (11%)
  between operations  1.04 us (3%)
    pallas_call x15, Pallas kernels, call(): pl.pallas_call(kernel, out_shape=outs, in_specs=(specs or [VMEM] * len(in...  20.3 us
    ppermute x9, starting transfers between devices, per_device(): got = lax.ppermute(payloads[c], 'seq', pairs)  11.3 us
    ppermute x9, waiting for transfers between devices, per_device(): got = lax.ppermute(payloads[c], 'seq', pairs)  4.43 us
    pallas_call x1, Pallas kernels, per_device(): pl.pallas_call(functools.partial(last_kernel, count, starts, ready), out_...  2.12 us
  transfers between devices with their start and end apart: 9, of which 3 were waited for; matrix products, arithmetic and copies ran while one was open for 0% of the time, Pallas kernels for 46%

profile of v6, /device:TPU:0, one launch (start us, length us, event | category | flops | bytes accessed | tf_op | source)
XLA Modules:
  0.0 39.2 jit_solution(16601534314195075497)
XLA Ops:
  0.6 2.4 %shard_map.94 = (bf16[6,128,128]{2,1,0:T(8,128)(2,1)S(1)}, f32[8,128]{1,0:T(8,128)}) custom-call(s32[1,16]{1,0:T(1,128)} %bitcast.5, f32[16,352]{1,0:T(8,128)} %bitcast.2, bf16[352,16,128]{2,1,0:T(8,128)(2,1)} %q.5, bf16[352,16,128]{2,1,0:T(8,128)(2,1)} %k.5, bf16[352,16,128]{2,1,0:T(8,128)(2,1)} %v.5, bf16[352,16,128]{2,1,0:T(8,128)(2,1)} %g.5), custom_call_target="tpu_custom_call" | custom-call | flops 69206016 | bytes 1048576 | tf_op jit(solution)/shard_map/pallas_call | solution.py:347
  3.0 2.6 %collective-permute-start.5 = (bf16[6,128,128]{2,1,0:T(8,128)(2,1)S(1)}, bf16[6,128,128]{2,1,0:T(8,128)(2,1)S(1)}, u32[]{:S(2)}, u32[]{:S(2)}) collective-permute-start(bf16[6,128,128]{2,1,0:T(8,128)(2,1)S(1)} %get-tuple-element.68), channel_id=1, source_target_pairs={{0,4},{12,8},{1,5},{13,9},{2,6},{14,10},{3,7},{15,11},{16,20},{28,... | collective-permute-start | bytes 589832 | tf_op jit(solution)/shard_map/ppermute | solution.py:425
  5.7 2.8 %shard_map.85 = (bf16[5,128,128]{2,1,0:T(8,128)(2,1)S(1)}, bf16[5,128,128]{2,1,0:T(8,128)(2,1)S(1)}, f32[8,128]{1,0:T(8,128)}) custom-call(s32[1,16]{1,0:T(1,128)} %bitcast.6, f32[16,352]{1,0:T(8,128)} %bitcast.3, bf16[352,16,128]{2,1,0:T(8,128)(2,1)} %q.5, bf16[352,16,128]{2,1,0:T(8,128)(2,1)} %k.5, bf16[352,16,128]{2,1,0:T(8,128)(2,1)} %v.5, ...), custom_call_target="tpu_custom_call" | custom-call | flops 115343360 | bytes 1048576 | tf_op jit(solution)/shard_map/pallas_call | solution.py:347
  8.5 0.0 copy-start
  8.5 1.3 %collective-permute-start = (bf16[5,128,128]{2,1,0:T(8,128)(2,1)S(1)}, bf16[5,128,128]{2,1,0:T(8,128)(2,1)S(1)}, u32[]{:S(2)}, u32[]{:S(2)}) collective-permute-start(bf16[5,128,128]{2,1,0:T(8,128)(2,1)S(1)} %get-tuple-element.52), channel_id=1, source_target_pairs={{0,4},{12,8},{1,5},{13,9},{2,6},{14,10},{3,7},{15,11},{16,20},{28,... | collective-permute-start | bytes 491528 | tf_op jit(solution)/shard_map/ppermute | solution.py:425
  9.8 1.3 %collective-permute-start.2 = (bf16[5,128,128]{2,1,0:T(8,128)(2,1)S(1)}, bf16[5,128,128]{2,1,0:T(8,128)(2,1)S(1)}, u32[]{:S(2)}, u32[]{:S(2)}) collective-permute-start(bf16[5,128,128]{2,1,0:T(8,128)(2,1)S(1)} %get-tuple-element.42.rest_0_), channel_id=1, source_target_pairs={{0,4},{12,8},{1,5},{13,9},{2,6},{14,10},{3,7},{15,11},{16,20},{28,... | collective-permute-start | bytes 491528 | tf_op jit(solution)/shard_map/ppermute | solution.py:425
  11.1 4.6 %shard_map.86 = (bf16[16,352,128]{2,1,0:T(8,128)(2,1)S(1)}, bf16[16,352,128]{2,1,0:T(8,128)(2,1)S(1)}, bf16[16,352,128]{2,1,0:T(8,128)(2,1)S(1)}, bf16[16,352,12...) custom-call(s32[1,16]{1,0:T(1,128)} %bitcast.7, ...), custom_call_target="tpu_custom_call" | custom-call | flops 369098752 | bytes 1048576 | tf_op jit(solution)/shard_map/pallas_call | solution.py:347
  15.7 0.6 %shard_map.87 = (f32[16,352,128]{2,1,0:T(8,128)S(1)}, f32[16,352,128]{2,1,0:T(8,128)S(1)}, f32[16,352,128]{2,1,0:T(8,128)S(1)}, f32[8,128]{1,0:T(8,128)S(1)}) custom-call(f32[16,352,128]{2,1,0:T(8,128)S(1)} %get-tuple-element.43.col, f32[16,1,384]{2,1,0:T(1,128)S(1)} %get-tuple-element.47.row, bf16[16,352,128]{2,1,0:T(8,128)(2,1)S(1)} %get-tuple-element.48.qh, ...), custom_call_target="tpu_custom_call" | custom-call | flops 57671680 | bytes 1048576 | tf_op jit(solution)/shard_map/pallas_call | solution.py:347
  16.3 0.0 collective-permute-done.5.got.rest_0_
  16.3 0.7 %collective-permute-start.6 = (bf16[6,128,128]{2,1,0:T(8,128)(2,1)S(1)}, bf16[6,128,128]{2,1,0:T(8,128)(2,1)S(1)}, u32[]{:S(2)}, u32[]{:S(2)}) collective-permute-start(bf16[6,128,128]{2,1,0:T(8,128)(2,1)S(1)} %get-tuple-element.70), channel_id=1, source_target_pairs={{4,8},{8,4},{5,9},{9,5},{6,10},{10,6},{7,11},{11,7},{20,24},{24,20... | collective-permute-start | bytes 589832 | tf_op jit(solution)/shard_map/ppermute | solution.py:425
  17.1 0.7 %collective-permute-start.1 = (bf16[5,128,128]{2,1,0:T(8,128)(2,1)S(1)}, bf16[5,128,128]{2,1,0:T(8,128)(2,1)S(1)}, u32[]{:S(2)}, u32[]{:S(2)}) collective-permute-start(bf16[5,128,128]{2,1,0:T(8,128)(2,1)S(1)} %get-tuple-element.56), channel_id=1, source_target_pairs={{4,8},{8,4},{5,9},{9,5},{6,10},{10,6},{7,11},{11,7},{20,24},{24,20... | collective-permute-start | bytes 491528 | tf_op jit(solution)/shard_map/ppermute | solution.py:425
  17.8 0.7 %collective-permute-start.3 = (bf16[5,128,128]{2,1,0:T(8,128)(2,1)S(1)}, bf16[5,128,128]{2,1,0:T(8,128)(2,1)S(1)}, u32[]{:S(2)}, u32[]{:S(2)}) collective-permute-start(bf16[5,128,128]{2,1,0:T(8,128)(2,1)S(1)} %get-tuple-element.61), channel_id=1, source_target_pairs={{4,8},{8,4},{5,9},{9,5},{6,10},{10,6},{7,11},{11,7},{20,24},{24,20... | collective-permute-start | bytes 491528 | tf_op jit(solution)/shard_map/ppermute | solution.py:425
  18.5 1.3 %collective-permute-start.7 = (bf16[6,128,128]{2,1,0:T(8,128)(2,1)S(1)}, bf16[6,128,128]{2,1,0:T(8,128)(2,1)S(1)}, u32[]{:S(2)}, u32[]{:S(2)}) collective-permute-start(bf16[6,128,128]{2,1,0:T(8,128)(2,1)S(1)} %get-tuple-element.71), channel_id=1, source_target_pairs={{8,12},{4,0},{9,13},{5,1},{10,14},{6,2},{11,15},{7,3},{24,28},{20,... | collective-permute-start | bytes 589832 | tf_op jit(solution)/shard_map/ppermute | solution.py:425
  19.8 1.5 %collective-permute-start.8 = (bf16[5,128,128]{2,1,0:T(8,128)(2,1)S(1)}, bf16[5,128,128]{2,1,0:T(8,128)(2,1)S(1)}, u32[]{:S(2)}, u32[]{:S(2)}) collective-permute-start(bf16[5,128,128]{2,1,0:T(8,128)(2,1)S(1)} %get-tuple-element.72), channel_id=1, source_target_pairs={{8,12},{4,0},{9,13},{5,1},{10,14},{6,2},{11,15},{7,3},{24,28},{20,... | collective-permute-start | bytes 491528 | tf_op jit(solution)/shard_map/ppermute | solution.py:425
  21.3 2.0 %shard_map.90 = (f32[16,352,128]{2,1,0:T(8,128)S(1)}, f32[16,352,128]{2,1,0:T(8,128)S(1)}, f32[16,352,128]{2,1,0:T(8,128)S(1)}, f32[8,128]{1,0:T(8,128)S(1)}) custom-call(f32[16,352,128]{2,1,0:T(8,128)S(1)} %get-tuple-element.43.col, f32[16,1,384]{2,1,0:T(1,128)S(1)} %get-tuple-element.47.row, ...), custom_call_target="tpu_custom_call", output_to_operand_aliasing={{0}: (6, {}), {1}: (7, {}), {2}: (8, {})} | custom-call | flops 288358400 | bytes 1048576 | tf_op jit(solution)/shard_map/pallas_call | solution.py:347
  23.4 1.3 %collective-permute-start.4 = (bf16[5,128,128]{2,1,0:T(8,128)(2,1)S(1)}, bf16[5,128,128]{2,1,0:T(8,128)(2,1)S(1)}, u32[]{:S(2)}, u32[]{:S(2)}) collective-permute-start(bf16[5,128,128]{2,1,0:T(8,128)(2,1)S(1)} %get-tuple-element.67), channel_id=1, source_target_pairs={{8,12},{4,0},{9,13},{5,1},{10,14},{6,2},{11,15},{7,3},{24,28},{20,... | collective-permute-start | bytes 491528 | tf_op jit(solution)/shard_map/ppermute | solution.py:425
  24.7 4.0 %shard_map.93 = (f32[16,352,128]{2,1,0:T(8,128)S(1)}, f32[16,352,128]{2,1,0:T(8,128)S(1)}, f32[16,352,128]{2,1,0:T(8,128)S(1)}, f32[8,128]{1,0:T(8,128)}) custom-call(f32[16,352,128]{2,1,0:T(8,128)S(1)} %get-tuple-element.43.col, f32[16,1,384]{2,1,0:T(1,128)S(1)} %get-tuple-element.47.row, ...), custom_call_target="tpu_custom_call", output_to_operand_aliasing={{0}: (6, {}), {1}: (7, {}), {2}: (8, {})} | custom-call | flops 576716800 | bytes 1048576 | tf_op jit(solution)/shard_map/pallas_call | solution.py:347
  28.7 2.3 %shard_map.99 = (bf16[352,16,128]{2,1,0:T(8,128)(2,1)}, bf16[352,16,128]{2,1,0:T(8,128)(2,1)}, bf16[352,16,128]{2,1,0:T(8,128)(2,1)}) custom-call(f32[16,352,128]{2,1,0:T(8,128)S(1)} %get-tuple-element.43.col, bf16[16,352,128]{2,1,0:T(8,128)(2,1)S(1)} %get-tuple-element.44.kh, bf16[16,352,128]{2,1,0:T(8,128)(2,1)S(1)} %get-tuple-element.45.vh, ...), custom_call_target="tpu_custom_call" | custom-call | flops 553648128 | bytes 1048576 | tf_op jit(solution)/shard_map/pallas_call | solution.py:347
  31.0 0.6 %collective-permute-done.7.got = bf16[6,128,128]{2,1,0:T(8,128)(2,1)S(1)} collective-permute-done((bf16[6,128,128]{2,1,0:T(8,128)(2,1)S(1)}, bf16[6,128,128]{2,1,0:T(8,128)(2,1)S(1)}, u32[]{:S(2)}, u32[]{:S(2)}) %collective-permute-start.7) | collective-permute-done | bytes 196640 | tf_op jit(solution)/shard_map/ppermute | solution.py:425
  31.6 0.5 %shard_map.97.rest_0_ = bf16[2,6,352,128]{3,2,1,0:T(8,128)(2,1)S(1)} custom-call(f32[16,352,128]{2,1,0:T(8,128)S(1)} %get-tuple-element.43.col, bf16[16,352,128]{2,1,0:T(8,128)(2,1)S(1)} %get-tuple-element.44.kh, bf16[16,352,128]{2,1,0:T(8,128)(2,1)S(1)} %get-tuple-element.45.vh, bf16[16,352,128]{2,1,0:T(8,128)(2,1)S(1)} %get-tuple-element.46.gh, ...), custom_call_target="tpu_custom_call" | custom-call | flops 138412032 | bytes 1048576 | tf_op jit(solution)/shard_map/pallas_call | solution.py:347
  32.1 3.0 %collective-permute-done.8.got = bf16[5,128,128]{2,1,0:T(8,128)(2,1)S(1)} collective-permute-done((bf16[5,128,128]{2,1,0:T(8,128)(2,1)S(1)}, bf16[5,128,128]{2,1,0:T(8,128)(2,1)S(1)}, u32[]{:S(2)}, u32[]{:S(2)}) %collective-permute-start.8) | collective-permute-done | bytes 163872 | tf_op jit(solution)/shard_map/ppermute | solution.py:425
  35.1 1.0 %shard_map.98 = (bf16[2,5,352,128]{3,2,1,0:T(8,128)(2,1)S(1)}, bf16[2,352,16,128]{3,2,1,0:T(8,128)(2,1)S(1)}) custom-call(f32[16,352,128]{2,1,0:T(8,128)S(1)} %get-tuple-element.43.col, bf16[16,352,128]{2,1,0:T(8,128)(2,1)S(1)} %get-tuple-element.44.kh, bf16[16,352,128]{2,1,0:T(8,128)(2,1)S(1)} %get-tuple-element.45.vh, ...), custom_call_target="tpu_custom_call" | custom-call | flops 115343360 | bytes 1048576 | tf_op jit(solution)/shard_map/pallas_call | solution.py:347
  36.1 0.8 %collective-permute-done.4.got = bf16[5,128,128]{2,1,0:T(8,128)(2,1)S(1)} collective-permute-done((bf16[5,128,128]{2,1,0:T(8,128)(2,1)S(1)}, bf16[5,128,128]{2,1,0:T(8,128)(2,1)S(1)}, u32[]{:S(2)}, u32[]{:S(2)}) %collective-permute-start.4) | collective-permute-done | bytes 163872 | tf_op jit(solution)/shard_map/ppermute | solution.py:425
  36.9 2.1 %shard_map.100 = (bf16[352,16,128]{2,1,0:T(8,128)(2,1)}, bf16[352,16,128]{2,1,0:T(8,128)(2,1)}, bf16[352,16,128]{2,1,0:T(8,128)(2,1)}, bf16[2,352,16,128]{3,2,1,0:T(8,128)(2,1)S(1)}) custom-call(f32[16,352,128]{2,1,0:T(8,128)S(1)} %get-tuple-element.43.col, ...), custom_call_target="tpu_custom_call", output_to_operand_aliasing={{0}: (11, {}), {1}: (12, {}), {2}: (13, {}), {3}: (10, {})} | custom-call | flops 115343360 | bytes 1048576 | tf_op jit(solution)/shard_map/pallas_call | solution.py:476
  (12 shorter events, 0.1 us)
Async XLA Ops:
  3.0 13.3 %collective-permute-start.5 = (bf16[6,128,128]{2,1,0:T(8,128)(2,1)S(1)}, bf16[6,128,128]{2,1,0:T(8,128)(2,1)S(1)}, u32[]{:S(2)}, u32[]{:S(2)}) collective-permute-start(bf16[6,128,128]{2,1,0:T(8,128)(2,1)S(1)} %get-tuple-element.68), channel_id=1, source_target_pairs={{0,4},{12,8},{1,5},{13,9},{2,6},{14,10},{3,7},{15,11},{16,20},{28,... | collective-permute-start | bytes 589832 | tf_op jit(solution)/shard_map/ppermute | solution.py:425
  8.5 2.6 %copy-start = (bf16[5,128,128]{2,1,0:T(8,128)(2,1)}, bf16[5,128,128]{2,1,0:T(8,128)(2,1)S(1)}, u32[]{:S(2)}) copy-start(bf16[5,128,128]{2,1,0:T(8,128)(2,1)S(1)} %get-tuple-element.42.rest_0_) | copy-start | bytes 491524
  8.5 8.5 %collective-permute-start = (bf16[5,128,128]{2,1,0:T(8,128)(2,1)S(1)}, bf16[5,128,128]{2,1,0:T(8,128)(2,1)S(1)}, u32[]{:S(2)}, u32[]{:S(2)}) collective-permute-start(bf16[5,128,128]{2,1,0:T(8,128)(2,1)S(1)} %get-tuple-element.52), channel_id=1, source_target_pairs={{0,4},{12,8},{1,5},{13,9},{2,6},{14,10},{3,7},{15,11},{16,20},{28,... | collective-permute-start | bytes 491528 | tf_op jit(solution)/shard_map/ppermute | solution.py:425
  9.8 7.9 %collective-permute-start.2 = (bf16[5,128,128]{2,1,0:T(8,128)(2,1)S(1)}, bf16[5,128,128]{2,1,0:T(8,128)(2,1)S(1)}, u32[]{:S(2)}, u32[]{:S(2)}) collective-permute-start(bf16[5,128,128]{2,1,0:T(8,128)(2,1)S(1)} %get-tuple-element.42.rest_0_), channel_id=1, source_target_pairs={{0,4},{12,8},{1,5},{13,9},{2,6},{14,10},{3,7},{15,11},{16,20},{28,... | collective-permute-start | bytes 491528 | tf_op jit(solution)/shard_map/ppermute | solution.py:425
  16.3 2.1 %collective-permute-start.6 = (bf16[6,128,128]{2,1,0:T(8,128)(2,1)S(1)}, bf16[6,128,128]{2,1,0:T(8,128)(2,1)S(1)}, u32[]{:S(2)}, u32[]{:S(2)}) collective-permute-start(bf16[6,128,128]{2,1,0:T(8,128)(2,1)S(1)} %get-tuple-element.70), channel_id=1, source_target_pairs={{4,8},{8,4},{5,9},{9,5},{6,10},{10,6},{7,11},{11,7},{20,24},{24,20... | collective-permute-start | bytes 589832 | tf_op jit(solution)/shard_map/ppermute | solution.py:425
  17.1 2.7 %collective-permute-start.1 = (bf16[5,128,128]{2,1,0:T(8,128)(2,1)S(1)}, bf16[5,128,128]{2,1,0:T(8,128)(2,1)S(1)}, u32[]{:S(2)}, u32[]{:S(2)}) collective-permute-start(bf16[5,128,128]{2,1,0:T(8,128)(2,1)S(1)} %get-tuple-element.56), channel_id=1, source_target_pairs={{4,8},{8,4},{5,9},{9,5},{6,10},{10,6},{7,11},{11,7},{20,24},{24,20... | collective-permute-start | bytes 491528 | tf_op jit(solution)/shard_map/ppermute | solution.py:425
  17.8 5.5 %collective-permute-start.3 = (bf16[5,128,128]{2,1,0:T(8,128)(2,1)S(1)}, bf16[5,128,128]{2,1,0:T(8,128)(2,1)S(1)}, u32[]{:S(2)}, u32[]{:S(2)}) collective-permute-start(bf16[5,128,128]{2,1,0:T(8,128)(2,1)S(1)} %get-tuple-element.61), channel_id=1, source_target_pairs={{4,8},{8,4},{5,9},{9,5},{6,10},{10,6},{7,11},{11,7},{20,24},{24,20... | collective-permute-start | bytes 491528 | tf_op jit(solution)/shard_map/ppermute | solution.py:425
  18.5 13.1 %collective-permute-start.7 = (bf16[6,128,128]{2,1,0:T(8,128)(2,1)S(1)}, bf16[6,128,128]{2,1,0:T(8,128)(2,1)S(1)}, u32[]{:S(2)}, u32[]{:S(2)}) collective-permute-start(bf16[6,128,128]{2,1,0:T(8,128)(2,1)S(1)} %get-tuple-element.71), channel_id=1, source_target_pairs={{8,12},{4,0},{9,13},{5,1},{10,14},{6,2},{11,15},{7,3},{24,28},{20,... | collective-permute-start | bytes 589832 | tf_op jit(solution)/shard_map/ppermute | solution.py:425
  19.8 15.3 %collective-permute-start.8 = (bf16[5,128,128]{2,1,0:T(8,128)(2,1)S(1)}, bf16[5,128,128]{2,1,0:T(8,128)(2,1)S(1)}, u32[]{:S(2)}, u32[]{:S(2)}) collective-permute-start(bf16[5,128,128]{2,1,0:T(8,128)(2,1)S(1)} %get-tuple-element.72), channel_id=1, source_target_pairs={{8,12},{4,0},{9,13},{5,1},{10,14},{6,2},{11,15},{7,3},{24,28},{20,... | collective-permute-start | bytes 491528 | tf_op jit(solution)/shard_map/ppermute | solution.py:425
  23.4 13.6 %collective-permute-start.4 = (bf16[5,128,128]{2,1,0:T(8,128)(2,1)S(1)}, bf16[5,128,128]{2,1,0:T(8,128)(2,1)S(1)}, u32[]{:S(2)}, u32[]{:S(2)}) collective-permute-start(bf16[5,128,128]{2,1,0:T(8,128)(2,1)S(1)} %get-tuple-element.67), channel_id=1, source_target_pairs={{8,12},{4,0},{9,13},{5,1},{10,14},{6,2},{11,15},{7,3},{24,28},{20,... | collective-permute-start | bytes 491528 | tf_op jit(solution)/shard_map/ppermute | solution.py:425

commit v7 on v6

--- a/solution.py
+++ b/solution.py
@@ -16,7 +16,7 @@
 UNROLL = 4
 CHUNKS = 3
 FIRST_LIMIT, SUMS_LIMIT = 63, 49
-DUE = {(0, 0): 1, (2, 1): 6}
+DUE = {(0, 0): 2, (2, 1): 6}
 MIB = 2**20
 TOKEN = jax.ShapeDtypeStruct((8, 128), F32)
 

time: 39.5 us -> 39.5 us (level)
  no operation moved by 1% of the time
where the time goes in v7:
time: 39.5 us; the launch traced here: 39.2 us
  Pallas kernels  22.5 us (57%)
  starting transfers between devices  11.3 us (29%)
  waiting for transfers between devices  4.4 us (11%)
  between operations  1.03 us (3%)
    pallas_call x15, Pallas kernels, call(): pl.pallas_call(kernel, out_shape=outs, in_specs=(specs or [VMEM] * len(in...  20.4 us
    ppermute x9, starting transfers between devices, per_device(): got = lax.ppermute(payloads[c], 'seq', pairs)  11.3 us
    ppermute x9, waiting for transfers between devices, per_device(): got = lax.ppermute(payloads[c], 'seq', pairs)  4.4 us
    pallas_call x1, Pallas kernels, per_device(): pl.pallas_call(functools.partial(last_kernel, count, starts, ready), out_...  2.12 us
  transfers between devices with their start and end apart: 9, of which 3 were waited for; matrix products, arithmetic and copies ran while one was open for 0% of the time, Pallas kernels for 46%

profile of v7, /device:TPU:0, one launch (start us, length us, event | category | flops | bytes accessed | tf_op | source)
XLA Modules:
  0.0 39.2 jit_solution(10379716275620500546)
XLA Ops:
  0.6 2.4 %shard_map.94 = (bf16[6,128,128]{2,1,0:T(8,128)(2,1)S(1)}, f32[8,128]{1,0:T(8,128)}) custom-call(s32[1,16]{1,0:T(1,128)} %bitcast.5, f32[16,352]{1,0:T(8,128)} %bitcast.2, bf16[352,16,128]{2,1,0:T(8,128)(2,1)} %q.5, bf16[352,16,128]{2,1,0:T(8,128)(2,1)} %k.5, bf16[352,16,128]{2,1,0:T(8,128)(2,1)} %v.5, bf16[352,16,128]{2,1,0:T(8,128)(2,1)} %g.5), custom_call_target="tpu_custom_call" | custom-call | flops 69206016 | bytes 1048576 | tf_op jit(solution)/shard_map/pallas_call | solution.py:347
  3.0 2.6 %collective-permute-start.5 = (bf16[6,128,128]{2,1,0:T(8,128)(2,1)S(1)}, bf16[6,128,128]{2,1,0:T(8,128)(2,1)S(1)}, u32[]{:S(2)}, u32[]{:S(2)}) collective-permute-start(bf16[6,128,128]{2,1,0:T(8,128)(2,1)S(1)} %get-tuple-element.68), channel_id=1, source_target_pairs={{0,4},{12,8},{1,5},{13,9},{2,6},{14,10},{3,7},{15,11},{16,20},{28,... | collective-permute-start | bytes 589832 | tf_op jit(solution)/shard_map/ppermute | solution.py:425
  5.7 2.8 %shard_map.85 = (bf16[5,128,128]{2,1,0:T(8,128)(2,1)S(1)}, bf16[5,128,128]{2,1,0:T(8,128)(2,1)S(1)}, f32[8,128]{1,0:T(8,128)}) custom-call(s32[1,16]{1,0:T(1,128)} %bitcast.6, f32[16,352]{1,0:T(8,128)} %bitcast.3, bf16[352,16,128]{2,1,0:T(8,128)(2,1)} %q.5, bf16[352,16,128]{2,1,0:T(8,128)(2,1)} %k.5, bf16[352,16,128]{2,1,0:T(8,128)(2,1)} %v.5, ...), custom_call_target="tpu_custom_call" | custom-call | flops 115343360 | bytes 1048576 | tf_op jit(solution)/shard_map/pallas_call | solution.py:347
  8.5 0.0 copy-start
  8.5 1.3 %collective-permute-start = (bf16[5,128,128]{2,1,0:T(8,128)(2,1)S(1)}, bf16[5,128,128]{2,1,0:T(8,128)(2,1)S(1)}, u32[]{:S(2)}, u32[]{:S(2)}) collective-permute-start(bf16[5,128,128]{2,1,0:T(8,128)(2,1)S(1)} %get-tuple-element.52), channel_id=1, source_target_pairs={{0,4},{12,8},{1,5},{13,9},{2,6},{14,10},{3,7},{15,11},{16,20},{28,... | collective-permute-start | bytes 491528 | tf_op jit(solution)/shard_map/ppermute | solution.py:425
  9.8 1.3 %collective-permute-start.2 = (bf16[5,128,128]{2,1,0:T(8,128)(2,1)S(1)}, bf16[5,128,128]{2,1,0:T(8,128)(2,1)S(1)}, u32[]{:S(2)}, u32[]{:S(2)}) collective-permute-start(bf16[5,128,128]{2,1,0:T(8,128)(2,1)S(1)} %get-tuple-element.42.rest_0_), channel_id=1, source_target_pairs={{0,4},{12,8},{1,5},{13,9},{2,6},{14,10},{3,7},{15,11},{16,20},{28,... | collective-permute-start | bytes 491528 | tf_op jit(solution)/shard_map/ppermute | solution.py:425
  11.1 4.6 %shard_map.86 = (bf16[16,352,128]{2,1,0:T(8,128)(2,1)S(1)}, bf16[16,352,128]{2,1,0:T(8,128)(2,1)S(1)}, bf16[16,352,128]{2,1,0:T(8,128)(2,1)S(1)}, bf16[16,352,12...) custom-call(s32[1,16]{1,0:T(1,128)} %bitcast.7, ...), custom_call_target="tpu_custom_call" | custom-call | flops 369098752 | bytes 1048576 | tf_op jit(solution)/shard_map/pallas_call | solution.py:347
  15.7 1.0 %shard_map.87 = (f32[16,352,128]{2,1,0:T(8,128)S(1)}, f32[16,352,128]{2,1,0:T(8,128)S(1)}, f32[16,352,128]{2,1,0:T(8,128)S(1)}, f32[8,128]{1,0:T(8,128)S(1)}) custom-call(f32[16,352,128]{2,1,0:T(8,128)S(1)} %get-tuple-element.43.col, f32[16,1,384]{2,1,0:T(1,128)S(1)} %get-tuple-element.47.row, bf16[16,352,128]{2,1,0:T(8,128)(2,1)S(1)} %get-tuple-element.48.qh, ...), custom_call_target="tpu_custom_call" | custom-call | flops 115343360 | bytes 1048576 | tf_op jit(solution)/shard_map/pallas_call | solution.py:347
  16.7 0.7 %collective-permute-start.6 = (bf16[6,128,128]{2,1,0:T(8,128)(2,1)S(1)}, bf16[6,128,128]{2,1,0:T(8,128)(2,1)S(1)}, u32[]{:S(2)}, u32[]{:S(2)}) collective-permute-start(bf16[6,128,128]{2,1,0:T(8,128)(2,1)S(1)} %get-tuple-element.70), channel_id=1, source_target_pairs={{4,8},{8,4},{5,9},{9,5},{6,10},{10,6},{7,11},{11,7},{20,24},{24,20... | collective-permute-start | bytes 589832 | tf_op jit(solution)/shard_map/ppermute | solution.py:425
  17.4 0.7 %collective-permute-start.1 = (bf16[5,128,128]{2,1,0:T(8,128)(2,1)S(1)}, bf16[5,128,128]{2,1,0:T(8,128)(2,1)S(1)}, u32[]{:S(2)}, u32[]{:S(2)}) collective-permute-start(bf16[5,128,128]{2,1,0:T(8,128)(2,1)S(1)} %get-tuple-element.56), channel_id=1, source_target_pairs={{4,8},{8,4},{5,9},{9,5},{6,10},{10,6},{7,11},{11,7},{20,24},{24,20... | collective-permute-start | bytes 491528 | tf_op jit(solution)/shard_map/ppermute | solution.py:425
  18.1 0.0 collective-permute-done.2.got.rest_4_
  18.1 0.7 %collective-permute-start.3 = (bf16[5,128,128]{2,1,0:T(8,128)(2,1)S(1)}, bf16[5,128,128]{2,1,0:T(8,128)(2,1)S(1)}, u32[]{:S(2)}, u32[]{:S(2)}) collective-permute-start(bf16[5,128,128]{2,1,0:T(8,128)(2,1)S(1)} %get-tuple-element.61), channel_id=1, source_target_pairs={{4,8},{8,4},{5,9},{9,5},{6,10},{10,6},{7,11},{11,7},{20,24},{24,20... | collective-permute-start | bytes 491528 | tf_op jit(solution)/shard_map/ppermute | solution.py:425
  18.9 1.3 %collective-permute-start.7 = (bf16[6,128,128]{2,1,0:T(8,128)(2,1)S(1)}, bf16[6,128,128]{2,1,0:T(8,128)(2,1)S(1)}, u32[]{:S(2)}, u32[]{:S(2)}) collective-permute-start(bf16[6,128,128]{2,1,0:T(8,128)(2,1)S(1)} %get-tuple-element.71), channel_id=1, source_target_pairs={{8,12},{4,0},{9,13},{5,1},{10,14},{6,2},{11,15},{7,3},{24,28},{20,... | collective-permute-start | bytes 589832 | tf_op jit(solution)/shard_map/ppermute | solution.py:425
  20.2 1.5 %collective-permute-start.8 = (bf16[5,128,128]{2,1,0:T(8,128)(2,1)S(1)}, bf16[5,128,128]{2,1,0:T(8,128)(2,1)S(1)}, u32[]{:S(2)}, u32[]{:S(2)}) collective-permute-start(bf16[5,128,128]{2,1,0:T(8,128)(2,1)S(1)} %get-tuple-element.72), channel_id=1, source_target_pairs={{8,12},{4,0},{9,13},{5,1},{10,14},{6,2},{11,15},{7,3},{24,28},{20,... | collective-permute-start | bytes 491528 | tf_op jit(solution)/shard_map/ppermute | solution.py:425
  21.7 1.7 %shard_map.90 = (f32[16,352,128]{2,1,0:T(8,128)S(1)}, f32[16,352,128]{2,1,0:T(8,128)S(1)}, f32[16,352,128]{2,1,0:T(8,128)S(1)}, f32[8,128]{1,0:T(8,128)S(1)}) custom-call(f32[16,352,128]{2,1,0:T(8,128)S(1)} %get-tuple-element.43.col, f32[16,1,384]{2,1,0:T(1,128)S(1)} %get-tuple-element.47.row, ...), custom_call_target="tpu_custom_call", output_to_operand_aliasing={{0}: (6, {}), {1}: (7, {}), {2}: (8, {})} | custom-call | flops 230686720 | bytes 1048576 | tf_op jit(solution)/shard_map/pallas_call | solution.py:347
  23.4 1.3 %collective-permute-start.4 = (bf16[5,128,128]{2,1,0:T(8,128)(2,1)S(1)}, bf16[5,128,128]{2,1,0:T(8,128)(2,1)S(1)}, u32[]{:S(2)}, u32[]{:S(2)}) collective-permute-start(bf16[5,128,128]{2,1,0:T(8,128)(2,1)S(1)} %get-tuple-element.67), channel_id=1, source_target_pairs={{8,12},{4,0},{9,13},{5,1},{10,14},{6,2},{11,15},{7,3},{24,28},{20,... | collective-permute-start | bytes 491528 | tf_op jit(solution)/shard_map/ppermute | solution.py:425
  24.7 4.0 %shard_map.93 = (f32[16,352,128]{2,1,0:T(8,128)S(1)}, f32[16,352,128]{2,1,0:T(8,128)S(1)}, f32[16,352,128]{2,1,0:T(8,128)S(1)}, f32[8,128]{1,0:T(8,128)}) custom-call(f32[16,352,128]{2,1,0:T(8,128)S(1)} %get-tuple-element.43.col, f32[16,1,384]{2,1,0:T(1,128)S(1)} %get-tuple-element.47.row, ...), custom_call_target="tpu_custom_call", output_to_operand_aliasing={{0}: (6, {}), {1}: (7, {}), {2}: (8, {})} | custom-call | flops 576716800 | bytes 1048576 | tf_op jit(solution)/shard_map/pallas_call | solution.py:347
  28.7 2.3 %shard_map.99 = (bf16[352,16,128]{2,1,0:T(8,128)(2,1)}, bf16[352,16,128]{2,1,0:T(8,128)(2,1)}, bf16[352,16,128]{2,1,0:T(8,128)(2,1)}) custom-call(f32[16,352,128]{2,1,0:T(8,128)S(1)} %get-tuple-element.43.col, bf16[16,352,128]{2,1,0:T(8,128)(2,1)S(1)} %get-tuple-element.44.kh, bf16[16,352,128]{2,1,0:T(8,128)(2,1)S(1)} %get-tuple-element.45.vh, ...), custom_call_target="tpu_custom_call" | custom-call | flops 553648128 | bytes 1048576 | tf_op jit(solution)/shard_map/pallas_call | solution.py:347
  31.0 0.6 %collective-permute-done.7.got = bf16[6,128,128]{2,1,0:T(8,128)(2,1)S(1)} collective-permute-done((bf16[6,128,128]{2,1,0:T(8,128)(2,1)S(1)}, bf16[6,128,128]{2,1,0:T(8,128)(2,1)S(1)}, u32[]{:S(2)}, u32[]{:S(2)}) %collective-permute-start.7) | collective-permute-done | bytes 196640 | tf_op jit(solution)/shard_map/ppermute | solution.py:425
  31.6 0.5 %shard_map.97.rest_0_ = bf16[2,6,352,128]{3,2,1,0:T(8,128)(2,1)S(1)} custom-call(f32[16,352,128]{2,1,0:T(8,128)S(1)} %get-tuple-element.43.col, bf16[16,352,128]{2,1,0:T(8,128)(2,1)S(1)} %get-tuple-element.44.kh, bf16[16,352,128]{2,1,0:T(8,128)(2,1)S(1)} %get-tuple-element.45.vh, bf16[16,352,128]{2,1,0:T(8,128)(2,1)S(1)} %get-tuple-element.46.gh, ...), custom_call_target="tpu_custom_call" | custom-call | flops 138412032 | bytes 1048576 | tf_op jit(solution)/shard_map/pallas_call | solution.py:347
  32.1 3.0 %collective-permute-done.8.got = bf16[5,128,128]{2,1,0:T(8,128)(2,1)S(1)} collective-permute-done((bf16[5,128,128]{2,1,0:T(8,128)(2,1)S(1)}, bf16[5,128,128]{2,1,0:T(8,128)(2,1)S(1)}, u32[]{:S(2)}, u32[]{:S(2)}) %collective-permute-start.8) | collective-permute-done | bytes 163872 | tf_op jit(solution)/shard_map/ppermute | solution.py:425
  35.1 1.0 %shard_map.98 = (bf16[2,5,352,128]{3,2,1,0:T(8,128)(2,1)S(1)}, bf16[2,352,16,128]{3,2,1,0:T(8,128)(2,1)S(1)}) custom-call(f32[16,352,128]{2,1,0:T(8,128)S(1)} %get-tuple-element.43.col, bf16[16,352,128]{2,1,0:T(8,128)(2,1)S(1)} %get-tuple-element.44.kh, bf16[16,352,128]{2,1,0:T(8,128)(2,1)S(1)} %get-tuple-element.45.vh, ...), custom_call_target="tpu_custom_call" | custom-call | flops 115343360 | bytes 1048576 | tf_op jit(solution)/shard_map/pallas_call | solution.py:347
  36.1 0.8 %collective-permute-done.4.got = bf16[5,128,128]{2,1,0:T(8,128)(2,1)S(1)} collective-permute-done((bf16[5,128,128]{2,1,0:T(8,128)(2,1)S(1)}, bf16[5,128,128]{2,1,0:T(8,128)(2,1)S(1)}, u32[]{:S(2)}, u32[]{:S(2)}) %collective-permute-start.4) | collective-permute-done | bytes 163872 | tf_op jit(solution)/shard_map/ppermute | solution.py:425
  36.9 2.1 %shard_map.100 = (bf16[352,16,128]{2,1,0:T(8,128)(2,1)}, bf16[352,16,128]{2,1,0:T(8,128)(2,1)}, bf16[352,16,128]{2,1,0:T(8,128)(2,1)}, bf16[2,352,16,128]{3,2,1,0:T(8,128)(2,1)S(1)}) custom-call(f32[16,352,128]{2,1,0:T(8,128)S(1)} %get-tuple-element.43.col, ...), custom_call_target="tpu_custom_call", output_to_operand_aliasing={{0}: (11, {}), {1}: (12, {}), {2}: (13, {}), {3}: (10, {})} | custom-call | flops 115343360 | bytes 1048576 | tf_op jit(solution)/shard_map/pallas_call | solution.py:476
  (12 shorter events, 0.1 us)
Async XLA Ops:
  3.0 13.6 %collective-permute-start.5 = (bf16[6,128,128]{2,1,0:T(8,128)(2,1)S(1)}, bf16[6,128,128]{2,1,0:T(8,128)(2,1)S(1)}, u32[]{:S(2)}, u32[]{:S(2)}) collective-permute-start(bf16[6,128,128]{2,1,0:T(8,128)(2,1)S(1)} %get-tuple-element.68), channel_id=1, source_target_pairs={{0,4},{12,8},{1,5},{13,9},{2,6},{14,10},{3,7},{15,11},{16,20},{28,... | collective-permute-start | bytes 589832 | tf_op jit(solution)/shard_map/ppermute | solution.py:425
  8.5 2.6 %copy-start = (bf16[5,128,128]{2,1,0:T(8,128)(2,1)}, bf16[5,128,128]{2,1,0:T(8,128)(2,1)S(1)}, u32[]{:S(2)}) copy-start(bf16[5,128,128]{2,1,0:T(8,128)(2,1)S(1)} %get-tuple-element.42.rest_0_) | copy-start | bytes 491524
  8.5 8.9 %collective-permute-start = (bf16[5,128,128]{2,1,0:T(8,128)(2,1)S(1)}, bf16[5,128,128]{2,1,0:T(8,128)(2,1)S(1)}, u32[]{:S(2)}, u32[]{:S(2)}) collective-permute-start(bf16[5,128,128]{2,1,0:T(8,128)(2,1)S(1)} %get-tuple-element.52), channel_id=1, source_target_pairs={{0,4},{12,8},{1,5},{13,9},{2,6},{14,10},{3,7},{15,11},{16,20},{28,... | collective-permute-start | bytes 491528 | tf_op jit(solution)/shard_map/ppermute | solution.py:425
  9.8 8.3 %collective-permute-start.2 = (bf16[5,128,128]{2,1,0:T(8,128)(2,1)S(1)}, bf16[5,128,128]{2,1,0:T(8,128)(2,1)S(1)}, u32[]{:S(2)}, u32[]{:S(2)}) collective-permute-start(bf16[5,128,128]{2,1,0:T(8,128)(2,1)S(1)} %get-tuple-element.42.rest_0_), channel_id=1, source_target_pairs={{0,4},{12,8},{1,5},{13,9},{2,6},{14,10},{3,7},{15,11},{16,20},{28,... | collective-permute-start | bytes 491528 | tf_op jit(solution)/shard_map/ppermute | solution.py:425
  16.7 2.1 %collective-permute-start.6 = (bf16[6,128,128]{2,1,0:T(8,128)(2,1)S(1)}, bf16[6,128,128]{2,1,0:T(8,128)(2,1)S(1)}, u32[]{:S(2)}, u32[]{:S(2)}) collective-permute-start(bf16[6,128,128]{2,1,0:T(8,128)(2,1)S(1)} %get-tuple-element.70), channel_id=1, source_target_pairs={{4,8},{8,4},{5,9},{9,5},{6,10},{10,6},{7,11},{11,7},{20,24},{24,20... | collective-permute-start | bytes 589832 | tf_op jit(solution)/shard_map/ppermute | solution.py:425
  17.4 2.7 %collective-permute-start.1 = (bf16[5,128,128]{2,1,0:T(8,128)(2,1)S(1)}, bf16[5,128,128]{2,1,0:T(8,128)(2,1)S(1)}, u32[]{:S(2)}, u32[]{:S(2)}) collective-permute-start(bf16[5,128,128]{2,1,0:T(8,128)(2,1)S(1)} %get-tuple-element.56), channel_id=1, source_target_pairs={{4,8},{8,4},{5,9},{9,5},{6,10},{10,6},{7,11},{11,7},{20,24},{24,20... | collective-permute-start | bytes 491528 | tf_op jit(solution)/shard_map/ppermute | solution.py:425
  18.1 5.2 %collective-permute-start.3 = (bf16[5,128,128]{2,1,0:T(8,128)(2,1)S(1)}, bf16[5,128,128]{2,1,0:T(8,128)(2,1)S(1)}, u32[]{:S(2)}, u32[]{:S(2)}) collective-permute-start(bf16[5,128,128]{2,1,0:T(8,128)(2,1)S(1)} %get-tuple-element.61), channel_id=1, source_target_pairs={{4,8},{8,4},{5,9},{9,5},{6,10},{10,6},{7,11},{11,7},{20,24},{24,20... | collective-permute-start | bytes 491528 | tf_op jit(solution)/shard_map/ppermute | solution.py:425
  18.9 12.7 %collective-permute-start.7 = (bf16[6,128,128]{2,1,0:T(8,128)(2,1)S(1)}, bf16[6,128,128]{2,1,0:T(8,128)(2,1)S(1)}, u32[]{:S(2)}, u32[]{:S(2)}) collective-permute-start(bf16[6,128,128]{2,1,0:T(8,128)(2,1)S(1)} %get-tuple-element.71), channel_id=1, source_target_pairs={{8,12},{4,0},{9,13},{5,1},{10,14},{6,2},{11,15},{7,3},{24,28},{20,... | collective-permute-start | bytes 589832 | tf_op jit(solution)/shard_map/ppermute | solution.py:425
  20.2 14.9 %collective-permute-start.8 = (bf16[5,128,128]{2,1,0:T(8,128)(2,1)S(1)}, bf16[5,128,128]{2,1,0:T(8,128)(2,1)S(1)}, u32[]{:S(2)}, u32[]{:S(2)}) collective-permute-start(bf16[5,128,128]{2,1,0:T(8,128)(2,1)S(1)} %get-tuple-element.72), channel_id=1, source_target_pairs={{8,12},{4,0},{9,13},{5,1},{10,14},{6,2},{11,15},{7,3},{24,28},{20,... | collective-permute-start | bytes 491528 | tf_op jit(solution)/shard_map/ppermute | solution.py:425
  23.4 13.6 %collective-permute-start.4 = (bf16[5,128,128]{2,1,0:T(8,128)(2,1)S(1)}, bf16[5,128,128]{2,1,0:T(8,128)(2,1)S(1)}, u32[]{:S(2)}, u32[]{:S(2)}) collective-permute-start(bf16[5,128,128]{2,1,0:T(8,128)(2,1)S(1)} %get-tuple-element.67), channel_id=1, source_target_pairs={{8,12},{4,0},{9,13},{5,1},{10,14},{6,2},{11,15},{7,3},{24,28},{20,... | collective-permute-start | bytes 491528 | tf_op jit(solution)/shard_map/ppermute | solution.py:425
